TPU v7x, 32 devices: a whole 2x2x4 slice. The times are simulated.
32 devices in a mesh: edge: 8 (over z, y), grp: 4 (over x, core).
Axes of the slice: x: 2, y: 2, z: 4, core: 2. Of those that a mesh axis runs over, the one named last changes fastest.
Arguments:
- atoms: bfloat16 [8192, 9, 128], P(('edge', 'grp')), may hold values from -4 to 4
- neighbours: int32 [8192, 64], P(('edge', 'grp')), may hold values from 0 to 8191, as said below
- live_mask: int32 [8192, 64], P(('edge', 'grp')), may hold values from 0 to 1, as said below
- distances: float32 [8192, 64], P(('edge', 'grp')), may hold values from 0.8 to 4.8
- w_iso1: bfloat16 [128, 128], replicated, may hold values from -0.5 to 0.5
- w_anti1: bfloat16 [128, 128], replicated, may hold values from -0.5 to 0.5
- w_sym1: bfloat16 [128, 128], replicated, may hold values from -0.5 to 0.5
- w_rad1: bfloat16 [32, 128], replicated, may hold values from -2 to 2
- b_rad1: bfloat16 [128], replicated, may hold values from -3 to 3
- w_rad2: bfloat16 [128, 256], replicated, may hold values from -0.75 to 0.75
- b_rad2: bfloat16 [256], replicated, may hold values from -3 to 3
- w_rad3: bfloat16 [256, 384], replicated, may hold values from -0.5 to 0.5
- b_rad3: bfloat16 [384], replicated, may hold values from -3 to 3
- w_iso2: bfloat16 [128, 128], replicated, may hold values from -1.5 to 1.5
- w_anti2: bfloat16 [128, 128], replicated, may hold values from -1.5 to 1.5
- w_sym2: bfloat16 [128, 128], replicated, may hold values from -1.5 to 1.5
- out_grad: bfloat16 [8192, 9, 128], P(('edge', 'grp')), may hold values from -6 to 6
Outputs:
- updated: bfloat16 [8192, 9, 128], P(('edge', 'grp'))
- grad_atoms: float32 [8192, 9, 128], P(('edge', 'grp'))
- grad_w_iso1: float32 [128, 128], replicated
- grad_w_anti1: float32 [128, 128], replicated
- grad_w_sym1: float32 [128, 128], replicated
- grad_w_rad1: float32 [32, 128], replicated
- grad_b_rad1: float32 [128], replicated
- grad_w_rad2: float32 [128, 256], replicated
- grad_b_rad2: float32 [256], replicated
- grad_w_rad3: float32 [256, 384], replicated
- grad_b_rad3: float32 [384], replicated
- grad_w_iso2: float32 [128, 128], replicated
- grad_w_anti2: float32 [128, 128], replicated
- grad_w_sym2: float32 [128, 128], replicated
Inputs may be any that keep to these rules, and one draw needn't show every extreme that they name: neighbours[i, s] is an atom of the molecule of atom i; molecules are runs of consecutive atoms of at most 256, so the difference of neighbours[i, s] and i is under 256 in size, and 255 occurs; a slot with live_mask 0 holds i itself. `live_mask`: in each row the live slots come first, at least one.
All inputs are finite; a program needn't handle non-finite values.
Results may differ from a plain program's by a relative error of at most 0.012.
Values may be sent and summed in bfloat16 or wider, within the bound.
No kernel may reach another device: no remote copies, remote signals or barrier semaphores. Data moves between devices by JAX's collectives and lax.ppermute only.
A program may use at most 192 MiB of HBM per device.

v0:
```python
import math

import jax
import jax.numpy as jnp
from jax import lax
from jax.sharding import PartitionSpec as P

MOL_MOST = 256


CUTOFF = 5.0


def with_halo(value, sides, width):
    for axis, dim in sides:
        peers, length = (lax.axis_size(axis), value.shape[dim])
        up = [(i, (i + 1) % peers) for i in range(peers - 1)]
        down = [(j, i) for i, j in up]
        last = lax.slice_in_dim(value, length - width, length, axis=dim)
        initial = lax.slice_in_dim(value, 0, width, axis=dim)
        before = lax.ppermute(last, axis, up)
        after = lax.ppermute(initial, axis, down)
        value = jnp.concatenate([before, value, after], axis=dim)
    return value


def from_behind(value, axis, by):
    peers = lax.axis_size(axis)
    pairs = [(i, i + by) for i in range(peers) if 0 <= i + by < peers]
    return lax.ppermute(value, axis, pairs)


def flip_pairs(tensor):
    leading = tensor.shape[0]
    return jnp.swapaxes(tensor.reshape(leading, 3, 3, -1), 1, 2).reshape(leading, 9, -1)


def split_parts(tensor):
    unit_diag = jnp.eye(3, dtype=jnp.float32).reshape(1, 9, 1)
    thirds = (tensor[:, 0] + tensor[:, 4] + tensor[:, 8]) / 3.0
    isotropic = thirds[:, None, :] * unit_diag
    flipped = flip_pairs(tensor)
    antisym = 0.5 * (tensor - flipped)
    symmetric = 0.5 * (tensor + flipped) - isotropic
    return (isotropic, antisym, symmetric)


def tensor_product(left_mat, right_mat):
    leading = left_mat.shape[0]
    left_view = left_mat.reshape(leading, 3, 3, 1, -1)
    right_view = right_mat.reshape(leading, 1, 3, 3, -1)
    return jnp.sum(left_view * right_view, axis=2).reshape(leading, 9, -1)


def channel_mix(tensor_parts, weight):
    return jnp.einsum("nmc,cd->nmd", tensor_parts, weight, preferred_element_type=jnp.float32)


def channel_back(gradient, weight):
    return jnp.einsum("nmd,cd->nmc", gradient, weight, preferred_element_type=jnp.float32)


def weight_grad(tensor_parts, gradient):
    return jnp.einsum("nmc,nmd->cd", tensor_parts, gradient, preferred_element_type=jnp.float32)


def radial_basis(lengths, basis_count):
    centres = jnp.arange(basis_count, dtype=jnp.float32) * (CUTOFF / (basis_count - 1))
    sharpness = 0.5 * ((basis_count - 1) / CUTOFF) ** 2
    return jnp.exp(-sharpness * (lengths[..., None] - centres) ** 2)


def smooth_cut(lengths):
    return 0.5 * (jnp.cos(math.pi * lengths / CUTOFF) + 1.0)


def silu_slope(values):
    sigmoid_val = jax.nn.sigmoid(values)
    return sigmoid_val * (1.0 + values * (1.0 - sigmoid_val))


def window_table(block_links, window_start, window_rows):
    relative = block_links.reshape(-1) - window_start
    return (relative[:, None] == jnp.arange(window_rows)[None, :]).astype(jnp.bfloat16)


def edge_terms(ext_rows, radial, block_links, block_live, block_dist, window_start, window_rows):
    w_rad1, b_rad1, w_rad2, b_rad2, w_rad3, b_rad3 = radial
    channels = ext_rows.shape[2]
    basis_vals = radial_basis(block_dist, w_rad1.shape[0]).astype(jnp.bfloat16)
    hidden1 = jnp.einsum(
        "akr,rc->akc", basis_vals, w_rad1, preferred_element_type=jnp.float32
    ) + b_rad1.astype(jnp.float32)
    active1 = jax.nn.silu(hidden1).astype(jnp.bfloat16)
    hidden2 = jnp.einsum(
        "akc,cd->akd", active1, w_rad2, preferred_element_type=jnp.float32
    ) + b_rad2.astype(jnp.float32)
    active2 = jax.nn.silu(hidden2).astype(jnp.bfloat16)
    hidden3 = jnp.einsum(
        "akc,cd->akd", active2, w_rad3, preferred_element_type=jnp.float32
    ) + b_rad3.astype(jnp.float32)
    gating = smooth_cut(block_dist) * block_live
    factors = jax.nn.silu(hidden3) * gating[..., None]
    table = window_table(block_links, window_start, window_rows)
    window = lax.dynamic_slice_in_dim(ext_rows, window_start, window_rows, 0).reshape(
        window_rows, 9 * channels
    )
    sources = jnp.dot(table, window, preferred_element_type=jnp.float32).reshape(-1, 9, channels)
    return (
        basis_vals,
        hidden1,
        active1,
        hidden2,
        active2,
        hidden3,
        gating,
        factors,
        split_parts(sources),
        table,
    )


def combine_messages(factors, source_parts, link_shape, channels):
    iso_src, anti_src, sym_src = source_parts
    block_shape = (link_shape[0], link_shape[1], 9, channels)
    summed = factors[:, :, None, :channels] * iso_src.reshape(block_shape)
    summed = summed + factors[:, :, None, channels : 2 * channels] * anti_src.reshape(block_shape)
    summed = summed + factors[:, :, None, 2 * channels :] * sym_src.reshape(block_shape)
    return jnp.sum(summed, axis=1)


def local(
    atoms,
    neighbours,
    live_mask,
    distances,
    w_iso1,
    w_anti1,
    w_sym1,
    w_rad1,
    b_rad1,
    w_rad2,
    b_rad2,
    w_rad3,
    b_rad3,
    w_iso2,
    w_anti2,
    w_sym2,
    out_grad,
):
    row_count = atoms.shape[0]
    channels = atoms.shape[2]
    halo_rows = MOL_MOST
    block_rows = min(64, row_count)
    block_count = row_count // block_rows
    window_rows = block_rows + 2 * halo_rows
    first_row = lax.axis_index(("edge", "grp")) * row_count
    radial = (w_rad1, b_rad1, w_rad2, b_rad2, w_rad3, b_rad3)
    atoms_float = atoms.astype(jnp.float32)
    scale_in = jnp.sum(atoms_float * atoms_float, axis=1, keepdims=True) + 1.0
    normed = atoms_float / scale_in
    iso_in, anti_in, sym_in = split_parts(normed)
    iso_in_b = iso_in.astype(jnp.bfloat16)
    anti_in_b = anti_in.astype(jnp.bfloat16)
    sym_in_b = sym_in.astype(jnp.bfloat16)
    mixed_rows = (
        channel_mix(iso_in_b, w_iso1)
        + channel_mix(anti_in_b, w_anti1)
        + channel_mix(sym_in_b, w_sym1)
    )
    mixed_b = mixed_rows.astype(jnp.bfloat16)
    ext_rows = with_halo(mixed_b, ((("edge", "grp"), 0),), halo_rows)
    local_links = neighbours - first_row + halo_rows
    link_blocks = local_links.reshape(block_count, block_rows, -1)
    live_blocks = live_mask.astype(jnp.float32).reshape(block_count, block_rows, -1)
    dist_blocks = distances.reshape(block_count, block_rows, -1)
    block_starts = jnp.arange(block_count) * block_rows

    def forward_block(block_args):
        block_links, block_live, block_dist, window_start = block_args
        edge_parts = edge_terms(
            ext_rows, radial, block_links, block_live, block_dist, window_start, window_rows
        )
        return combine_messages(edge_parts[7], edge_parts[8], block_links.shape, channels)

    messages = lax.map(
        forward_block, (link_blocks, live_blocks, dist_blocks, block_starts)
    ).reshape(row_count, 9, channels)
    mixed_float = mixed_b.astype(jnp.float32)
    paired = tensor_product(mixed_float, messages) + tensor_product(messages, mixed_float)
    scale_mid = jnp.sum(paired * paired, axis=1, keepdims=True) + 1.0
    iso_pair, anti_pair, sym_pair = split_parts(paired)
    iso_mid = iso_pair / scale_mid
    anti_mid = anti_pair / scale_mid
    sym_mid = sym_pair / scale_mid
    iso_mid_b = iso_mid.astype(jnp.bfloat16)
    anti_mid_b = anti_mid.astype(jnp.bfloat16)
    sym_mid_b = sym_mid.astype(jnp.bfloat16)
    update = (
        channel_mix(iso_mid_b, w_iso2)
        + channel_mix(anti_mid_b, w_anti2)
        + channel_mix(sym_mid_b, w_sym2)
    )
    updated = (normed + update + tensor_product(update, update)).astype(jnp.bfloat16)
    grad_out_float = out_grad.astype(jnp.float32)
    update_flip = flip_pairs(update)
    grad_update = (
        grad_out_float
        + tensor_product(grad_out_float, update_flip)
        + tensor_product(update_flip, grad_out_float)
    )
    grad_update_b = grad_update.astype(jnp.bfloat16)
    grad_w_iso2 = weight_grad(iso_mid_b, grad_update_b)
    grad_w_anti2 = weight_grad(anti_mid_b, grad_update_b)
    grad_w_sym2 = weight_grad(sym_mid_b, grad_update_b)
    grad_iso_mid = channel_back(grad_update_b, w_iso2)
    grad_anti_mid = channel_back(grad_update_b, w_anti2)
    grad_sym_mid = channel_back(grad_update_b, w_sym2)
    projected = jnp.sum(
        grad_iso_mid * iso_mid + grad_anti_mid * anti_mid + grad_sym_mid * sym_mid,
        axis=1,
        keepdims=True,
    )
    grad_paired = (
        split_parts(grad_iso_mid)[0] + split_parts(grad_anti_mid)[1] + split_parts(grad_sym_mid)[2]
    ) / scale_mid
    grad_paired = grad_paired - 2.0 * paired * projected / scale_mid
    mixed_flip = flip_pairs(mixed_float)
    messages_flip = flip_pairs(messages)
    grad_messages_b = (
        tensor_product(mixed_flip, grad_paired) + tensor_product(grad_paired, mixed_flip)
    ).astype(jnp.bfloat16)
    grad_from_pair = tensor_product(grad_paired, messages_flip) + tensor_product(
        messages_flip, grad_paired
    )
    grad_blocks = grad_messages_b.reshape(block_count, block_rows, 9, channels)

    def backward_block(running, block_args):
        grad_ext, radial_grads = running
        block_links, block_live, block_dist, block_grad, window_start = block_args
        (
            basis_vals,
            hidden1,
            active1,
            hidden2,
            active2,
            hidden3,
            gating,
            factors,
            source_parts,
            table,
        ) = edge_terms(
            ext_rows, radial, block_links, block_live, block_dist, window_start, window_rows
        )
        iso_src, anti_src, sym_src = source_parts
        block_shape = (block_links.shape[0], block_links.shape[1], 9, channels)
        grad_msg = block_grad.astype(jnp.float32)
        grad_wide = grad_msg[:, None]
        grad_fac_iso = jnp.sum(grad_wide * iso_src.reshape(block_shape), axis=2)
        grad_fac_anti = jnp.sum(grad_wide * anti_src.reshape(block_shape), axis=2)
        grad_fac_sym = jnp.sum(grad_wide * sym_src.reshape(block_shape), axis=2)
        grad_factors = jnp.concatenate([grad_fac_iso, grad_fac_anti, grad_fac_sym], axis=-1)
        msg_iso, msg_anti, msg_sym = split_parts(grad_msg)
        to_sources = factors[:, :, None, :channels] * msg_iso[:, None]
        to_sources = to_sources + factors[:, :, None, channels : 2 * channels] * msg_anti[:, None]
        to_sources = to_sources + factors[:, :, None, 2 * channels :] * msg_sym[:, None]
        flat_terms = to_sources.reshape(-1, 9 * channels)
        high_part = flat_terms.astype(jnp.bfloat16)
        rest_part = (flat_terms - high_part.astype(jnp.float32)).astype(jnp.bfloat16)
        gathered_back = jnp.einsum(
            "ew,ef->wf", table, high_part, preferred_element_type=jnp.float32
        )
        gathered_back = gathered_back + jnp.einsum(
            "ew,ef->wf", table, rest_part, preferred_element_type=jnp.float32
        )
        current = lax.dynamic_slice_in_dim(grad_ext, window_start, window_rows, 0)
        grad_ext = lax.dynamic_update_slice_in_dim(
            grad_ext, current + gathered_back.reshape(window_rows, 9, channels), window_start, 0
        )
        grad_hid3 = (grad_factors * gating[..., None] * silu_slope(hidden3)).astype(jnp.bfloat16)
        grad_w3 = jnp.einsum("akc,akd->cd", active2, grad_hid3, preferred_element_type=jnp.float32)
        grad_b3 = jnp.sum(grad_hid3.astype(jnp.float32), axis=(0, 1))
        grad_hid2 = (
            jnp.einsum("akd,cd->akc", grad_hid3, w_rad3, preferred_element_type=jnp.float32)
            * silu_slope(hidden2)
        ).astype(jnp.bfloat16)
        grad_w2 = jnp.einsum("akc,akd->cd", active1, grad_hid2, preferred_element_type=jnp.float32)
        grad_b2 = jnp.sum(grad_hid2.astype(jnp.float32), axis=(0, 1))
        grad_hid1 = (
            jnp.einsum("akd,cd->akc", grad_hid2, w_rad2, preferred_element_type=jnp.float32)
            * silu_slope(hidden1)
        ).astype(jnp.bfloat16)
        grad_w1 = jnp.einsum(
            "akr,akc->rc", basis_vals, grad_hid1, preferred_element_type=jnp.float32
        )
        grad_b1 = jnp.sum(grad_hid1.astype(jnp.float32), axis=(0, 1))
        fresh = (grad_w1, grad_b1, grad_w2, grad_b2, grad_w3, grad_b3)
        radial_grads = tuple((older + newer for older, newer in zip(radial_grads, fresh)))
        return ((grad_ext, radial_grads), None)

    ext_zero = jnp.zeros((row_count + 2 * halo_rows, 9, channels), jnp.float32)
    radial_zero = tuple((jnp.zeros(weight.shape, jnp.float32) for weight in radial))
    (grad_ext, radial_grads), unused = lax.scan(
        backward_block,
        (ext_zero, radial_zero),
        (link_blocks, live_blocks, dist_blocks, grad_blocks, block_starts),
    )
    lower_rim = grad_ext[:halo_rows]
    upper_rim = grad_ext[halo_rows + row_count :]
    from_above = from_behind(lower_rim.astype(jnp.bfloat16), ("edge", "grp"), -1).astype(
        lower_rim.dtype
    )
    from_below = from_behind(upper_rim.astype(jnp.bfloat16), ("edge", "grp"), 1).astype(
        upper_rim.dtype
    )
    own_part = grad_ext[halo_rows : halo_rows + row_count]
    own_part = own_part + from_above
    own_part = own_part + from_below
    grad_mixed_b = (grad_from_pair + own_part).astype(jnp.bfloat16)
    grad_w_iso1 = weight_grad(iso_in_b, grad_mixed_b)
    grad_w_anti1 = weight_grad(anti_in_b, grad_mixed_b)
    grad_w_sym1 = weight_grad(sym_in_b, grad_mixed_b)
    grad_normed = grad_out_float + split_parts(channel_back(grad_mixed_b, w_iso1))[0]
    grad_normed = grad_normed + split_parts(channel_back(grad_mixed_b, w_anti1))[1]
    grad_normed = grad_normed + split_parts(channel_back(grad_mixed_b, w_sym1))[2]
    grad_atoms = (
        grad_normed / scale_in
        - 2.0 * atoms_float * jnp.sum(grad_normed * normed, axis=1, keepdims=True) / scale_in
    )
    summed = lax.psum(
        (
            grad_w_iso1,
            grad_w_anti1,
            grad_w_sym1,
            radial_grads[0],
            radial_grads[1],
            radial_grads[2],
            radial_grads[3],
            radial_grads[4],
            radial_grads[5],
            grad_w_iso2,
            grad_w_anti2,
            grad_w_sym2,
        ),
        ("edge", "grp"),
    )
    return (
        updated,
        grad_atoms,
        summed[0],
        summed[1],
        summed[2],
        summed[3],
        summed[4],
        summed[5],
        summed[6],
        summed[7],
        summed[8],
        summed[9],
        summed[10],
        summed[11],
    )


def solution(mesh):
    placed = (
        P(("edge", "grp"), None, None),
        P(("edge", "grp"), None),
        P(("edge", "grp"), None),
        P(("edge", "grp"), None),
        P(),
        P(),
        P(),
        P(),
        P(),
        P(),
        P(),
        P(),
        P(),
        P(),
        P(),
        P(),
        P(("edge", "grp"), None, None),
    )
    return jax.shard_map(
        local,
        mesh=mesh,
        in_specs=placed,
        out_specs=(
            P(("edge", "grp"), None, None),
            P(("edge", "grp"), None, None),
            P(),
            P(),
            P(),
            P(),
            P(),
            P(),
            P(),
            P(),
            P(),
            P(),
            P(),
            P(),
        ),
        check_vma=False,
    )
```

profile of v0, /device:TPU:0, one launch (start us, length us, event | category | flops | bytes accessed | tf_op | source)
XLA Modules:
  0.0 1832.6 jit_solution(6991604120228324275)
XLA Ops:
  24.3 562.5 %while.37 = (s32[]{:T(128)}, f32[4,64,9,128]{3,1,0,2:T(8,128)}, f32[4,64,64]{2,1,0:T(8,128)S(1)}, bf16[32,128]{1,0:T(8,128)(2,1)S(1)}, bf16[128]{0:T(256)(128)(2...) while((s32[]{:T(128)}, f32[4,64,9,128]{3,1,0,2:T(8,128)}, ...), condition=%wide.region_3.4_spmd, body=%wide.region_1.3_spmd.sunk | while | flops 6618821632 | bytes 313623136 | solution.py:186
  57.0 18.7 %copy.339 = f32[4096,1152]{1,0:T(8,128)} copy(f32[4096,1152]{0,1:T(8,128)} %copy-done.2) | data formatting | bytes 37748736 | tf_op jit(solution)/shard_map/while/body/eval_jaxpr/dot_general | solution.py:108
  75.7 24.4 %reshape.552 = f32[64,64,9,128]{3,2,1,0:T(8,128)} reshape(f32[4096,1152]{1,0:T(8,128)} %copy.339) | data formatting | bytes 37748736 | tf_op jit(solution)/shard_map/while/body/eval_jaxpr/reshape | solution.py:108
  132.7 31.5 %fusion.211 = f32[64,9,128]{2,1,0:T(8,128)S(1)} fusion(f32[64,64,9,128]{3,2,1,0:T(8,128)} %reshape.552, f32[64,64,9,128]{3,1,0,2:T(8,128)} %bitcast.413, f32[64,64,128]{2,1,0:T(8,128)} %get-tuple-element.969, f32[64,64,128]{2,1,0:T(8,128)} %get-tuple-element.970, f32[9]{0:T(128)S(1)} %reshape.553, f32[64,64,128]{2,1,0:T(8,128)S(1)} %bitcast.418, ...), kind=kLoop, calls=%fused_computation.7.clone.1 | loop fusion | flops 51830784 | bytes 46432292 | tf_op jit(solution)/shard_map/while/body/eval_jaxpr/reduce_sum | solution.py:129
  197.6 18.7 %copy.339 = f32[4096,1152]{1,0:T(8,128)} copy(f32[4096,1152]{0,1:T(8,128)} %copy-done.2) | data formatting | bytes 37748736 | tf_op jit(solution)/shard_map/while/body/eval_jaxpr/dot_general | solution.py:108
  216.3 24.4 %reshape.552 = f32[64,64,9,128]{3,2,1,0:T(8,128)} reshape(f32[4096,1152]{1,0:T(8,128)} %copy.339) | data formatting | bytes 37748736 | tf_op jit(solution)/shard_map/while/body/eval_jaxpr/reshape | solution.py:108
  273.3 31.5 %fusion.211 = f32[64,9,128]{2,1,0:T(8,128)S(1)} fusion(f32[64,64,9,128]{3,2,1,0:T(8,128)} %reshape.552, f32[64,64,9,128]{3,1,0,2:T(8,128)} %bitcast.413, f32[64,64,128]{2,1,0:T(8,128)} %get-tuple-element.969, f32[64,64,128]{2,1,0:T(8,128)} %get-tuple-element.970, f32[9]{0:T(128)S(1)} %reshape.553, f32[64,64,128]{2,1,0:T(8,128)S(1)} %bitcast.418, ...), kind=kLoop, calls=%fused_computation.7.clone.1 | loop fusion | flops 51830784 | bytes 46432292 | tf_op jit(solution)/shard_map/while/body/eval_jaxpr/reduce_sum | solution.py:129
  338.1 18.7 %copy.339 = f32[4096,1152]{1,0:T(8,128)} copy(f32[4096,1152]{0,1:T(8,128)} %copy-done.2) | data formatting | bytes 37748736 | tf_op jit(solution)/shard_map/while/body/eval_jaxpr/dot_general | solution.py:108
  356.7 24.4 %reshape.552 = f32[64,64,9,128]{3,2,1,0:T(8,128)} reshape(f32[4096,1152]{1,0:T(8,128)} %copy.339) | data formatting | bytes 37748736 | tf_op jit(solution)/shard_map/while/body/eval_jaxpr/reshape | solution.py:108
  413.8 31.5 %fusion.211 = f32[64,9,128]{2,1,0:T(8,128)S(1)} fusion(f32[64,64,9,128]{3,2,1,0:T(8,128)} %reshape.552, f32[64,64,9,128]{3,1,0,2:T(8,128)} %bitcast.413, f32[64,64,128]{2,1,0:T(8,128)} %get-tuple-element.969, f32[64,64,128]{2,1,0:T(8,128)} %get-tuple-element.970, f32[9]{0:T(128)S(1)} %reshape.553, f32[64,64,128]{2,1,0:T(8,128)S(1)} %bitcast.418, ...), kind=kLoop, calls=%fused_computation.7.clone.1 | loop fusion | flops 51830784 | bytes 46432292 | tf_op jit(solution)/shard_map/while/body/eval_jaxpr/reduce_sum | solution.py:129
  478.5 18.7 %copy.339 = f32[4096,1152]{1,0:T(8,128)} copy(f32[4096,1152]{0,1:T(8,128)} %copy-done.2) | data formatting | bytes 37748736 | tf_op jit(solution)/shard_map/while/body/eval_jaxpr/dot_general | solution.py:108
  497.2 24.4 %reshape.552 = f32[64,64,9,128]{3,2,1,0:T(8,128)} reshape(f32[4096,1152]{1,0:T(8,128)} %copy.339) | data formatting | bytes 37748736 | tf_op jit(solution)/shard_map/while/body/eval_jaxpr/reshape | solution.py:108
  554.2 31.5 %fusion.211 = f32[64,9,128]{2,1,0:T(8,128)S(1)} fusion(f32[64,64,9,128]{3,2,1,0:T(8,128)} %reshape.552, f32[64,64,9,128]{3,1,0,2:T(8,128)} %bitcast.413, f32[64,64,128]{2,1,0:T(8,128)} %get-tuple-element.969, f32[64,64,128]{2,1,0:T(8,128)} %get-tuple-element.970, f32[9]{0:T(128)S(1)} %reshape.553, f32[64,64,128]{2,1,0:T(8,128)S(1)} %bitcast.418, ...), kind=kLoop, calls=%fused_computation.7.clone.1 | loop fusion | flops 51830784 | bytes 46432292 | tf_op jit(solution)/shard_map/while/body/eval_jaxpr/reduce_sum | solution.py:129
  604.0 997.8 %while.38 = (s32[]{:T(128)}, f32[768,9,128]{2,0,1:T(8,128)}, f32[32,128]{1,0:T(8,128)}, f32[128]{0:T(128)}, f32[128,256]{1,0:T(8,128)}, /*index=5*/f32[256]{0:T(...) while((s32[]{:T(128)}, f32[768,9,128]{2,0,1:T(8,128)}, ...), condition=%wide.region_22.23_spmd.clone, body=%wide.region_15.22_spmd.clone.sunk | while | flops 19765080064 | bytes 555671424 | solution.py:303
  637.9 18.7 %copy.350 = f32[4096,1152]{1,0:T(8,128)} copy(f32[4096,1152]{0,1:T(8,128)} %copy-done.3) | data formatting | bytes 37748736 | tf_op jit(solution)/shard_map/while/body/eval_jaxpr/dot_general | solution.py:108
  656.6 24.4 %reshape.555 = f32[64,64,9,128]{3,2,1,0:T(8,128)} reshape(f32[4096,1152]{1,0:T(8,128)} %copy.350) | data formatting | bytes 37748736 | tf_op jit(solution)/shard_map/while/body/eval_jaxpr/reshape | solution.py:108
  700.4 46.5 %fusion.227 = (f32[64,64,128]{2,1,0:T(8,128)S(1)}, f32[64,64,128]{2,1,0:T(8,128)S(1)}, f32[64,64,128]{2,1,0:T(8,128)S(1)}) fusion(f32[64,64,9,128]{3,2,1,0:T(8,128)} %reshape.555, f32[64,64,9,128]{3,1,0,2:T(8,128)} %bitcast.414, f32[64,9,128]{2,1,0:T(8,128)S(1)} %copy.352, f32[9]{0:T(128)S(1)} %reshape.554, f32[64,64,128]{2,1,0:T(8,128)S(1)} %bitcast.419, ...), kind=kLoop, calls=%fused_computation.40.clone.1 | loop fusion | flops 50331648 | bytes 46727204 | tf_op jit(solution)/shard_map/while/body/eval_jaxpr/reduce_sum | solution.py:260
  788.8 19.9 %fusion.232 = f32[576,1152]{1,0:T(8,128)} fusion(f32[576,1152]{1,0:T(8,128)S(1)} %fusion.231, f32[512,8,9,128]{3,2,1,0:T(8,128)} %bitcast.416, s32[4096]{0:T(1024)S(1)} %sub.377), kind=kOutput, calls=%fused_computation.66.clone.1 | convolution fusion | flops 5438840832 | bytes 24199168 | tf_op jit(solution)/shard_map/while/body/eval_jaxpr/ew,ef->wf/dot_general | solution.py:270
  886.3 18.7 %copy.350 = f32[4096,1152]{1,0:T(8,128)} copy(f32[4096,1152]{0,1:T(8,128)} %copy-done.3) | data formatting | bytes 37748736 | tf_op jit(solution)/shard_map/while/body/eval_jaxpr/dot_general | solution.py:108
  905.0 24.4 %reshape.555 = f32[64,64,9,128]{3,2,1,0:T(8,128)} reshape(f32[4096,1152]{1,0:T(8,128)} %copy.350) | data formatting | bytes 37748736 | tf_op jit(solution)/shard_map/while/body/eval_jaxpr/reshape | solution.py:108
  948.7 46.5 %fusion.227 = (f32[64,64,128]{2,1,0:T(8,128)S(1)}, f32[64,64,128]{2,1,0:T(8,128)S(1)}, f32[64,64,128]{2,1,0:T(8,128)S(1)}) fusion(f32[64,64,9,128]{3,2,1,0:T(8,128)} %reshape.555, f32[64,64,9,128]{3,1,0,2:T(8,128)} %bitcast.414, f32[64,9,128]{2,1,0:T(8,128)S(1)} %copy.352, f32[9]{0:T(128)S(1)} %reshape.554, f32[64,64,128]{2,1,0:T(8,128)S(1)} %bitcast.419, ...), kind=kLoop, calls=%fused_computation.40.clone.1 | loop fusion | flops 50331648 | bytes 46727204 | tf_op jit(solution)/shard_map/while/body/eval_jaxpr/reduce_sum | solution.py:260
  1037.4 19.9 %fusion.232 = f32[576,1152]{1,0:T(8,128)} fusion(f32[576,1152]{1,0:T(8,128)S(1)} %fusion.231, f32[512,8,9,128]{3,2,1,0:T(8,128)} %bitcast.416, s32[4096]{0:T(1024)S(1)} %sub.377), kind=kOutput, calls=%fused_computation.66.clone.1 | convolution fusion | flops 5438840832 | bytes 24199168 | tf_op jit(solution)/shard_map/while/body/eval_jaxpr/ew,ef->wf/dot_general | solution.py:270
  1134.7 18.7 %copy.350 = f32[4096,1152]{1,0:T(8,128)} copy(f32[4096,1152]{0,1:T(8,128)} %copy-done.3) | data formatting | bytes 37748736 | tf_op jit(solution)/shard_map/while/body/eval_jaxpr/dot_general | solution.py:108
  1153.4 24.4 %reshape.555 = f32[64,64,9,128]{3,2,1,0:T(8,128)} reshape(f32[4096,1152]{1,0:T(8,128)} %copy.350) | data formatting | bytes 37748736 | tf_op jit(solution)/shard_map/while/body/eval_jaxpr/reshape | solution.py:108
  1197.1 46.5 %fusion.227 = (f32[64,64,128]{2,1,0:T(8,128)S(1)}, f32[64,64,128]{2,1,0:T(8,128)S(1)}, f32[64,64,128]{2,1,0:T(8,128)S(1)}) fusion(f32[64,64,9,128]{3,2,1,0:T(8,128)} %reshape.555, f32[64,64,9,128]{3,1,0,2:T(8,128)} %bitcast.414, f32[64,9,128]{2,1,0:T(8,128)S(1)} %copy.352, f32[9]{0:T(128)S(1)} %reshape.554, f32[64,64,128]{2,1,0:T(8,128)S(1)} %bitcast.419, ...), kind=kLoop, calls=%fused_computation.40.clone.1 | loop fusion | flops 50331648 | bytes 46727204 | tf_op jit(solution)/shard_map/while/body/eval_jaxpr/reduce_sum | solution.py:260
  1285.5 19.9 %fusion.232 = f32[576,1152]{1,0:T(8,128)} fusion(f32[576,1152]{1,0:T(8,128)S(1)} %fusion.231, f32[512,8,9,128]{3,2,1,0:T(8,128)} %bitcast.416, s32[4096]{0:T(1024)S(1)} %sub.377), kind=kOutput, calls=%fused_computation.66.clone.1 | convolution fusion | flops 5438840832 | bytes 24199168 | tf_op jit(solution)/shard_map/while/body/eval_jaxpr/ew,ef->wf/dot_general | solution.py:270
  1382.7 18.7 %copy.350 = f32[4096,1152]{1,0:T(8,128)} copy(f32[4096,1152]{0,1:T(8,128)} %copy-done.3) | data formatting | bytes 37748736 | tf_op jit(solution)/shard_map/while/body/eval_jaxpr/dot_general | solution.py:108
  1401.4 24.4 %reshape.555 = f32[64,64,9,128]{3,2,1,0:T(8,128)} reshape(f32[4096,1152]{1,0:T(8,128)} %copy.350) | data formatting | bytes 37748736 | tf_op jit(solution)/shard_map/while/body/eval_jaxpr/reshape | solution.py:108
  1445.1 46.5 %fusion.227 = (f32[64,64,128]{2,1,0:T(8,128)S(1)}, f32[64,64,128]{2,1,0:T(8,128)S(1)}, f32[64,64,128]{2,1,0:T(8,128)S(1)}) fusion(f32[64,64,9,128]{3,2,1,0:T(8,128)} %reshape.555, f32[64,64,9,128]{3,1,0,2:T(8,128)} %bitcast.414, f32[64,9,128]{2,1,0:T(8,128)S(1)} %copy.352, f32[9]{0:T(128)S(1)} %reshape.554, f32[64,64,128]{2,1,0:T(8,128)S(1)} %bitcast.419, ...), kind=kLoop, calls=%fused_computation.40.clone.1 | loop fusion | flops 50331648 | bytes 46727204 | tf_op jit(solution)/shard_map/while/body/eval_jaxpr/reduce_sum | solution.py:260
  1533.6 19.9 %fusion.232 = f32[576,1152]{1,0:T(8,128)} fusion(f32[576,1152]{1,0:T(8,128)S(1)} %fusion.231, f32[512,8,9,128]{3,2,1,0:T(8,128)} %bitcast.416, s32[4096]{0:T(1024)S(1)} %sub.377), kind=kOutput, calls=%fused_computation.66.clone.1 | convolution fusion | flops 5438840832 | bytes 24199168 | tf_op jit(solution)/shard_map/while/body/eval_jaxpr/ew,ef->wf/dot_general | solution.py:270
  1622.7 46.6 %all-reduce = (f32[32,128]{1,0:T(8,128)}, f32[128]{0:T(128)}, f32[256]{0:T(256)}, f32[384]{0:T(512)}) all-reduce(f32[32,128]{1,0:T(8,128)S(1)} %copy-done.76, f32[128]{0:T(128)S(1)} %copy-done.73, f32[256]{0:T(256)S(1)} %copy-done.66, f32[384]{0:T(512)S(1)} %copy-done.60), channel_id=1, replica_groups=mesh['edge'=8,'grp'=4] {'edge','grp'}, use_global_device_ids=true, to_apply=%region_27.28 | all-reduce | flops 4864 | bytes 38912 | tf_op jit(solution)/shard_map/psum | solution.py:330
  1684.6 128.7 %all-reduce.4.cloned.1.call-done = (f32[128,128]{1,0:T(8,128)}, f32[128,128]{1,0:T(8,128)}, f32[128,128]{1,0:T(8,128)}, f32[128,256]{1,0:T(8,128)}, f32[256,384]...) async-done(((f32[128,128]{1,0:T(8,128)}, f32[128,128]{1,0:T(8,128)}, f32[128,128]{1,0:T(8,128)}, f32[128,256]{1,0:T(8,128)}, ...) | async-done | bytes 917520 | tf_op jit(solution)/shard_map/psum | solution.py:330
  (695 shorter events, 881.7 us)
Async XLA Ops:
  7.2 585.4 %copy-start = (bf16[128,128]{1,0:T(8,128)(2,1)S(1)}, bf16[128,128]{1,0:T(8,128)(2,1)}, u32[]{:S(2)}) copy-start(bf16[128,128]{1,0:T(8,128)(2,1)} %param.36) | copy-start | bytes 98308
  7.2 1806.2 %all-reduce.4.cloned.1.call-start = ((), (), s32[]{:S(2)}) async-start(), calls=%async_computation | async-start | bytes 1835008 | tf_op jit(solution)/shard_map/psum | solution.py:330
  12.1 8.5 copy-start.16
  12.1 6.9 collective-permute-start
  14.5 6.1 collective-permute-start.1
  38.4 7.7 copy-start.2
  179.0 7.7 copy-start.2
  319.5 7.7 copy-start.2
  459.9 7.7 copy-start.2
  590.4 7.3 copy-start.34
  604.4 95.4 %copy-start.18 = (bf16[4,64,9,128]{3,1,0,2:T(8,128)(2,1)}, bf16[4,64,9,128]{3,1,0,2:T(8,128)(2,1)S(1)}, u32[]{:S(2)}) copy-start(bf16[4,64,9,128]{3,1,0,2:T(8,128)(2,1)S(1)} %get-tuple-element.1129) | copy-start | bytes 1769476 | tf_op jit(solution)/shard_map/while
  619.1 7.7 copy-start.3
  852.7 95.4 %copy-start.18 = (bf16[4,64,9,128]{3,1,0,2:T(8,128)(2,1)}, bf16[4,64,9,128]{3,1,0,2:T(8,128)(2,1)S(1)}, u32[]{:S(2)}) copy-start(bf16[4,64,9,128]{3,1,0,2:T(8,128)(2,1)S(1)} %get-tuple-element.1129) | copy-start | bytes 1769476 | tf_op jit(solution)/shard_map/while
  867.4 7.7 copy-start.3
  997.7 6.4 copy-start.85
  1101.0 95.5 %copy-start.18 = (bf16[4,64,9,128]{3,1,0,2:T(8,128)(2,1)}, bf16[4,64,9,128]{3,1,0,2:T(8,128)(2,1)S(1)}, u32[]{:S(2)}) copy-start(bf16[4,64,9,128]{3,1,0,2:T(8,128)(2,1)S(1)} %get-tuple-element.1129) | copy-start | bytes 1769476 | tf_op jit(solution)/shard_map/while
  1115.6 7.7 copy-start.3
  1246.0 6.4 copy-start.85
  1349.3 95.3 %copy-start.18 = (bf16[4,64,9,128]{3,1,0,2:T(8,128)(2,1)}, bf16[4,64,9,128]{3,1,0,2:T(8,128)(2,1)S(1)}, u32[]{:S(2)}) copy-start(bf16[4,64,9,128]{3,1,0,2:T(8,128)(2,1)S(1)} %get-tuple-element.1129) | copy-start | bytes 1769476 | tf_op jit(solution)/shard_map/while
  1363.9 7.7 copy-start.3
  1604.2 17.3 copy-start.27
  1604.2 17.3 copy-start.28
  1605.3 17.4 copy-start.60
  1605.3 17.4 copy-start.66
  1605.3 17.4 copy-start.73
  1605.3 17.4 copy-start.76
  1605.3 64.0 %copy-start.9 = (bf16[256,9,128]{2,0,1:T(8,128)(2,1)S(1)}, bf16[256,9,128]{2,0,1:T(8,128)(2,1)}, u32[]{:S(2)}) copy-start(bf16[256,9,128]{2,0,1:T(8,128)(2,1)} %copy-done.8) | copy-start | bytes 1769476
  1605.3 64.0 %copy-start.11 = (f32[256,9,128]{2,0,1:T(8,128)S(1)}, f32[256,9,128]{2,0,1:T(8,128)}, u32[]{:S(2)}) copy-start(f32[256,9,128]{2,0,1:T(8,128)} %copy-done.10) | copy-start | bytes 3538948
  1605.3 67.1 %collective-permute-start.2 = (bf16[256,9,128]{2,0,1:T(8,128)(2,1)}, bf16[256,9,128]{2,0,1:T(8,128)(2,1)}, u32[]{:S(2)}, u32[]{:S(2)}) collective-permute-start(bf16[256,9,128]{2,0,1:T(8,128)(2,1)} %get-tuple-element.753), channel_id=1, source_target_pairs={{1,0},{2,1},{3,2},{4,3},{5,4},{6,5},{7,6},{8,7},{9,8},{10,9},{11,1... | collective-permute-start | bytes 1769480 | tf_op jit(solution)/shard_map/ppermute | solution.py:30
  1606.7 65.6 %collective-permute-start.3 = (bf16[256,9,128]{2,0,1:T(8,128)(2,1)}, bf16[256,9,128]{2,0,1:T(8,128)(2,1)}, u32[]{:S(2)}, u32[]{:S(2)}) collective-permute-start(bf16[256,9,128]{2,0,1:T(8,128)(2,1)} %get-tuple-element.754), channel_id=1, source_target_pairs={{0,1},{1,2},{2,3},{3,4},{4,5},{5,6},{6,7},{7,8},{8,9},{9,10},{10,1... | collective-permute-start | bytes 1769480 | tf_op jit(solution)/shard_map/ppermute | solution.py:30
  1621.5 48.8 %copy-start.7 = (f32[256,9,128]{2,0,1:T(8,128)S(1)}, f32[256,9,128]{2,0,1:T(8,128)}, u32[]{:S(2)}) copy-start(f32[256,9,128]{2,0,1:T(8,128)} %copy-done.6) | copy-start | bytes 3538948
  1681.8 143.8 %copy-start.1 = (bf16[128,128]{1,0:T(8,128)(2,1)S(1)}, bf16[128,128]{1,0:T(8,128)(2,1)}, u32[]{:S(2)}) copy-start(bf16[128,128]{1,0:T(8,128)(2,1)} %param.36) | copy-start | bytes 98308
  (134 other events, 344.0 us)
Sparse Core Ops, SparseCore 0:
  1681.9 131.4 all-reduce.3
where the time goes:
time: 1850 us; the launch traced here: 1830 us
  local copies, waits for them, and re-layouts  788 us (43%)
  other arithmetic  468 us (25%)
  matrix products  341 us (18%)
  waiting for transfers between devices  130 us (7%)
  blocking collectives  46.6 us (3%)
  loops' own time  24.1 us (1%)
  starting transfers between devices  19.9 us (1%)
    reshape x8, local copies, waits for them, and re-layouts, edge_terms(): jnp.dot(table, window, preferred_element_type=jnp.float32)  195 us
    reduce_sum x4, other arithmetic, backward_block(): grad_fac_anti = jnp.sum(grad_wide * anti_src.reshape(block_shape), axis=2)  186 us
    reshape x13, local copies, waits for them, and re-layouts, flip_pairs(): tensor.reshape(leading, 3, 3, -1)  150 us
    dot_general x8, local copies, waits for them, and re-layouts, edge_terms(): jnp.dot(table, window, preferred_element_type=jnp.float32)  149 us
    psum x1, waiting for transfers between devices, local(): lax.psum((grad_w_iso1, grad_w_anti1, grad_w_sym1, radial_grads[0], radial...  129 us
    reduce_sum x4, other arithmetic, combine_messages(): return jnp.sum(summed, axis=1)  126 us
    while x216, local copies, waits for them, and re-layouts  109 us
    dot_general x4, matrix products, backward_block(): jnp.einsum('ew,ef->wf', table, high_part, preferred_element_type=jnp.floa...  79.7 us
  transfers between devices with their start and end apart: 5, of which 2 were waited for; matrix products, arithmetic and copies ran while one was open for 1% of the time, Pallas kernels for 0%

commit v1 on v0

v1 whole, which is shorter than its diff:
```python
import functools
import math

import jax
import jax.numpy as jnp
from jax import lax
from jax.experimental import pallas as pl
from jax.experimental.pallas import tpu as pltpu
from jax.sharding import PartitionSpec as P

MOL_MOST = 256
CUTOFF = 5.0
LANES = 128
GROUP = 8
WINDOW = 256
KIND = (0, 1, 1, 1, 2, 2, 2, 2, 2)
AXES = ("edge", "grp")
F32 = jnp.float32
BF16 = jnp.bfloat16


def col(c):
    return slice(c * LANES, (c + 1) * LANES)


def to_matrix(coords):
    t, a01, a02, a12, s01, s02, s12, s00, s11 = coords
    return [
        [t + s00, s01 + a01, s02 + a02],
        [s01 - a01, t + s11, s12 + a12],
        [s02 - a02, s12 - a12, t - s00 - s11],
    ]


def primal(m):
    t = (m[0][0] + m[1][1] + m[2][2]) * (1.0 / 3.0)
    return [
        t,
        0.5 * (m[0][1] - m[1][0]),
        0.5 * (m[0][2] - m[2][0]),
        0.5 * (m[1][2] - m[2][1]),
        0.5 * (m[0][1] + m[1][0]),
        0.5 * (m[0][2] + m[2][0]),
        0.5 * (m[1][2] + m[2][1]),
        m[0][0] - t,
        m[1][1] - t,
    ]


def dual(m):
    return [
        m[0][0] + m[1][1] + m[2][2],
        m[0][1] - m[1][0],
        m[0][2] - m[2][0],
        m[1][2] - m[2][1],
        m[0][1] + m[1][0],
        m[0][2] + m[2][0],
        m[1][2] + m[2][1],
        m[0][0] - m[2][2],
        m[1][1] - m[2][2],
    ]


def dual_of_primal(c):
    return [3.0 * c[0]] + [2.0 * v for v in c[1:7]] + [2.0 * c[7] + c[8], 2.0 * c[8] + c[7]]


def primal_of_dual(d):
    third = 1.0 / 3.0
    return (
        [d[0] * third]
        + [0.5 * v for v in d[1:7]]
        + [(2.0 * d[7] - d[8]) * third, (2.0 * d[8] - d[7]) * third]
    )


def product(a, b):
    return [
        [a[p][0] * b[0][q] + a[p][1] * b[1][q] + a[p][2] * b[2][q] for q in range(3)]
        for p in range(3)
    ]


def add(a, b):
    return [[a[p][q] + b[p][q] for q in range(3)] for p in range(3)]


def both_ways(a, b):
    return add(product(a, b), product(b, a))


def flip(m):
    return [[m[q][p] for q in range(3)] for p in range(3)]


def flat(m):
    return [m[p][q] for p in range(3) for q in range(3)]


def square(parts):
    return [list(parts[0:3]), list(parts[3:6]), list(parts[6:9])]


def total(values):
    out = values[0]
    for v in values[1:]:
        out = out + v
    return out


def dot(a, b):
    return jnp.dot(a, b, preferred_element_type=F32)


def dot_first(a, b):
    return lax.dot_general(a, b, (((0,), (0,)), ((), ())), preferred_element_type=F32)


def dot_last(a, b):
    return lax.dot_general(a, b, (((1,), (1,)), ((), ())), preferred_element_type=F32)


def by_kind(coords, weights, multiply):
    rows = coords[0].shape[0]
    out = []
    for kind, (lo, hi) in enumerate(((0, 1), (1, 4), (4, 9))):
        stacked = jnp.concatenate([v.astype(BF16) for v in coords[lo:hi]], axis=0)
        result = multiply(stacked, weights[kind])
        out += [result[n * rows : (n + 1) * rows] for n in range(hi - lo)]
    return out


def kind_grads(parts, gradients):
    out = []
    for lo, hi in ((0, 1), (1, 4), (4, 9)):
        left = jnp.concatenate([v.astype(BF16) for v in parts[lo:hi]], axis=0)
        right = jnp.concatenate([v.astype(BF16) for v in gradients[lo:hi]], axis=0)
        out.append(dot_first(left, right))
    return out


def half_silu(u):
    t = jnp.tanh(u)
    v = u * t
    return u + v, (1.0 + t) * (1.0 + u - v)


def parts_kernel(atoms_ref, out_ref):
    values = [atoms_ref[:, col(c)].astype(F32) for c in range(9)]
    scale = 1.0 / (1.0 + total([v * v for v in values]))
    coords = primal(square([v * scale for v in values]))
    for c in range(9):
        out_ref[:, col(c)] = coords[c].astype(BF16)


def main_kernel(
    win_ref, low_ref, own_ref, high_ref, atoms_ref, outgrad_ref, rows_ref,
    w1_ref, w2_ref, b2_ref, w3_ref, b3_ref,
    iso1_ref, anti1_ref, sym1_ref, iso2_ref, anti2_ref, sym2_ref,
    upd_ref, f_ref, gmp_ref, gfp_ref, d3_ref, d2_ref, d1_ref, dw2_ref,
    table, x_s, basis_s, a1_s, l1_s, a2_s, l2_s, l3_s, msg_s, gmd_s,
):
    step = pl.program_id(0)
    chunks, _, edges = rows_ref.shape
    halo = low_ref.shape[0]
    own = own_ref.shape[0]
    atoms = upd_ref.shape[0]
    pairs = edges // 16

    @pl.when(step == 0)
    def _():
        weights = (iso1_ref[...], anti1_ref[...], sym1_ref[...])
        place = 0
        for ref in (low_ref, own_ref, high_ref):
            for c in range(9):
                table[place : place + ref.shape[0], col(c)] = dot(
                    ref[:, col(c)], weights[KIND[c]]
                ).astype(BF16)
            place += ref.shape[0]
        table[place:, :] = jnp.zeros((table.shape[0] - place, table.shape[1]), BF16)
        d3_ref[...] = jnp.zeros_like(d3_ref)
        d2_ref[...] = jnp.zeros_like(d2_ref)
        d1_ref[...] = jnp.zeros_like(d1_ref)
        dw2_ref[...] = jnp.zeros_like(dw2_ref)

    def forward_chunk(j, carry):
        base = pl.multiple_of(j * edges, edges)
        here = pl.ds(base, edges)
        cols = jnp.transpose(rows_ref[j])
        dist, gate, link = cols[:, 0:1], cols[:, 1:2], cols[:, 2:3]
        first = win_ref[step * chunks + j, 0]
        count = win_ref[step * chunks + j, 1]
        near = lax.broadcasted_iota(jnp.int32, (edges, WINDOW), 1).astype(F32)

        def picked(w, accumulate):
            start = pl.multiple_of(first + w * WINDOW, 16)
            hot = (link - start.astype(F32) == near).astype(BF16)
            for lo in range(0, 9 * LANES, 2 * LANES):
                hi = min(lo + 2 * LANES, 9 * LANES)
                got = dot(hot, table[pl.ds(start, WINDOW), lo:hi]).astype(BF16)
                if accumulate:
                    got = x_s[here, lo:hi] + got
                x_s[here, lo:hi] = got

        picked(0, False)

        @pl.loop(1, count)
        def _(w):
            picked(w, True)

        lane = lax.broadcasted_iota(jnp.int32, (edges, LANES), 1)
        off = dist - lane.astype(F32) * (CUTOFF / 31.0)
        basis = jnp.exp(off * off * (-0.5 * (31.0 / CUTOFF) ** 2))
        basis = jnp.where(lane < 32, basis, jnp.where(lane == 32, 1.0, 0.0)).astype(BF16)
        basis_s[here, :] = basis
        act, slope = half_silu(dot(basis, w1_ref[...]))
        act1 = act.astype(BF16)
        a1_s[here, :] = act1
        l1_s[here, :] = slope.astype(BF16)
        act, slope = half_silu(dot(act1, w2_ref[...]) + b2_ref[...])
        act2 = act.astype(BF16)
        a2_s[here, :] = act2
        l2_s[here, :] = slope.astype(BF16)
        act, slope = half_silu(dot(act2, w3_ref[...]) + b3_ref[...])
        factors = act * gate
        f_ref[here, :] = factors.astype(BF16)
        l3_s[here, :] = (slope * (0.5 * gate)).astype(BF16)
        for c in range(9):
            terms = factors[:, col(KIND[c])] * x_s[here, col(c)].astype(F32)
            msg_s[pl.ds(pl.multiple_of(j * GROUP, GROUP), GROUP), col(c)] = jnp.sum(
                terms.reshape(edges // GROUP, GROUP, LANES), axis=0
            )
        return carry

    lax.fori_loop(0, chunks, forward_chunk, 0)

    weights2 = (iso2_ref[...], anti2_ref[...], sym2_ref[...])
    at = pl.ds(pl.multiple_of(halo + step * atoms, 16), atoms)
    mixed = to_matrix([table[at, col(c)].astype(F32) for c in range(9)])
    messages = to_matrix([msg_s[:, col(c)] for c in range(9)])
    paired = both_ways(mixed, messages)
    inverse = 1.0 / (1.0 + total([v * v for v in flat(paired)]))
    pair_coords = primal(paired)
    mid = [v * inverse for v in pair_coords]
    update = to_matrix(by_kind(mid, weights2, dot))
    values = [atoms_ref[:, col(c)].astype(F32) for c in range(9)]
    inverse_in = 1.0 / (1.0 + total([v * v for v in values]))
    squared = flat(product(update, update))
    for c, (v, u, s) in enumerate(zip(values, flat(update), squared)):
        upd_ref[:, col(c)] = (v * inverse_in + u + s).astype(BF16)
    out_grad = square([outgrad_ref[:, col(c)].astype(F32) for c in range(9)])
    grad_update = add(out_grad, both_ways(out_grad, flip(update)))
    grad_dual = [v.astype(BF16) for v in dual(grad_update)]
    for kind, grad in enumerate(kind_grads(mid, grad_dual)):
        dw2_ref[kind * LANES : (kind + 1) * LANES, :] += grad
    mid_dual = by_kind(grad_dual, weights2, dot_last)
    projected = total([a * b for a, b in zip(mid_dual, pair_coords)]) * (2.0 * inverse * inverse)
    grad_paired = to_matrix([v * inverse for v in primal_of_dual(mid_dual)])
    grad_paired = [
        [grad_paired[p][q] - paired[p][q] * projected for q in range(3)] for p in range(3)
    ]
    grad_messages = both_ways(flip(mixed), grad_paired)
    from_pair = primal(both_ways(grad_paired, flip(messages)))
    for c in range(9):
        gfp_ref[:, col(c)] = from_pair[c]
    for c, (a, b) in enumerate(zip(dual(grad_messages), primal(grad_messages))):
        for ref, v in ((gmd_s, a), (gmp_ref, b)):
            twice = v.reshape(chunks, 1, GROUP, LANES)
            twice = jnp.concatenate([twice, twice], axis=1).reshape(2 * atoms, LANES)
            ref[:, col(c)] = twice.astype(BF16)

    def backward_chunk(j, carry):
        base = pl.multiple_of(j * edges, edges)
        here = pl.ds(base, edges)
        two = pl.ds(pl.multiple_of(j * 2 * GROUP, 2 * GROUP), 2 * GROUP)
        terms = [
            x_s[here, col(c)].reshape(pairs, 16, LANES) * gmd_s[two, col(c)][None]
            for c in range(9)
        ]
        grads = [terms[0], total(terms[1:4]), total(terms[4:9])]
        grad3 = jnp.concatenate([g.reshape(edges, LANES) for g in grads], axis=1) * l3_s[here, :]
        ones = jnp.ones((16, edges), BF16)
        act2 = jnp.concatenate([jnp.transpose(a2_s[here, :]), ones], axis=0)
        d3_ref[...] += dot(act2, grad3)
        grad2 = dot_last(grad3, w3_ref[...]).astype(BF16) * l2_s[here, :]
        act1 = jnp.concatenate([jnp.transpose(a1_s[here, :]), ones], axis=0)
        d2_ref[...] += dot(act1, grad2)
        grad1 = dot_last(grad2, w2_ref[...]).astype(BF16) * l1_s[here, :]
        d1_ref[...] += dot(jnp.transpose(basis_s[here, :]), grad1)
        return carry

    lax.fori_loop(0, chunks, backward_chunk, 0)


def scatter_kernel(
    win_ref, low_ref, own_ref, high_ref, rows_ref, f_ref, gmp_ref, gfp_ref,
    rim_low_ref, own_out_ref, rim_high_ref, dw1_ref,
    spread,
):
    step = pl.program_id(0)
    chunks, _, edges = rows_ref.shape
    halo = low_ref.shape[0]
    own = own_ref.shape[0]
    pairs = edges // 16

    @pl.when(step == 0)
    def _():
        spread[...] = jnp.zeros_like(spread)
        spread[halo : halo + own, :] = gfp_ref[...]

    def chunk(j, carry):
        here = pl.ds(pl.multiple_of(j * edges, edges), edges)
        two = pl.ds(pl.multiple_of(j * 2 * GROUP, 2 * GROUP), 2 * GROUP)
        link = rows_ref[j][2:3, :]
        first = win_ref[step * chunks + j, 0]
        count = win_ref[step * chunks + j, 1]
        factors = [f_ref[here, col(k)].reshape(pairs, 16, LANES) for k in range(3)]
        values = jnp.concatenate(
            [
                (factors[KIND[c]] * gmp_ref[two, col(c)][None]).reshape(edges, LANES)
                for c in range(9)
            ],
            axis=1,
        )
        near = lax.broadcasted_iota(jnp.int32, (WINDOW, edges), 0).astype(F32)

        @pl.loop(0, count)
        def _(w):
            start = pl.multiple_of(first + w * WINDOW, 16)
            hot = (link - start.astype(F32) == near).astype(BF16)
            spread[pl.ds(start, WINDOW), :] += dot(hot, values)

        return carry

    lax.fori_loop(0, chunks, chunk, 0)

    @pl.when(step == pl.num_programs(0) - 1)
    def _():
        grads = [None] * 3
        place = 0
        for ref, out in ((low_ref, rim_low_ref), (own_ref, own_out_ref), (high_ref, rim_high_ref)):
            rows = ref.shape[0]
            coords = [spread[place : place + rows, col(c)] for c in range(9)]
            for c in range(9):
                out[:, col(c)] = coords[c].astype(out.dtype)
            fresh = kind_grads([ref[:, col(c)] for c in range(9)], dual_of_primal(coords))
            grads = [n if o is None else o + n for o, n in zip(grads, fresh)]
            place += rows
        for kind in range(3):
            dw1_ref[kind * LANES : (kind + 1) * LANES, :] = grads[kind]


def final_kernel(
    own_ref, above_ref, below_ref, atoms_ref, outgrad_ref, iso1_ref, anti1_ref, sym1_ref, out_ref
):
    weights = (iso1_ref[...], anti1_ref[...], sym1_ref[...])
    grad_mixed = [
        own_ref[:, col(c)] + above_ref[:, col(c)].astype(F32) + below_ref[:, col(c)].astype(F32)
        for c in range(9)
    ]
    back = flat(to_matrix(by_kind(grad_mixed, weights, dot_last)))
    values = [atoms_ref[:, col(c)].astype(F32) for c in range(9)]
    inverse = 1.0 / (1.0 + total([v * v for v in values]))
    grad = [outgrad_ref[:, col(c)].astype(F32) + back[c] for c in range(9)]
    along = total([g * v for g, v in zip(grad, values)]) * (2.0 * inverse)
    for c in range(9):
        out_ref[:, col(c)] = (grad[c] - values[c] * along) * inverse


def whole(shape):
    return pl.BlockSpec(shape, lambda *_: (0,) * len(shape))


def block(shape):
    return pl.BlockSpec(shape, lambda i, *_: (i,) + (0,) * (len(shape) - 1))


def shape_of(shape, kind):
    return jax.ShapeDtypeStruct(shape, kind)


def reduce_everywhere(value, axes):
    peers = math.prod(lax.axis_size(a) for a in axes)
    rows = value.shape[0]
    share = -(-rows // (peers * 8)) * 8
    padded = jnp.pad(value, ((0, share * peers - rows), (0, 0))).astype(BF16)
    mine = lax.all_to_all(padded.reshape(peers, share, -1), axes, 0, 0, tiled=True)
    summed = jnp.sum(mine.astype(F32), axis=0).astype(BF16)
    copies = jnp.broadcast_to(summed[None], (peers,) + summed.shape)
    back = lax.all_to_all(copies, axes, 0, 0, tiled=True)
    return back.reshape(share * peers, -1)[:rows].astype(F32)


def local(
    atoms, neighbours, live_mask, distances,
    w_iso1, w_anti1, w_sym1, w_rad1, b_rad1, w_rad2, b_rad2, w_rad3, b_rad3,
    w_iso2, w_anti2, w_sym2, out_grad,
):
    rows, _, channels = atoms.shape
    slots = neighbours.shape[1]
    halo = MOL_MOST
    wide = 9 * channels
    ext = rows + 2 * halo
    edges = GROUP * slots
    chunk_count = rows // GROUP
    steps = 4
    chunks = chunk_count // steps
    block_atoms = rows // steps
    block_edges = block_atoms * slots
    vmem = 56 * 1024 * 1024
    me = lax.axis_index(AXES)
    peers = math.prod(lax.axis_size(a) for a in AXES)
    up = [(i, i + 1) for i in range(peers - 1)]
    down = [(i + 1, i) for i in range(peers - 1)]

    atoms_flat = atoms.reshape(rows, wide)
    out_grad_flat = out_grad.reshape(rows, wide)
    own = pl.pallas_call(
        parts_kernel,
        out_shape=shape_of((rows, wide), BF16),
        compiler_params=pltpu.CompilerParams(vmem_limit_bytes=vmem),
        name="parts",
    )(atoms_flat)
    low = lax.ppermute(own, AXES, up)
    high = lax.ppermute(own, AXES, down)

    links = neighbours - (me * rows - halo)
    gating = 0.5 * (jnp.cos(math.pi * distances / CUTOFF) + 1.0) * live_mask.astype(F32)

    def as_rows(v):
        return jnp.swapaxes(v.reshape(chunk_count, GROUP, slots), 1, 2).reshape(
            chunk_count, 1, edges
        )

    edge_rows = jnp.concatenate(
        [as_rows(distances), as_rows(gating), as_rows(links.astype(F32))]
        + [jnp.zeros((chunk_count, 5, edges), F32)],
        axis=1,
    )
    grouped = links.reshape(chunk_count, edges)
    first = jnp.min(grouped, axis=1) // 16 * 16
    count = (jnp.max(grouped, axis=1) - first) // WINDOW + 1
    windows = jnp.stack([first, count], axis=1)

    w1_ext = jnp.zeros((LANES, channels), F32)
    w1_ext = w1_ext.at[: w_rad1.shape[0]].set(0.5 * w_rad1.astype(F32))
    w1_ext = w1_ext.at[w_rad1.shape[0]].set(0.5 * b_rad1.astype(F32)).astype(BF16)
    w2_half = (0.5 * w_rad2.astype(F32)).astype(BF16)
    w3_half = (0.5 * w_rad3.astype(F32)).astype(BF16)
    b2_half = 0.5 * b_rad2.astype(F32)[None]
    b3_half = 0.5 * b_rad3.astype(F32)[None]

    mid_width, last_width = w_rad2.shape[1], w_rad3.shape[1]
    small = whole((channels, channels))
    smem = pl.BlockSpec(memory_space=pltpu.SMEM)
    updated, factors, gmp, gfp, d3, d2, d1, dw2 = pl.pallas_call(
        main_kernel,
        grid=(steps,),
        in_specs=[
            smem, whole((halo, wide)), whole((rows, wide)), whole((halo, wide)),
            block((block_atoms, wide)), block((block_atoms, wide)), block((chunks, 8, edges)),
            whole((LANES, channels)), whole((channels, mid_width)), whole((1, mid_width)),
            whole((mid_width, last_width)), whole((1, last_width)),
            small, small, small, small, small, small,
        ],
        out_specs=[
            block((block_atoms, wide)), block((block_edges, last_width)),
            block((2 * block_atoms, wide)), block((block_atoms, wide)),
            whole((mid_width + 16, last_width)), whole((channels + 16, mid_width)),
            whole((LANES, channels)), whole((3 * channels, channels)),
        ],
        out_shape=[
            shape_of((rows, wide), BF16), shape_of((rows * slots, last_width), BF16),
            shape_of((2 * rows, wide), BF16), shape_of((rows, wide), F32),
            shape_of((mid_width + 16, last_width), F32), shape_of((channels + 16, mid_width), F32),
            shape_of((LANES, channels), F32), shape_of((3 * channels, channels), F32),
        ],
        scratch_shapes=[
            pltpu.VMEM((ext + WINDOW, wide), BF16),
            pltpu.VMEM((block_edges, wide), BF16),
            pltpu.VMEM((block_edges, LANES), BF16),
            pltpu.VMEM((block_edges, channels), BF16),
            pltpu.VMEM((block_edges, channels), BF16),
            pltpu.VMEM((block_edges, mid_width), BF16),
            pltpu.VMEM((block_edges, mid_width), BF16),
            pltpu.VMEM((block_edges, last_width), BF16),
            pltpu.VMEM((block_atoms, wide), F32),
            pltpu.VMEM((2 * block_atoms, wide), BF16),
        ],
        compiler_params=pltpu.CompilerParams(vmem_limit_bytes=vmem),
        name="main",
    )(
        windows, low, own, high, atoms_flat, out_grad_flat, edge_rows,
        w1_ext, w2_half, b2_half, w3_half, b3_half,
        w_iso1, w_anti1, w_sym1, w_iso2, w_anti2, w_sym2,
    )

    rim_low, own_grad, rim_high, dw1 = pl.pallas_call(
        scatter_kernel,
        grid=(steps,),
        in_specs=[
            smem, whole((halo, wide)), whole((rows, wide)), whole((halo, wide)),
            block((chunks, 8, edges)), block((block_edges, last_width)),
            block((2 * block_atoms, wide)), whole((rows, wide)),
        ],
        out_specs=[
            whole((halo, wide)), whole((rows, wide)), whole((halo, wide)),
            whole((3 * channels, channels)),
        ],
        out_shape=[
            shape_of((halo, wide), BF16), shape_of((rows, wide), F32),
            shape_of((halo, wide), BF16), shape_of((3 * channels, channels), F32),
        ],
        scratch_shapes=[pltpu.VMEM((ext + WINDOW, wide), F32)],
        compiler_params=pltpu.CompilerParams(vmem_limit_bytes=vmem),
        name="scatter",
    )(windows, low, own, high, edge_rows, factors, gmp, gfp)

    above = lax.ppermute(rim_low, AXES, down)
    below = lax.ppermute(rim_high, AXES, up)

    grad_atoms = pl.pallas_call(
        final_kernel,
        out_shape=shape_of((rows, wide), F32),
        compiler_params=pltpu.CompilerParams(vmem_limit_bytes=vmem),
        name="final",
    )(own_grad, above, below, atoms_flat, out_grad_flat, w_iso1, w_anti1, w_sym1)

    basis_count = w_rad1.shape[0]
    pieces = [dw1, dw2, d1[:basis_count], d1[basis_count : basis_count + 1]]
    pieces += [d2[:channels, col(n)] for n in range(mid_width // LANES)]
    pieces += [d2[channels : channels + 1, col(n)] for n in range(mid_width // LANES)]
    pieces += [d3[:mid_width, col(n)] for n in range(last_width // LANES)]
    pieces += [d3[mid_width : mid_width + 1, col(n)] for n in range(last_width // LANES)]
    summed = reduce_everywhere(jnp.concatenate(pieces, axis=0), AXES)
    place = 0

    def take(count, lanes):
        nonlocal place
        got = []
        for _ in range(lanes // LANES):
            got.append(summed[place : place + count])
            place += count
        return jnp.concatenate(got, axis=1) if len(got) > 1 else got[0]

    small_grads = [take(channels, LANES) for _ in range(6)]
    g_w1 = take(basis_count, LANES)
    g_b1 = take(1, LANES)[0]
    g_w2 = take(channels, mid_width)
    g_b2 = take(1, mid_width)[0]
    g_w3 = take(mid_width, last_width)
    g_b3 = take(1, last_width)[0]
    return (
        updated.reshape(atoms.shape),
        grad_atoms.reshape(atoms.shape),
        *small_grads[:3],
        g_w1, g_b1, g_w2, g_b2, g_w3, g_b3,
        *small_grads[3:],
    )


def solution(mesh):
    split3 = P(AXES, None, None)
    split2 = P(AXES, None)
    return jax.shard_map(
        local,
        mesh=mesh,
        in_specs=(split3, split2, split2, split2) + (P(),) * 12 + (split3,),
        out_specs=(split3, split3) + (P(),) * 12,
        check_vma=False,
    )
```

time: 1850 us -> 245 us (0.13)
  the two profiles are of different devices: /device:TPU:0 before, /device:TPU:13 now
where the time goes in v1:
time: 245 us; the launch traced here: 246 us
  Pallas kernels  166 us (68%)
  waiting for transfers between devices  19.1 us (8%)
  local copies, waits for them, and re-layouts  18 us (7%)
  blocking collectives  16.4 us (7%)
  starting transfers between devices  16 us (7%)
  other arithmetic  9.29 us (4%)
    pallas_call x1, Pallas kernels, local(): pl.pallas_call(main_kernel, grid=(steps,), in_specs=[smem, whole((halo, w...  117 us
    pallas_call x1, Pallas kernels, local(): pl.pallas_call(scatter_kernel, grid=(steps,), in_specs=[smem, whole((halo...  43.4 us
    all_to_all x1, blocking collectives, reduce_everywhere(): lax.all_to_all(padded.reshape(peers, share, -1), axes, 0, 0, tiled=True)  16.4 us
    ppermute x1, waiting for transfers between devices, local(): above = lax.ppermute(rim_low, AXES, down)  14.4 us
    unnamed x42, local copies, waits for them, and re-layouts  6.29 us
  transfers between devices with their start and end apart: 5, of which 2 were waited for; matrix products, arithmetic and copies ran while one was open for 5% of the time, Pallas kernels for 2%

profile of v1, /device:TPU:13, one launch (start us, length us, event | category | flops | bytes accessed | tf_op | source)
XLA Modules:
  0.0 245.6 jit_solution(17804812869004629044)
XLA Ops:
  0.6 1.3 copy.93
  2.0 1.1 copy.94.atoms_ref
  3.1 2.2 parts.1.own_ref
  5.3 2.6 %collective-permute-start.1 = (bf16[256,1152]{1,0:T(8,128)(2,1)}, bf16[256,1152]{1,0:T(8,128)(2,1)S(1)}, u32[]{:S(2)}, u32[]{:S(2)}) collective-permute-start(bf16[256,1152]{1,0:T(8,128)(2,1)} %parts.1.own_ref), channel_id=1, source_target_pairs={{1,0},{2,1},{3,2},{4,3},{5,4},{6,5},{7,6},{8,7},{9,8},{10,9},{11,1... | collective-permute-start | bytes 1769480 | tf_op jit(solution)/shard_map/ppermute | solution.py:425
  7.9 3.0 %collective-permute-start = (bf16[256,1152]{1,0:T(8,128)(2,1)}, bf16[256,1152]{1,0:T(8,128)(2,1)S(1)}, u32[]{:S(2)}, u32[]{:S(2)}) collective-permute-start(bf16[256,1152]{1,0:T(8,128)(2,1)} %parts.1.own_ref), channel_id=1, source_target_pairs={{0,1},{1,2},{2,3},{3,4},{4,5},{5,6},{6,7},{7,8},{8,9},{9,10},{10,1... | collective-permute-start | bytes 1769480 | tf_op jit(solution)/shard_map/ppermute | solution.py:424
  13.7 0.7 copy.104.win_ref
  15.2 1.1 copy.106.outgrad_ref
  17.0 0.7 multiply_convert_fusion.w3_ref
  17.7 1.0 maximum_maximum_fusion.rows_ref
  18.7 4.6 %collective-permute-done.1.high_ref = bf16[256,1152]{1,0:T(8,128)(2,1)S(1)} collective-permute-done((bf16[256,1152]{1,0:T(8,128)(2,1)}, bf16[256,1152]{1,0:T(8,128)(2,1)S(1)}, u32[]{:S(2)}, u32[]{:S(2)}) %collective-permute-start.1) | collective-permute-done | bytes 589856 | tf_op jit(solution)/shard_map/ppermute | solution.py:425
  23.3 0.8 copy-done
  24.3 116.5 %main.1 = (bf16[256,1152]{1,0:T(8,128)(2,1)}, bf16[16384,384]{1,0:T(8,128)(2,1)}, bf16[512,1152]{1,0:T(8,128)(2,1)}, f32[256,1152]{1,0:T(8,128)}, f32[272,384]{1...) custom-call(s32[32,2]{1,0:T(8,128)} %copy.104.win_ref, bf16[256,1152]{1,0:T(8,128)(2,1)} %copy-done.1, ...), custom_call_target="tpu_custom_call" | custom-call | tf_op jit(solution)/shard_map/main/pallas_call | solution.py:456
  140.9 1.0 convert.40
  141.9 1.0 convert.41
  143.0 0.7 slice.197
  143.7 43.4 %scatter.13 = (bf16[256,1152]{1,0:T(8,128)(2,1)}, f32[256,1152]{1,0:T(8,128)}, bf16[256,1152]{1,0:T(8,128)(2,1)}, f32[384,128]{1,0:T(8,128)}) custom-call(s32[32,2]{1,0:T(8,128)} %copy.104.win_ref, bf16[256,1152]{1,0:T(8,128)(2,1)} %copy-done.1, bf16[256,1152]{1,0:T(8,128)(2,1)} %parts.1.own_ref, bf16[256,1152]{1,0:T(8,128)(2,1)} %copy-done, ...), custom_call_target="tpu_custom_call" | custom-call | tf_op jit(solution)/shard_map/scatter/pallas_call | solution.py:498
  187.2 0.9 convert.37
  188.1 1.6 concatenate.25
  189.7 16.4 %all_to_all.10 = bf16[32,64,128]{2,1,0:T(8,128)(2,1)S(1)} all-to-all(bf16[32,64,128]{2,1,0:T(8,128)(2,1)S(1)} %bitcast.47), channel_id=1, replica_groups=mesh['edge'=8,'grp'=4] {'edge','grp'}, dimensions={0} | all-to-all | bytes 1048576 | tf_op jit(solution)/shard_map/all_to_all | solution.py:387
  206.2 0.9 broadcast_in_dim.5
  207.1 4.9 %all-to-all-start.1 = ((bf16[32,64,128]{2,1,0:T(8,128)(2,1)}), bf16[32,64,128]{2,1,0:T(8,128)(2,1)S(1)}, u32[]{:S(2)}, u32[]{:S(2)}) async-start(bf16[32,64,128]{2,1,0:T(8,128)(2,1)} %broadcast_in_dim.5), calls=%async_computation.1 | async-start | bytes 1048576 | tf_op jit(solution)/shard_map/all_to_all | solution.py:390
  212.0 2.3 collective-permute-start.2
  214.3 3.3 %collective-permute-start.3 = (bf16[256,1152]{1,0:T(8,128)(2,1)S(1)}, bf16[256,1152]{1,0:T(8,128)(2,1)S(1)}, u32[]{:S(2)}, u32[]{:S(2)}) collective-permute-start(bf16[256,1152]{1,0:T(8,128)(2,1)S(1)} %copy-done.15), channel_id=1, source_target_pairs={{0,1},{1,2},{2,3},{3,4},{4,5},{5,6},{6,7},{7,8},{8,9},{9,10},{10,1... | collective-permute-start | bytes 1769480 | tf_op jit(solution)/shard_map/ppermute | solution.py:520
  217.8 1.1 copy.112
  218.9 14.4 %collective-permute-done.2.above_ref = bf16[256,1152]{1,0:T(8,128)(2,1)S(1)} collective-permute-done((bf16[256,1152]{1,0:T(8,128)(2,1)}, bf16[256,1152]{1,0:T(8,128)(2,1)S(1)}, u32[]{:S(2)}, u32[]{:S(2)}) %collective-permute-start.2) | collective-permute-done | bytes 589856 | tf_op jit(solution)/shard_map/ppermute | solution.py:519
  233.3 0.8 copy-done.2
  234.3 3.7 %final.1 = f32[256,1152]{1,0:T(8,128)} custom-call(f32[256,1152]{1,0:T(8,128)} %get-tuple-element.54.own_ref, bf16[256,1152]{1,0:T(8,128)(2,1)} %copy-done.2, bf16[256,1152]{1,0:T(8,128)(2,1)} %copy-done.3, bf16[256,1152]{1,0:T(8,128)(2,1)} %copy.94.atoms_ref, bf16[256,1152]{1,0:T(8,128)(2,1)} %copy.106.outgrad_ref, bf16[128,128]{1,0:T(8,128)(2,1)} %iso1_ref.3, ...), custom_call_target="tpu_custom_call" | custom-call | tf_op jit(solution)/shard_map/final/pallas_call | solution.py:522
  238.1 1.6 copy.111
  239.7 1.4 copy.113
  242.3 0.7 fusion.2
  243.6 0.7 pad_maximum_fusion.1
  244.9 0.8 pad_maximum_fusion
  (78 shorter events, 7.4 us)
Async XLA Ops:
  1.9 9.0 %copy-start.16 = (bf16[128]{0:T(256)(128)(2,1)S(1)}, bf16[128]{0:T(256)(128)(2,1)}, u32[]{:S(2)}) copy-start(bf16[128]{0:T(256)(128)(2,1)} %param.29) | copy-start | bytes 772
  2.0 9.0 %copy-start.14 = (bf16[384]{0:T(512)(128)(2,1)S(1)}, bf16[384]{0:T(512)(128)(2,1)}, u32[]{:S(2)}) copy-start(bf16[384]{0:T(512)(128)(2,1)} %param.33) | copy-start | bytes 2308
  2.0 9.6 %copy-start.13 = (bf16[32,128]{1,0:T(8,128)(2,1)S(1)}, bf16[32,128]{1,0:T(8,128)(2,1)}, u32[]{:S(2)}) copy-start(bf16[32,128]{1,0:T(8,128)(2,1)} %param.28) | copy-start | bytes 24580
  2.0 9.6 %copy-start.6 = (f32[256,64]{0,1:T(8,128)S(1)}, f32[256,64]{0,1:T(8,128)}, u32[]{:S(2)}) copy-start(f32[256,64]{0,1:T(8,128)} %param.24) | copy-start | bytes 196612
  2.0 9.6 %copy-start.10 = (s32[256,64]{0,1:T(8,128)S(1)}, s32[256,64]{0,1:T(8,128)}, u32[]{:S(2)}) copy-start(s32[256,64]{0,1:T(8,128)} %param.23) | copy-start | bytes 196612
  3.1 8.9 %copy-start.12 = (bf16[128,256]{1,0:T(8,128)(2,1)S(1)}, bf16[128,256]{1,0:T(8,128)(2,1)}, u32[]{:S(2)}) copy-start(bf16[128,256]{1,0:T(8,128)(2,1)} %param.30) | copy-start | bytes 196612
  3.1 9.8 %copy-start.11 = (s32[256,64]{0,1:T(8,128)S(1)}, s32[256,64]{0,1:T(8,128)}, u32[]{:S(2)}) copy-start(s32[256,64]{0,1:T(8,128)} %param.22) | copy-start | bytes 196612
  5.3 18.0 %collective-permute-start.1 = (bf16[256,1152]{1,0:T(8,128)(2,1)}, bf16[256,1152]{1,0:T(8,128)(2,1)S(1)}, u32[]{:S(2)}, u32[]{:S(2)}) collective-permute-start(bf16[256,1152]{1,0:T(8,128)(2,1)} %parts.1.own_ref), channel_id=1, source_target_pairs={{1,0},{2,1},{3,2},{4,3},{5,4},{6,5},{7,6},{8,7},{9,8},{10,9},{11,1... | collective-permute-start | bytes 1769480 | tf_op jit(solution)/shard_map/ppermute | solution.py:425
  7.9 15.4 %collective-permute-start = (bf16[256,1152]{1,0:T(8,128)(2,1)}, bf16[256,1152]{1,0:T(8,128)(2,1)S(1)}, u32[]{:S(2)}, u32[]{:S(2)}) collective-permute-start(bf16[256,1152]{1,0:T(8,128)(2,1)} %parts.1.own_ref), channel_id=1, source_target_pairs={{0,1},{1,2},{2,3},{3,4},{4,5},{5,6},{6,7},{7,8},{8,9},{9,10},{10,1... | collective-permute-start | bytes 1769480 | tf_op jit(solution)/shard_map/ppermute | solution.py:424
  12.8 2.1 copy-start.4
  14.9 1.4 copy-start.17
  14.9 2.0 copy-start.7
  16.4 6.9 %copy-start.9 = (bf16[128,128]{1,0:T(8,128)(2,1)}, bf16[128,128]{1,0:T(8,128)(2,1)S(1)}, u32[]{:S(2)}) copy-start(bf16[128,128]{1,0:T(8,128)(2,1)S(1)} %scatter.12.w1_ref) | copy-start | bytes 98308
  23.3 0.8 copy-start
  23.3 1.0 copy-start.1
  140.9 2.8 %copy-start.8 = (f32[384,128]{1,0:T(8,128)S(1)}, f32[384,128]{1,0:T(8,128)}, u32[]{:S(2)}) copy-start(f32[384,128]{1,0:T(8,128)} %get-tuple-element.58) | copy-start | bytes 589828
  206.1 8.2 %copy-start.15 = (bf16[256,1152]{1,0:T(8,128)(2,1)S(1)}, bf16[256,1152]{1,0:T(8,128)(2,1)}, u32[]{:S(2)}) copy-start(bf16[256,1152]{1,0:T(8,128)(2,1)} %get-tuple-element.56) | copy-start | bytes 1769476
  206.1 11.5 %copy-start.5 = (bf16[256,1152]{1,0:T(8,128)(2,1)S(1)}, bf16[256,1152]{1,0:T(8,128)(2,1)}, u32[]{:S(2)}) copy-start(bf16[256,1152]{1,0:T(8,128)(2,1)} %get-tuple-element.50) | copy-start | bytes 1769476
  207.1 34.0 %all-to-all-start.1 = ((bf16[32,64,128]{2,1,0:T(8,128)(2,1)}), bf16[32,64,128]{2,1,0:T(8,128)(2,1)S(1)}, u32[]{:S(2)}, u32[]{:S(2)}) async-start(bf16[32,64,128]{2,1,0:T(8,128)(2,1)} %broadcast_in_dim.5), calls=%async_computation.1 | async-start | bytes 1048576 | tf_op jit(solution)/shard_map/all_to_all | solution.py:390
  212.0 21.3 %collective-permute-start.2 = (bf16[256,1152]{1,0:T(8,128)(2,1)}, bf16[256,1152]{1,0:T(8,128)(2,1)S(1)}, u32[]{:S(2)}, u32[]{:S(2)}) collective-permute-start(bf16[256,1152]{1,0:T(8,128)(2,1)} %get-tuple-element.55), channel_id=1, source_target_pairs={{1,0},{2,1},{3,2},{4,3},{5,4},{6,5},{7,6},{8,7},{9,8},{10,9},{11,1... | collective-permute-start | bytes 1769480 | tf_op jit(solution)/shard_map/ppermute | solution.py:519
  214.3 19.0 %collective-permute-start.3 = (bf16[256,1152]{1,0:T(8,128)(2,1)S(1)}, bf16[256,1152]{1,0:T(8,128)(2,1)S(1)}, u32[]{:S(2)}, u32[]{:S(2)}) collective-permute-start(bf16[256,1152]{1,0:T(8,128)(2,1)S(1)} %copy-done.15), channel_id=1, source_target_pairs={{0,1},{1,2},{2,3},{3,4},{4,5},{5,6},{6,7},{7,8},{8,9},{9,10},{10,1... | collective-permute-start | bytes 1769480 | tf_op jit(solution)/shard_map/ppermute | solution.py:520
  233.3 0.8 copy-start.2
  233.3 1.0 copy-start.3

commit v2 on v1

v2 whole, which is shorter than its diff:
```python
import functools
import math

import jax
import jax.numpy as jnp
from jax import lax
from jax.experimental import pallas as pl
from jax.experimental.pallas import tpu as pltpu
from jax.sharding import PartitionSpec as P

MOL_MOST = 256
CUTOFF = 5.0
LANES = 128
GROUP = 8
BASES = 32
UNROLL = 2
PAIRS = ((0, 1), (2, 3), (4, 5), (6, 7), (8,))
SCHEDULE = "".join(n + s for n in "01" for s in "HaTDb0G1cWd2E3eF4xVyUz")
WINDOW = 256
KIND = (0, 1, 1, 1, 2, 2, 2, 2, 2)
AXES = ("edge", "grp")
F32 = jnp.float32
BF16 = jnp.bfloat16


def col(c):
    return slice(c * LANES, (c + 1) * LANES)


def to_matrix(coords):
    t, a01, a02, a12, s01, s02, s12, s00, s11 = coords
    return [
        [t + s00, s01 + a01, s02 + a02],
        [s01 - a01, t + s11, s12 + a12],
        [s02 - a02, s12 - a12, t - s00 - s11],
    ]


def primal(m):
    t = (m[0][0] + m[1][1] + m[2][2]) * (1.0 / 3.0)
    return [
        t,
        0.5 * (m[0][1] - m[1][0]),
        0.5 * (m[0][2] - m[2][0]),
        0.5 * (m[1][2] - m[2][1]),
        0.5 * (m[0][1] + m[1][0]),
        0.5 * (m[0][2] + m[2][0]),
        0.5 * (m[1][2] + m[2][1]),
        m[0][0] - t,
        m[1][1] - t,
    ]


def dual(m):
    return [
        m[0][0] + m[1][1] + m[2][2],
        m[0][1] - m[1][0],
        m[0][2] - m[2][0],
        m[1][2] - m[2][1],
        m[0][1] + m[1][0],
        m[0][2] + m[2][0],
        m[1][2] + m[2][1],
        m[0][0] - m[2][2],
        m[1][1] - m[2][2],
    ]


def primal_of_dual(d):
    third = 1.0 / 3.0
    return (
        [d[0] * third]
        + [0.5 * v for v in d[1:7]]
        + [(2.0 * d[7] - d[8]) * third, (2.0 * d[8] - d[7]) * third]
    )


def product(a, b):
    return [
        [a[p][0] * b[0][q] + a[p][1] * b[1][q] + a[p][2] * b[2][q] for q in range(3)]
        for p in range(3)
    ]


def add(a, b):
    return [[a[p][q] + b[p][q] for q in range(3)] for p in range(3)]


def both_ways(a, b):
    return add(product(a, b), product(b, a))


def flip(m):
    return [[m[q][p] for q in range(3)] for p in range(3)]


def flat(m):
    return [m[p][q] for p in range(3) for q in range(3)]


def square(parts):
    return [list(parts[0:3]), list(parts[3:6]), list(parts[6:9])]


def total(values):
    out = values[0]
    for v in values[1:]:
        out = out + v
    return out


def dot(a, b):
    return jnp.dot(a, b, preferred_element_type=F32)


def dot_first(a, b):
    return lax.dot_general(a, b, (((0,), (0,)), ((), ())), preferred_element_type=F32)


def dot_last(a, b):
    return lax.dot_general(a, b, (((1,), (1,)), ((), ())), preferred_element_type=F32)


def stack(values):
    return jnp.concatenate([v.astype(BF16) for v in values], axis=0)


def pieces_of(value, rows):
    return [value[n * rows : (n + 1) * rows] for n in range(value.shape[0] // rows)]


def rounded_parts(m):
    coords = primal(m)
    return [v.astype(BF16) for v in coords + [-coords[7] - coords[8]]]


def parts_in(atoms_ref, at):
    values = [atoms_ref[c, at : at + 64, :].astype(F32) for c in range(9)]
    scale = 1.0 / (1.0 + total([v * v for v in values]))
    return rounded_parts(square([v * scale for v in values]))


def mix_parts(parts, weights):
    rows = parts[0].shape[0]
    t, a01, a02, a12, s01, s02, s12, s00, s11, s22 = (
        pieces_of(dot(parts[0], weights[0]), rows)
        + pieces_of(dot(stack(parts[1:4]), weights[1]), rows)
        + pieces_of(dot(stack(parts[4:10]), weights[2]), rows)
    )
    return [
        [t + s00, s01 + a01, s02 + a02],
        [s01 - a01, t + s11, s12 + a12],
        [s02 - a02, s12 - a12, t + s22],
    ]


def seen_by_kind(grad):
    diagonal = [grad[0][0], grad[1][1], grad[2][2]]
    skew = [grad[0][1], grad[1][0], grad[0][2], grad[2][0], grad[1][2], grad[2][1]]
    return [stack(v) for v in (diagonal, skew, skew + diagonal)]


def back_parts(grad, weights):
    rows = grad[0][0].shape[0]
    seen = seen_by_kind(grad)
    iso, anti, sym = (pieces_of(dot_last(v, w), rows) for v, w in zip(seen, weights))
    coords = [
        iso[0] + iso[1] + iso[2],
        anti[0] - anti[1], anti[2] - anti[3], anti[4] - anti[5],
        sym[0] + sym[1], sym[2] + sym[3], sym[4] + sym[5],
        sym[6] - sym[8], sym[7] - sym[8],
    ]
    return seen, coords


def weight_grads(parts, seen):
    p = parts
    lefts = (
        [p[0]] * 3,
        [p[1], -p[1], p[2], -p[2], p[3], -p[3]],
        [p[4], p[4], p[5], p[5], p[6], p[6], p[7], p[8], p[9]],
    )
    return [dot_first(stack(left), right) for left, right in zip(lefts, seen)]


def half_silu(u):
    t = jnp.tanh(u)
    p = 1.0 + t
    act = u * p
    return act, p + act * (1.0 - t)


SLOPE3, ACT2, SLOPE2 = slice(0, 384), slice(384, 640), slice(640, 896)
ACT1, SLOPE1 = slice(896, 1024), slice(1024, 1152)
KEPT = 1152
HALF = 64
AHEAD = 6

ORDER = ((0, 1), (1, 0), (0, 2), (2, 0), (1, 2), (2, 1), (0, 0), (1, 1), (2, 2))


class Network:
    def __init__(self, rows, out, factors, basis, at, refs):
        self.rows, self.out, self.factors, self.basis, self.refs = rows, out, factors, basis, refs
        edges = rows.shape[1]
        self.here = pl.ds(pl.multiple_of(at * edges, edges), edges)
        self.half = pl.ds(pl.multiple_of(at * (edges // 2), edges // 2), edges // 2)

    def run(self):
        self.layer1()
        self.active1()
        self.layer2()
        self.active2()
        self.layer3()
        for kind in range(3):
            self.active3(kind)

    def layer1(self):
        cols = jnp.transpose(self.rows)
        self.gate = cols[:, 1:2]
        deep = cols.shape[0] // 2
        lane = lax.broadcasted_iota(jnp.int32, (deep, LANES), 1)
        dist = jnp.where(lane < HALF, cols[:deep, 0:1], cols[deep:, 0:1])
        lane = lane % HALF
        off = dist - lane.astype(F32) * (CUTOFF / 31.0)
        basis = jnp.exp(off * off * (-0.5 * (31.0 / CUTOFF) ** 2))
        last = jnp.where(lane == BASES, 1.0, 0.0)
        basis = jnp.where(lane < BASES, basis, last).astype(BF16)
        self.basis[self.half, :] = basis
        inner = dot(basis, self.refs[0][...])
        self.inner = jnp.concatenate([inner[:, :LANES], inner[:, LANES:]], axis=0)

    def active1(self):
        act, slope = half_silu(self.inner)
        self.act = act.astype(BF16)
        self.out[self.here, ACT1] = self.act
        self.out[self.here, SLOPE1] = slope.astype(BF16)

    def layer2(self):
        one = lax.broadcasted_iota(jnp.int32, self.act.shape, 1) == 0
        one = jnp.where(one, 1.0, 0.0).astype(BF16)
        self.inner = dot(jnp.concatenate([self.act, one], axis=1), self.refs[1][...])

    def active2(self):
        act, slope = half_silu(self.inner)
        self.act = act.astype(BF16)
        self.out[self.here, ACT2] = self.act
        self.out[self.here, SLOPE2] = slope.astype(BF16)

    def layer3(self):
        self.inner = dot(self.act, self.refs[2][...])

    def active3(self, kind):
        act, slope = half_silu(self.inner[:, col(kind)] + self.refs[3][:, col(kind)])
        self.factors[self.here, col(kind)] = act * self.gate
        self.out[self.here, col(kind)] = (slope * (0.5 * self.gate)).astype(BF16)


def halve_weights(w1_ref, w2_ref, w3_ref, bias_ref, w1_s, w2_s, w3_s, b3_s):
    half = 0.5 * bias_ref[...].astype(F32)

    def biased(weights, bias, rows):
        below = lax.broadcasted_iota(jnp.int32, (rows - weights.shape[0], bias.shape[1]), 0)
        bias = jnp.where(below == 0, bias, 0.0)
        return jnp.concatenate([0.5 * weights.astype(F32), bias], axis=0).astype(BF16)

    w1_s[...] = jnp.zeros_like(w1_s)
    first = biased(w1_ref[...], half[0:1], HALF)
    w1_s[:HALF, :LANES] = first
    w1_s[HALF:, LANES:] = first
    wide2 = jnp.concatenate([half[1:2], half[2:3]], axis=1)
    w2_s[...] = biased(w2_ref[...], wide2, w2_s.shape[0])
    w3_s[...] = (0.5 * w3_ref[...].astype(F32)).astype(BF16)
    b3_s[...] = jnp.concatenate([half[3:4], half[4:5], half[5:6]], axis=1)


def network_kernel(
    rows_ref, w1_raw, w2_raw, w3_raw, bias_ref, out_ref, fac_ref, basis_ref, w1_s, w2_s, w3_s, b3_s
):
    net_refs = (w1_s, w2_s, w3_s, b3_s)

    @pl.when(pl.program_id(0) == 0)
    def _():
        halve_weights(w1_raw, w2_raw, w3_raw, bias_ref, *net_refs)

    Network(rows_ref[0], out_ref, fac_ref, basis_ref, 0, net_refs).run()


def window_key(link, first, w):
    start = first + w * WINDOW
    base = pl.multiple_of(first // 16 * 16 + w * WINDOW, 16)
    off = first % 16
    rel = link - start.astype(F32)
    key = rel + off.astype(F32)
    key = jnp.where(key >= WINDOW, key - WINDOW, key)
    key = jnp.where(jnp.logical_and(rel >= 0, rel < WINDOW), key, -1.0)
    return key, base, off


def main_kernel(
    win_ref, low_ref, own_ref, high_ref, outgrad_ref, rows_ref,
    w1_raw, w2_raw, w3_raw, bias_ref,
    iso1_ref, anti1_ref, sym1_ref, iso2_ref, anti2_ref, sym2_ref, net_first, fac_first, basis_first,
    upd_ref, rim_low_ref, own_out_ref, rim_high_ref, grads_ref,
    table, net_a, net_b, fac_a, fac_b, basis_a, basis_b, x_s, msg_s, gm_s, spread,
    d3_ref, d2_ref, d1_ref, dw2_ref, w1_ref, w2_ref, w3_ref, b3_ref, sems,
):
    step = pl.program_id(0)
    steps = pl.num_programs(0)
    edges = rows_ref.shape[2]
    halo = low_ref.shape[1]
    atoms = upd_ref.shape[1]
    chunks = atoms // GROUP
    slots = edges // GROUP
    pairs = edges // 16
    wide = 9 * LANES
    radial = (w1_ref, w2_ref, w3_ref, b3_ref)

    def fetches(j):
        here = pl.ds(pl.multiple_of(j * edges, edges), edges)
        half = pl.ds(pl.multiple_of(j * (edges // 2), edges // 2), edges // 2)
        return (
            pltpu.make_async_copy(net_first.at[here], net_a.at[here], sems.at[j, 0]),
            pltpu.make_async_copy(fac_first.at[here], fac_a.at[here], sems.at[j, 1]),
            pltpu.make_async_copy(basis_first.at[half], basis_a.at[half], sems.at[j, 2]),
        )

    @pl.when(step == 0)
    def _():
        for j in range(AHEAD):
            for copy in fetches(j):
                copy.start()
        halve_weights(w1_raw, w2_raw, w3_raw, bias_ref, *radial)
        weights = (iso1_ref[...], anti1_ref[...], sym1_ref[...])
        place = 0
        for ref in (low_ref, own_ref, high_ref):
            for at in range(0, ref.shape[1], 64):
                here = slice(place + at, place + at + 64)
                mixed = mix_parts(parts_in(ref, at), weights)
                for n, (p, q) in enumerate(ORDER):
                    table[here, col(n)] = mixed[p][q].astype(BF16)
            place += ref.shape[1]
        table[place:, :] = jnp.zeros((table.shape[0] - place, wide), BF16)
        d3_ref[...] = jnp.zeros_like(d3_ref)
        d2_ref[...] = jnp.zeros_like(d2_ref)
        d1_ref[...] = jnp.zeros_like(d1_ref)
        dw2_ref[...] = jnp.zeros_like(dw2_ref)
        spread[...] = jnp.zeros_like(spread)

        @pl.loop(AHEAD, chunks)
        def _(j):
            Network(rows_ref[j], net_a, fac_a, basis_a, j, radial).run()

    def gather(fac, j, w, more):
        here = pl.ds(pl.multiple_of(j * edges, edges), edges)
        index = step * chunks + j
        key, base, off = window_key(rows_ref[index][2:3, :], win_ref[index, 0], w)
        key = jnp.transpose(jnp.broadcast_to(key, (8, edges)))[:, 0:1]
        near = lax.broadcasted_iota(jnp.int32, (edges, WINDOW), 1).astype(F32)
        hot = (key == near).astype(BF16)
        kept = lax.broadcasted_iota(jnp.int32, (16, LANES), 0) >= off
        kept = jnp.where(kept, 1.0, 0.0).astype(BF16)[:, 0:1]
        factors = [fac[here, col(k)] for k in range(3)]
        to = pl.ds(pl.multiple_of(j * GROUP, GROUP), GROUP)

        def rows_of(lanes):
            top = table[pl.ds(base, 16), lanes] * kept
            top += table[pl.ds(base + WINDOW, 16), lanes] * (1.0 - kept)
            rest = table[pl.ds(base + 16, WINDOW - 16), lanes]
            got = dot(hot, jnp.concatenate([top, rest], axis=0))
            return [got[:, col(n)] for n in range(got.shape[1] // LANES)]

        def use(c, x):
            rounded = x.astype(BF16)
            message = factors[KIND[c]] * x
            message = jnp.sum(message.reshape(slots, GROUP, LANES), axis=0)
            x_s[here, col(c)] = x_s[here, col(c)] + rounded if more else rounded
            msg_s[to, col(c)] = msg_s[to, col(c)] + message if more else message

        for n in range(3):
            one, other = rows_of(slice(2 * n * LANES, 2 * (n + 1) * LANES))
            use(1 + n, one - other)
            use(4 + n, one + other)
        x00, x11 = rows_of(slice(6 * LANES, 8 * LANES))
        (x22,) = rows_of(slice(8 * LANES, 9 * LANES))
        trace = x00 + x11 + x22
        third = trace * (1.0 / 3.0)
        use(0, trace)
        use(7, x00 - third)
        use(8, x11 - third)

    even = step % 2 == 0

    def collect(fac):
        @pl.loop(0, chunks // UNROLL)
        def _(pair):
            if fac is fac_a:

                @pl.when(jnp.logical_and(step == 0, pair < AHEAD // UNROLL))
                def _():
                    for n in range(UNROLL):
                        for copy in fetches(pair * UNROLL + n):
                            copy.wait()

            for n in range(UNROLL):
                gather(fac, pair * UNROLL + n, 0, False)

        @pl.loop(0, chunks)
        def _(j):
            @pl.loop(1, win_ref[step * chunks + j, 1])
            def _(w):
                gather(fac, j, w, True)

    @pl.when(even)
    def _():
        collect(fac_a)

    @pl.when(jnp.logical_not(even))
    def _():
        collect(fac_b)

    weights2 = (iso2_ref[...], anti2_ref[...], sym2_ref[...])
    put = pl.ds(pl.multiple_of(halo + step * atoms, 16), atoms)
    mixed = [[None] * 3 for _ in range(3)]
    for n, (p, q) in enumerate(ORDER):
        mixed[p][q] = table[put, col(n)].astype(F32)
    sums = [msg_s[:, col(c)] for c in range(9)]
    messages = to_matrix([sums[0] * (1.0 / 3.0)] + [0.5 * v for v in sums[1:7]] + sums[7:])
    paired = both_ways(mixed, messages)
    inverse = 1.0 / (1.0 + total([v * v for v in flat(paired)]))
    pair_coords = primal(paired)
    mid = [(v * inverse).astype(BF16) for v in pair_coords]
    mid.append(((-pair_coords[7] - pair_coords[8]) * inverse).astype(BF16))
    update = mix_parts(mid, weights2)
    at = pl.ds(pl.multiple_of(step * atoms, 16), atoms)
    values = [own_ref[c, at, :].astype(F32) for c in range(9)]
    inverse_in = 1.0 / (1.0 + total([v * v for v in values]))
    squared = flat(product(update, update))
    for c, (v, u, s) in enumerate(zip(values, flat(update), squared)):
        upd_ref[c] = (v * inverse_in + u + s).astype(BF16)
    out_grad = square([outgrad_ref[c].astype(F32) for c in range(9)])
    grad_update = add(out_grad, both_ways(out_grad, flip(update)))
    seen, mid_dual = back_parts(grad_update, weights2)
    for kind, grad in enumerate(weight_grads(mid, seen)):
        dw2_ref[kind * LANES : (kind + 1) * LANES, :] += grad
    projected = total([a * b for a, b in zip(mid_dual, pair_coords)]) * (2.0 * inverse * inverse)
    grad_paired = to_matrix([v * inverse for v in primal_of_dual(mid_dual)])
    grad_paired = [
        [grad_paired[p][q] - paired[p][q] * projected for q in range(3)] for p in range(3)
    ]
    from_pair = primal(both_ways(grad_paired, flip(messages)))
    for c in range(9):
        spread[put, col(c)] += from_pair[c]
    grad_messages = [
        [v.astype(BF16).astype(F32) for v in row] for row in both_ways(flip(mixed), grad_paired)
    ]
    for c, v in enumerate(primal(grad_messages) + dual(grad_messages)[7:]):
        twice = v.reshape(chunks, 1, GROUP, LANES)
        twice = jnp.concatenate([twice, twice], axis=1).reshape(2 * atoms, LANES)
        gm_s[:, col(c)] = twice.astype(BF16)

    def chunk_places(j):
        here = pl.ds(pl.multiple_of(j * edges, edges), edges)
        two = pl.ds(pl.multiple_of(j * 2 * GROUP, 2 * GROUP), 2 * GROUP)
        return here, two

    def scatter_hot(j, w):
        index = step * chunks + j
        key, base, off = window_key(rows_ref[index][2:3, :], win_ref[index, 0], w)
        near = lax.broadcasted_iota(jnp.int32, (WINDOW, edges), 0).astype(F32)
        kept = lax.broadcasted_iota(jnp.int32, (16, LANES), 0) >= off
        return (key == near).astype(BF16), base, kept

    def scatter(fac, j, hot_base_kept, cs):
        here, two = chunk_places(j)
        hot, base, kept = hot_base_kept
        terms = [
            (fac[here, col(KIND[c])].astype(BF16).reshape(pairs, 16, LANES) * gm_s[two, col(c)]).reshape(
                edges, LANES
            )
            for c in cs
        ]
        sums = dot(hot, jnp.concatenate(terms, axis=1))
        for n, c in enumerate(cs):
            top = sums[:16, col(n)]
            spread[pl.ds(base, 16), col(c)] += jnp.where(kept, top, 0.0)
            spread[pl.ds(base + WINDOW, 16), col(c)] += jnp.where(kept, 0.0, top)
            spread[pl.ds(base + 16, WINDOW - 16), col(c)] += sums[16:, col(n)]

    class Backward:
        def __init__(self, j, now, after):
            self.j, self.now = j, now
            self.net, self.fac, self.basis = now
            self.here, self.two = chunk_places(j)
            self.half = pl.ds(pl.multiple_of(j * (edges // 2), edges // 2), edges // 2)
            self.ahead = None
            if after is not None:
                self.ahead = Network(rows_ref[(step + 1) * chunks + j], *after, j, radial)

        def hot(self):
            self.key = scatter_hot(self.j, 0)

        def spread(self, n):
            scatter(self.fac, self.j, self.key, PAIRS[n])

        def terms(self):
            here, two = self.here, self.two
            terms = [
                x_s[here, col(c)].reshape(pairs, 16, LANES) * gm_s[two, col(c if c < 7 else c + 2)]
                for c in range(9)
            ]
            grads = [terms[0], total(terms[1:4]), total(terms[4:9])]
            grad3 = jnp.concatenate([v.reshape(edges, LANES) for v in grads], axis=1)
            self.grad3 = grad3 * self.net[here, SLOPE3]

        def back3(self):
            self.inner2 = dot_last(self.grad3, w3_ref[...])

        def grads2(self):
            slope = self.net[self.here, SLOPE2].astype(F32)
            self.grad2 = (self.inner2 * slope).astype(BF16)

        def back2(self):
            self.inner1 = dot_last(self.grad2, w2_ref[:LANES, :])

        def grads1(self):
            slope = self.net[self.here, SLOPE1].astype(F32)
            grad1 = (self.inner1 * slope).astype(BF16)
            self.grad1 = jnp.concatenate([grad1[: edges // 2], grad1[edges // 2 :]], axis=1)

        def weights3(self):
            ones = jnp.ones((16, edges), BF16)
            act2 = jnp.concatenate([jnp.transpose(self.net[self.here, ACT2]), ones], axis=0)
            d3_ref[...] += dot(act2, self.grad3)

        def weights2(self):
            ones = jnp.ones((16, edges), BF16)
            act1 = jnp.concatenate([jnp.transpose(self.net[self.here, ACT1]), ones], axis=0)
            d2_ref[...] += dot(act1, self.grad2)

        def weights1(self):
            d1_ref[...] += dot(jnp.transpose(self.basis[self.half, :]), self.grad1)

    def sweep(now, after):
        steps_of = {
            "H": lambda b: b.hot(), "T": lambda b: b.terms(),
            "0": lambda b: b.spread(0), "1": lambda b: b.spread(1), "2": lambda b: b.spread(2),
            "3": lambda b: b.spread(3), "4": lambda b: b.spread(4),
            "D": lambda b: b.back3(), "G": lambda b: b.grads2(),
            "E": lambda b: b.back2(), "F": lambda b: b.grads1(),
            "W": lambda b: b.weights3(), "V": lambda b: b.weights2(), "U": lambda b: b.weights1(),
            "a": lambda b: b.ahead.layer1(), "b": lambda b: b.ahead.active1(),
            "c": lambda b: b.ahead.layer2(), "d": lambda b: b.ahead.active2(),
            "e": lambda b: b.ahead.layer3(), "x": lambda b: b.ahead.active3(0),
            "y": lambda b: b.ahead.active3(1), "z": lambda b: b.ahead.active3(2),
        }

        @pl.loop(0, chunks // UNROLL)
        def _(pair):
            both = [Backward(pair * UNROLL + n, now, after) for n in range(UNROLL)]
            for which, name in zip(SCHEDULE[::2], SCHEDULE[1::2]):
                if after is not None or not name.islower():
                    steps_of[name](both[int(which)])

        @pl.loop(0, chunks)
        def _(j):
            @pl.loop(1, win_ref[step * chunks + j, 1])
            def _(w):
                more = scatter_hot(j, w)
                for cs in PAIRS:
                    scatter(now[1], j, more, cs)

    last = step == steps - 1

    @pl.when(jnp.logical_and(even, jnp.logical_not(last)))
    def _():
        sweep((net_a, fac_a, basis_a), (net_b, fac_b, basis_b))

    @pl.when(jnp.logical_not(jnp.logical_or(even, last)))
    def _():
        sweep((net_b, fac_b, basis_b), (net_a, fac_a, basis_a))

    @pl.when(last)
    def _():
        sweep((net_b, fac_b, basis_b), None)
        grads = [None] * 3
        place = 0
        for ref, out in ((low_ref, rim_low_ref), (own_ref, own_out_ref), (high_ref, rim_high_ref)):
            for at in range(0, out.shape[0], 64):
                here = slice(place + at, place + at + 64)
                coords = [spread[here, col(c)] for c in range(9)]
                for c in range(9):
                    out[at : at + 64, col(c)] = coords[c].astype(out.dtype)
                seen = seen_by_kind(to_matrix(coords))
                fresh = weight_grads(parts_in(ref, at), seen)
                grads = [n if o is None else o + n for o, n in zip(grads, fresh)]
            place += out.shape[0]
        first = d1_ref[:HALF, :LANES] + d1_ref[HALF:, LANES:]
        place = 0
        for value in (*grads, dw2_ref[...], first[:BASES]):
            grads_ref[place : place + value.shape[0], :] = value.astype(BF16)
            place += value.shape[0]
        biases = [first[BASES : BASES + 1]]
        for ref in (d2_ref, d3_ref):
            deep = ref.shape[0] - 16
            for n in range(ref.shape[1] // LANES):
                grads_ref[place : place + deep, :] = ref[:deep, col(n)].astype(BF16)
                biases.append(ref[deep : deep + 1, col(n)])
                place += deep
        biases.append(jnp.zeros((grads_ref.shape[0] - place - len(biases), LANES), F32))
        grads_ref[place:, :] = jnp.concatenate(biases, axis=0).astype(BF16)


def unpack_kernel(grads_ref, *out_refs):
    small, g_w1, g_w2, g_w3 = out_refs[:6], out_refs[6], out_refs[8], out_refs[10]
    place = 0
    for ref in (*small, g_w1):
        ref[...] = grads_ref[place : place + ref.shape[0], :].astype(F32)
        place += ref.shape[0]
    for ref in (g_w2, g_w3):
        for n in range(ref.shape[1] // LANES):
            ref[:, col(n)] = grads_ref[place : place + ref.shape[0], :].astype(F32)
            place += ref.shape[0]
    biases = grads_ref[place : place + 16, :].astype(F32)
    row = 0
    for ref in (out_refs[7], out_refs[9], out_refs[11]):
        for n in range(ref.shape[1] // LANES):
            ref[:, col(n)] = biases[row : row + 1, :]
            row += 1


def final_kernel(
    own_ref, above_ref, below_ref, atoms_ref, outgrad_ref, iso1_ref, anti1_ref, sym1_ref, out_ref
):
    weights = (iso1_ref[...], anti1_ref[...], sym1_ref[...])
    grad_mixed = [
        own_ref[:, col(c)] + above_ref[:, col(c)].astype(F32) + below_ref[:, col(c)].astype(F32)
        for c in range(9)
    ]
    back = flat(to_matrix(primal_of_dual(back_parts(to_matrix(grad_mixed), weights)[1])))
    values = [atoms_ref[c].astype(F32) for c in range(9)]
    inverse = 1.0 / (1.0 + total([v * v for v in values]))
    grad = [outgrad_ref[c].astype(F32) + back[c] for c in range(9)]
    along = total([g * v for g, v in zip(grad, values)]) * (2.0 * inverse)
    for c in range(9):
        out_ref[c] = (grad[c] - values[c] * along) * inverse


def whole(shape):
    return pl.BlockSpec(shape, lambda *_: (0,) * len(shape), pipeline_mode=pl.Buffered(1))


def block(shape):
    return pl.BlockSpec(shape, lambda i, *_: (i,) + (0,) * (len(shape) - 1))


def shape_of(shape, kind):
    return jax.ShapeDtypeStruct(shape, kind)


def part(value, index):
    return lax.dynamic_index_in_dim(value, index, 0, keepdims=False)


def reduce_everywhere(value, axes, beside):
    beside = list(beside)

    def between(v):
        return lax.optimization_barrier((v, beside.pop(0)()))[0] if beside else v

    peers = math.prod(lax.axis_size(a) for a in axes)
    me = lax.axis_index(axes)
    runs, at = [], 1
    while at < peers:
        size = min(2 if at == 1 else 4, peers // at)
        runs.append((at, size))
        at *= size

    def swapped(v, by):
        return lax.ppermute(v, axes, [(i, i ^ by) for i in range(peers)])

    for at, size in runs[:-1]:
        shares = value.reshape(size, value.shape[0] // size, value.shape[1])
        mine = me // at % size
        kept = part(shares, mine).astype(F32)
        for k in range(1, size):
            kept = kept + swapped(part(shares, mine ^ k), k * at).astype(F32)
        value = between(kept.astype(BF16))
    at, size = runs[-1]
    kept = value.astype(F32)
    for k in range(1, size):
        kept = kept + swapped(value, k * at).astype(F32)
    value = between(kept.astype(BF16))
    for at, size in runs[-2::-1]:
        mine = me // at % size
        full = jnp.zeros((size,) + value.shape, value.dtype)
        full = lax.dynamic_update_index_in_dim(full, value, mine, 0)
        for k in range(1, size):
            full = lax.dynamic_update_index_in_dim(full, swapped(value, k * at), mine ^ k, 0)
        value = full.reshape(size * value.shape[0], value.shape[1])
    return value


def local(
    atoms, neighbours, live_mask, distances,
    w_iso1, w_anti1, w_sym1, w_rad1, b_rad1, w_rad2, b_rad2, w_rad3, b_rad3,
    w_iso2, w_anti2, w_sym2, out_grad,
):
    rows, _, channels = atoms.shape
    slots = neighbours.shape[1]
    halo = MOL_MOST
    wide = 9 * channels
    ext = rows + 2 * halo
    edges = GROUP * slots
    chunk_count = rows // GROUP
    steps = 4
    chunks = chunk_count // steps
    block_atoms = rows // steps
    block_edges = block_atoms * slots
    vmem = 62 * 1024 * 1024
    me = lax.axis_index(AXES)
    peers = math.prod(lax.axis_size(a) for a in AXES)
    up = [(i, i + 1) for i in range(peers - 1)]
    down = [(i + 1, i) for i in range(peers - 1)]

    by_component = jnp.swapaxes(atoms, 0, 1)
    out_grad_by_component = jnp.swapaxes(out_grad, 0, 1)
    low = lax.ppermute(by_component, AXES, up)
    high = lax.ppermute(by_component, AXES, down)

    links = neighbours - (me * rows - halo)
    gating = 0.5 * (jnp.cos(math.pi * distances / CUTOFF) + 1.0) * live_mask.astype(F32)

    def as_rows(v):
        return jnp.swapaxes(v.reshape(chunk_count, GROUP, slots), 1, 2).reshape(
            chunk_count, 1, edges
        )

    edge_rows = jnp.concatenate(
        [as_rows(distances), as_rows(gating), as_rows(links.astype(F32))]
        + [jnp.zeros((chunk_count, 5, edges), F32)],
        axis=1,
    )
    grouped = links.reshape(chunk_count, edges)
    first = jnp.min(grouped, axis=1)
    count = (jnp.max(grouped, axis=1) - first) // WINDOW + 1
    windows = jnp.stack([first, count], axis=1)

    biases = jnp.concatenate([b_rad1, b_rad2, b_rad3]).reshape(-1, LANES)
    mid_width, last_width = w_rad2.shape[1], w_rad3.shape[1]
    small = whole((channels, channels))
    components = pl.BlockSpec((9, block_atoms, channels), lambda i: (0, i, 0))
    smem = pl.BlockSpec(memory_space=pltpu.SMEM)
    net_args = (w_rad1, w_rad2, w_rad3, biases)
    net_specs = [whole(v.shape) for v in net_args]
    net_scratch = [
        pltpu.VMEM((LANES, 2 * channels), BF16),
        pltpu.VMEM((2 * channels, mid_width), BF16),
        pltpu.VMEM((mid_width, last_width), BF16), pltpu.VMEM((1, last_width), F32),
    ]
    net0 = pl.pallas_call(
        network_kernel,
        grid=(AHEAD,),
        in_specs=[block((1, 8, edges))] + net_specs,
        out_specs=[
            block((edges, KEPT)), block((edges, last_width)), block((edges // 2, LANES))
        ],
        out_shape=[
            shape_of((AHEAD * edges, KEPT), BF16), shape_of((AHEAD * edges, last_width), F32),
            shape_of((AHEAD * edges // 2, LANES), BF16),
        ],
        scratch_shapes=net_scratch,
        compiler_params=pltpu.CompilerParams(vmem_limit_bytes=vmem),
        cost_estimate=pl.CostEstimate(
            flops=2 * block_edges * 135168, bytes_accessed=block_edges * KEPT * 2, transcendentals=0
        ),
        name="network",
    )(edge_rows, *net_args)

    grad_rows = 6 * channels + BASES + mid_width // LANES * channels
    grad_rows += last_width // LANES * mid_width + 16
    grad_rows = -(-grad_rows // 128) * 128
    updated, rim_low, own_grad, rim_high, grads = pl.pallas_call(
        main_kernel,
        grid=(steps,),
        in_specs=[
            smem, whole(low.shape), whole(by_component.shape), whole(high.shape),
            components, whole((chunk_count, 8, edges)), *net_specs,
            small, small, small, small, small, small,
            *[pl.BlockSpec(memory_space=pl.ANY)] * 3,
        ],
        out_specs=[
            components, whole((halo, wide)), whole((rows, wide)), whole((halo, wide)),
            whole((grad_rows, channels)),
        ],
        out_shape=[
            shape_of((9, rows, channels), BF16),
            shape_of((halo, wide), BF16), shape_of((rows, wide), F32),
            shape_of((halo, wide), BF16), shape_of((grad_rows, channels), BF16),
        ],
        scratch_shapes=[
            pltpu.VMEM((ext + WINDOW, wide), BF16),
            pltpu.VMEM((block_edges, KEPT), BF16),
            pltpu.VMEM((block_edges, KEPT), BF16),
            pltpu.VMEM((block_edges, last_width), F32),
            pltpu.VMEM((block_edges, last_width), F32),
            pltpu.VMEM((block_edges // 2, LANES), BF16),
            pltpu.VMEM((block_edges // 2, LANES), BF16),
            pltpu.VMEM((block_edges, wide), BF16),
            pltpu.VMEM((block_atoms, wide), F32),
            pltpu.VMEM((2 * block_atoms, wide + 2 * channels), BF16),
            pltpu.VMEM((ext + WINDOW, wide), F32),
            pltpu.VMEM((mid_width + 16, last_width), F32),
            pltpu.VMEM((channels + 16, mid_width), F32),
            pltpu.VMEM((LANES, 2 * channels), F32),
            pltpu.VMEM((3 * channels, channels), F32),
            *net_scratch,
            pltpu.SemaphoreType.DMA((AHEAD, 3)),
        ],
        compiler_params=pltpu.CompilerParams(vmem_limit_bytes=vmem),
        name="main",
    )(
        windows, low, by_component, high, out_grad_by_component, edge_rows, *net_args,
        w_iso1, w_anti1, w_sym1, w_iso2, w_anti2, w_sym2, *net0,
    )

    kept = {}

    def send_rims():
        kept["above"] = lax.ppermute(rim_low, AXES, down)
        kept["below"] = lax.ppermute(rim_high, AXES, up)
        return kept["above"], kept["below"]

    def finish():
        grad_atoms = pl.pallas_call(
            final_kernel,
            out_shape=shape_of((9, rows, channels), F32),
            compiler_params=pltpu.CompilerParams(vmem_limit_bytes=vmem),
            name="final",
        )(
            own_grad, kept["above"], kept["below"], by_component, out_grad_by_component,
            w_iso1, w_anti1, w_sym1,
        )
        kept["outs"] = jnp.swapaxes(updated, 0, 1), jnp.swapaxes(grad_atoms, 0, 1)
        return kept["outs"]

    summed = reduce_everywhere(grads, AXES, (lambda: (), send_rims, finish))
    square_shape = (channels, channels)
    shapes = [square_shape] * 6 + [w_rad1.shape, (1, channels), w_rad2.shape, (1, mid_width)]
    shapes += [w_rad3.shape, (1, last_width)]
    out = pl.pallas_call(
        unpack_kernel,
        out_shape=[shape_of(shape, F32) for shape in shapes],
        compiler_params=pltpu.CompilerParams(vmem_limit_bytes=16 * 1024 * 1024),
        name="unpack",
    )(summed)
    return (
        *kept["outs"],
        *out[:3],
        *(v if n % 2 == 0 else v[0] for n, v in enumerate(out[6:])),
        *out[3:6],
    )


def solution(mesh):
    split3 = P(AXES, None, None)
    split2 = P(AXES, None)
    return jax.shard_map(
        local,
        mesh=mesh,
        in_specs=(split3, split2, split2, split2) + (P(),) * 12 + (split3,),
        out_specs=(split3, split3) + (P(),) * 12,
        check_vma=False,
    )
```

time: 245 us -> 146 us (0.60)
  the two profiles are of different devices: /device:TPU:13 before, /device:TPU:0 now
where the time goes in v2:
time: 146 us; the launch traced here: 147 us
  Pallas kernels  92.3 us (63%)
  starting transfers between devices  31 us (21%)
  waiting for transfers between devices  11.1 us (8%)
  local copies, waits for them, and re-layouts  5.93 us (4%)
  other arithmetic  5.48 us (4%)
    pallas_call x1, Pallas kernels, local(): pl.pallas_call(main_kernel, grid=(steps,), in_specs=[smem, whole(low.shap...  78.7 us
    ppermute x11, starting transfers between devices, swapped(): return lax.ppermute(v, axes, [(i, i ^ by) for i in range(peers)])  22.9 us
    ppermute x11, waiting for transfers between devices, swapped(): return lax.ppermute(v, axes, [(i, i ^ by) for i in range(peers)])  11.1 us
    pallas_call x1, Pallas kernels, local(): pl.pallas_call(network_kernel, grid=(AHEAD,), in_specs=[block((1, 8, edge...  8.7 us
    pallas_call x1, Pallas kernels, finish(): pl.pallas_call(final_kernel, out_shape=shape_of((9, rows, channels), F32)...  3.93 us
    ppermute x1, starting transfers between devices, send_rims(): kept['below'] = lax.ppermute(rim_high, AXES, up)  3.07 us
  transfers between devices with their start and end apart: 15, of which 7 were waited for; matrix products, arithmetic and copies ran while one was open for 6% of the time, Pallas kernels for 9%

profile of v2, /device:TPU:0, one launch (start us, length us, event | category | flops | bytes accessed | tf_op | source)
XLA Modules:
  0.0 146.7 jit_solution(11995757959132727243)
XLA Ops:
  0.6 2.4 %collective-permute-start = (bf16[9,256,128]{2,1,0:T(8,128)(2,1)}, bf16[9,256,128]{2,1,0:T(8,128)(2,1)S(1)}, u32[]{:S(2)}, u32[]{:S(2)}) collective-permute-start(bf16[9,256,128]{2,1,0:T(8,128)(2,1)} %bitcast.61), channel_id=1, source_target_pairs={{0,1},{1,2},{2,3},{3,4},{4,5},{5,6},{6,7},{7,8},{8,9},{9,10},{10,1... | collective-permute-start | bytes 1769480 | tf_op jit(solution)/shard_map/ppermute | solution.py:727
  3.0 1.3 collective-permute-start.1
  4.4 0.9 copy.61
  5.9 0.7 copy.70.win_ref
  6.9 0.9 copy.62
  7.8 1.1 convert_multiply_fusion
  9.7 1.3 maximum_bitcast_fusion.bias_ref
  11.0 1.0 maximum_maximum_fusion.rows_ref
  12.0 8.7 %network.1 = (bf16[3072,1152]{1,0:T(8,128)(2,1)}, f32[3072,384]{1,0:T(8,128)}, bf16[1536,128]{1,0:T(8,128)(2,1)}) custom-call(f32[32,8,512]{2,1,0:T(8,128)} %maximum_maximum_fusion.rows_ref, bf16[32,128]{1,0:T(8,128)(2,1)} %w1_raw.3, bf16[128,256]{1,0:T(8,128)(2,1)} %w2_raw.3, bf16[256,384]{1,0:T(8,128)(2,1)} %w3_raw.3, ...), custom_call_target="tpu_custom_call" | custom-call | flops 1107296256 | bytes 9437184 | tf_op jit(solution)/shard_map/network/pallas_call | solution.py:760
  20.7 0.8 copy-done
  21.7 78.7 %main.1 = (bf16[9,256,128]{2,1,0:T(8,128)(2,1)}, bf16[256,1152]{1,0:T(8,128)(2,1)}, f32[256,1152]{1,0:T(8,128)}, bf16[256,1152]{1,0:T(8,128)(2,1)}, bf16[1920,128]{1,0:T(8,128)(2,1)}) custom-call(s32[32,2]{1,0:T(8,128)} %copy.70.win_ref, bf16[9,256,128]{2,1,0:T(8,128)(2,1)} %copy-done, bf16[9,256,128]{2,1,0:T(8,128)(2,1)} %bitcast.63, ...), custom_call_target="tpu_custom_call" | custom-call | tf_op jit(solution)/shard_map/main/pallas_call | solution.py:782
  100.4 1.0 dynamic-slice_bitcast_fusion
  101.4 1.4 collective-permute-start.4
  102.8 1.3 collective-permute-start.2
  104.1 3.1 %collective-permute-start.3 = (bf16[256,1152]{1,0:T(8,128)(2,1)}, bf16[256,1152]{1,0:T(8,128)(2,1)S(1)}, u32[]{:S(2)}, u32[]{:S(2)}) collective-permute-start(bf16[256,1152]{1,0:T(8,128)(2,1)} %get-tuple-element.42), channel_id=1, source_target_pairs={{0,1},{1,2},{2,3},{3,4},{4,5},{5,6},{6,7},{7,8},{8,9},{9,10},{10,1... | collective-permute-start | bytes 1769480 | tf_op jit(solution)/shard_map/ppermute | solution.py:830
  107.1 1.0 fusion
  108.2 6.0 %collective-permute-start.7 = (bf16[240,128]{1,0:T(8,128)(2,1)S(1)}, bf16[240,128]{1,0:T(8,128)(2,1)S(1)}, u32[]{:S(2)}, u32[]{:S(2)}) collective-permute-start(bf16[240,128]{1,0:T(8,128)(2,1)S(1)} %get-tuple-element.61), channel_id=1, source_target_pairs={{0,6},{1,7},{2,4},{3,5},{4,2},{5,3},{6,0},{7,1},{8,14},{9,15},{10,... | collective-permute-start | bytes 184328 | tf_op jit(solution)/shard_map/ppermute | solution.py:679
  114.2 0.6 collective-permute-start.5
  114.8 5.9 %collective-permute-done.7 = bf16[240,128]{1,0:T(8,128)(2,1)S(1)} collective-permute-done((bf16[240,128]{1,0:T(8,128)(2,1)S(1)}, bf16[240,128]{1,0:T(8,128)(2,1)S(1)}, u32[]{:S(2)}, u32[]{:S(2)}) %collective-permute-start.7) | collective-permute-done | bytes 61472 | tf_op jit(solution)/shard_map/ppermute | solution.py:679
  120.7 0.3 collective-permute-done.5
  121.1 10.7 %collective-permute-start.10 = (bf16[240,128]{1,0:T(8,128)(2,1)S(1)}, bf16[240,128]{1,0:T(8,128)(2,1)S(1)}, u32[]{:S(2)}, u32[]{:S(2)}) collective-permute-start(bf16[240,128]{1,0:T(8,128)(2,1)S(1)} %fusion.3), channel_id=1, source_target_pairs={{0,24},{1,25},{2,26},{3,27},{4,28},{5,29},{6,30},{7,31},{8,16},{9,... | collective-permute-start | bytes 184328 | tf_op jit(solution)/shard_map/ppermute | solution.py:679
  131.8 0.6 collective-permute-start.8
  132.4 3.9 %final.1 = f32[9,256,128]{2,1,0:T(8,128)} custom-call(f32[256,1152]{1,0:T(8,128)} %get-tuple-element.40.own_ref, bf16[256,1152]{1,0:T(8,128)(2,1)} %copy-done.2, bf16[256,1152]{1,0:T(8,128)(2,1)} %copy-done.3, bf16[9,256,128]{2,1,0:T(8,128)(2,1)} %bitcast.64, bf16[9,256,128]{2,1,0:T(8,128)(2,1)} %bitcast.66, bf16[128,128]{1,0:T(8,128)(2,1)} %iso1_ref.3, ...), custom_call_target="tpu_custom_call" | custom-call | tf_op jit(solution)/shard_map/final/pallas_call | solution.py:834
  136.3 1.4 collective-permute-done.9
  137.8 0.3 collective-permute-start.11
  138.1 3.3 %collective-permute-start.13 = (bf16[240,128]{1,0:T(8,128)(2,1)S(1)}, bf16[240,128]{1,0:T(8,128)(2,1)S(1)}, u32[]{:S(2)}, u32[]{:S(2)}) collective-permute-start(bf16[240,128]{1,0:T(8,128)(2,1)S(1)} %add_convert_fusion), channel_id=1, source_target_pairs={{0,6},{1,7},{2,4},{3,5},{4,2},{5,3},{6,0},{7,1},{8,14},{9,15},{10,... | collective-permute-start | bytes 184328 | tf_op jit(solution)/shard_map/ppermute | solution.py:679
  141.4 1.1 collective-permute-done.11
  142.5 0.3 collective-permute-done.12
  142.8 0.7 collective-permute-done.13
  143.8 1.4 collective-permute-done.14
  145.2 1.0 unpack.1
  146.1 0.6 reduce.4
  (46 shorter events, 2.3 us)
Async XLA Ops:
  0.6 20.0 %collective-permute-start = (bf16[9,256,128]{2,1,0:T(8,128)(2,1)}, bf16[9,256,128]{2,1,0:T(8,128)(2,1)S(1)}, u32[]{:S(2)}, u32[]{:S(2)}) collective-permute-start(bf16[9,256,128]{2,1,0:T(8,128)(2,1)} %bitcast.61), channel_id=1, source_target_pairs={{0,1},{1,2},{2,3},{3,4},{4,5},{5,6},{6,7},{7,8},{8,9},{9,10},{10,1... | collective-permute-start | bytes 1769480 | tf_op jit(solution)/shard_map/ppermute | solution.py:727
  3.0 17.6 %collective-permute-start.1 = (bf16[9,256,128]{2,1,0:T(8,128)(2,1)}, bf16[9,256,128]{2,1,0:T(8,128)(2,1)S(1)}, u32[]{:S(2)}, u32[]{:S(2)}) collective-permute-start(bf16[9,256,128]{2,1,0:T(8,128)(2,1)} %bitcast.62), channel_id=1, source_target_pairs={{1,0},{2,1},{3,2},{4,3},{5,4},{6,5},{7,6},{8,7},{9,8},{10,9},{11,1... | collective-permute-start | bytes 1769480 | tf_op jit(solution)/shard_map/ppermute | solution.py:728
  20.7 0.8 copy-start
  20.7 1.0 copy-start.1
  101.4 5.7 %collective-permute-start.4 = (bf16[960,128]{1,0:T(8,128)(2,1)S(1)}, bf16[960,128]{1,0:T(8,128)(2,1)S(1)}, u32[]{:S(2)}, u32[]{:S(2)}) collective-permute-start(bf16[960,128]{1,0:T(8,128)(2,1)S(1)} %dynamic-slice_bitcast_fusion), channel_id=1, source_target_pairs={{0,1},{1,0},{2,3},{3,2},{4,5},{5,4},{6,7},{7,6},{8,9},{9,8},{10,11... | collective-permute-start | bytes 737288 | tf_op jit(solution)/shard_map/ppermute | solution.py:679
  102.8 18.3 %collective-permute-start.2 = (bf16[256,1152]{1,0:T(8,128)(2,1)}, bf16[256,1152]{1,0:T(8,128)(2,1)S(1)}, u32[]{:S(2)}, u32[]{:S(2)}) collective-permute-start(bf16[256,1152]{1,0:T(8,128)(2,1)} %get-tuple-element.41), channel_id=1, source_target_pairs={{1,0},{2,1},{3,2},{4,3},{5,4},{6,5},{7,6},{8,7},{9,8},{10,9},{11,1... | collective-permute-start | bytes 1769480 | tf_op jit(solution)/shard_map/ppermute | solution.py:829
  104.1 17.0 %collective-permute-start.3 = (bf16[256,1152]{1,0:T(8,128)(2,1)}, bf16[256,1152]{1,0:T(8,128)(2,1)S(1)}, u32[]{:S(2)}, u32[]{:S(2)}) collective-permute-start(bf16[256,1152]{1,0:T(8,128)(2,1)} %get-tuple-element.42), channel_id=1, source_target_pairs={{0,1},{1,2},{2,3},{3,4},{4,5},{5,6},{6,7},{7,8},{8,9},{9,10},{10,1... | collective-permute-start | bytes 1769480 | tf_op jit(solution)/shard_map/ppermute | solution.py:830
  108.2 12.5 %collective-permute-start.7 = (bf16[240,128]{1,0:T(8,128)(2,1)S(1)}, bf16[240,128]{1,0:T(8,128)(2,1)S(1)}, u32[]{:S(2)}, u32[]{:S(2)}) collective-permute-start(bf16[240,128]{1,0:T(8,128)(2,1)S(1)} %get-tuple-element.61), channel_id=1, source_target_pairs={{0,6},{1,7},{2,4},{3,5},{4,2},{5,3},{6,0},{7,1},{8,14},{9,15},{10,... | collective-permute-start | bytes 184328 | tf_op jit(solution)/shard_map/ppermute | solution.py:679
  114.2 6.5 %collective-permute-start.6 = (bf16[240,128]{1,0:T(8,128)(2,1)S(1)}, bf16[240,128]{1,0:T(8,128)(2,1)S(1)}, u32[]{:S(2)}, u32[]{:S(2)}) collective-permute-start(bf16[240,128]{1,0:T(8,128)(2,1)S(1)} %get-tuple-element.62), channel_id=1, source_target_pairs={{0,4},{1,5},{2,6},{3,7},{4,0},{5,1},{6,2},{7,3},{8,12},{9,13},{10,... | collective-permute-start | bytes 184328 | tf_op jit(solution)/shard_map/ppermute | solution.py:679
  114.2 6.8 %collective-permute-start.5 = (bf16[240,128]{1,0:T(8,128)(2,1)S(1)}, bf16[240,128]{1,0:T(8,128)(2,1)S(1)}, u32[]{:S(2)}, u32[]{:S(2)}) collective-permute-start(bf16[240,128]{1,0:T(8,128)(2,1)S(1)} %get-tuple-element.60), channel_id=1, source_target_pairs={{0,2},{1,3},{2,0},{3,1},{4,6},{5,7},{6,4},{7,5},{8,10},{9,11},{10,... | collective-permute-start | bytes 184328 | tf_op jit(solution)/shard_map/ppermute | solution.py:679
  121.0 11.3 %copy-start.2 = (bf16[256,1152]{1,0:T(8,128)(2,1)}, bf16[256,1152]{1,0:T(8,128)(2,1)S(1)}, u32[]{:S(2)}) copy-start(bf16[256,1152]{1,0:T(8,128)(2,1)S(1)} %collective-permute-done.2.above_ref) | copy-start | bytes 1769476
  121.1 11.3 %copy-start.3 = (bf16[256,1152]{1,0:T(8,128)(2,1)}, bf16[256,1152]{1,0:T(8,128)(2,1)S(1)}, u32[]{:S(2)}) copy-start(bf16[256,1152]{1,0:T(8,128)(2,1)S(1)} %collective-permute-done.3.below_ref) | copy-start | bytes 1769476
  121.1 15.2 %collective-permute-start.10 = (bf16[240,128]{1,0:T(8,128)(2,1)S(1)}, bf16[240,128]{1,0:T(8,128)(2,1)S(1)}, u32[]{:S(2)}, u32[]{:S(2)}) collective-permute-start(bf16[240,128]{1,0:T(8,128)(2,1)S(1)} %fusion.3), channel_id=1, source_target_pairs={{0,24},{1,25},{2,26},{3,27},{4,28},{5,29},{6,30},{7,31},{8,16},{9,... | collective-permute-start | bytes 184328 | tf_op jit(solution)/shard_map/ppermute | solution.py:679
  131.7 6.0 %collective-permute-start.9 = (bf16[240,128]{1,0:T(8,128)(2,1)S(1)}, bf16[240,128]{1,0:T(8,128)(2,1)S(1)}, u32[]{:S(2)}, u32[]{:S(2)}) collective-permute-start(bf16[240,128]{1,0:T(8,128)(2,1)S(1)} %fusion.3), channel_id=1, source_target_pairs={{0,16},{1,17},{2,18},{3,19},{4,20},{5,21},{6,22},{7,23},{8,24},{9,... | collective-permute-start | bytes 184328 | tf_op jit(solution)/shard_map/ppermute | solution.py:679
  131.8 6.0 %collective-permute-start.8 = (bf16[240,128]{1,0:T(8,128)(2,1)S(1)}, bf16[240,128]{1,0:T(8,128)(2,1)S(1)}, u32[]{:S(2)}, u32[]{:S(2)}) collective-permute-start(bf16[240,128]{1,0:T(8,128)(2,1)S(1)} %fusion.3), channel_id=1, source_target_pairs={{0,8},{1,9},{2,10},{3,11},{4,12},{5,13},{6,14},{7,15},{8,0},{9,1},... | collective-permute-start | bytes 184328 | tf_op jit(solution)/shard_map/ppermute | solution.py:679
  137.8 4.7 %collective-permute-start.11 = (bf16[240,128]{1,0:T(8,128)(2,1)S(1)}, bf16[240,128]{1,0:T(8,128)(2,1)S(1)}, u32[]{:S(2)}, u32[]{:S(2)}) collective-permute-start(bf16[240,128]{1,0:T(8,128)(2,1)S(1)} %add_convert_fusion), channel_id=1, source_target_pairs={{0,2},{1,3},{2,0},{3,1},{4,6},{5,7},{6,4},{7,5},{8,10},{9,11},{10,... | collective-permute-start | bytes 184328 | tf_op jit(solution)/shard_map/ppermute | solution.py:679
  138.1 4.7 %collective-permute-start.12 = (bf16[240,128]{1,0:T(8,128)(2,1)S(1)}, bf16[240,128]{1,0:T(8,128)(2,1)S(1)}, u32[]{:S(2)}, u32[]{:S(2)}) collective-permute-start(bf16[240,128]{1,0:T(8,128)(2,1)S(1)} %add_convert_fusion), channel_id=1, source_target_pairs={{0,4},{1,5},{2,6},{3,7},{4,0},{5,1},{6,2},{7,3},{8,12},{9,13},{10,... | collective-permute-start | bytes 184328 | tf_op jit(solution)/shard_map/ppermute | solution.py:679
  138.1 5.5 %collective-permute-start.13 = (bf16[240,128]{1,0:T(8,128)(2,1)S(1)}, bf16[240,128]{1,0:T(8,128)(2,1)S(1)}, u32[]{:S(2)}, u32[]{:S(2)}) collective-permute-start(bf16[240,128]{1,0:T(8,128)(2,1)S(1)} %add_convert_fusion), channel_id=1, source_target_pairs={{0,6},{1,7},{2,4},{3,5},{4,2},{5,3},{6,0},{7,1},{8,14},{9,15},{10,... | collective-permute-start | bytes 184328 | tf_op jit(solution)/shard_map/ppermute | solution.py:679
  143.6 1.6 %collective-permute-start.14 = (bf16[960,128]{1,0:T(8,128)(2,1)S(1)}, bf16[960,128]{1,0:T(8,128)(2,1)S(1)}, u32[]{:S(2)}, u32[]{:S(2)}) collective-permute-start(bf16[960,128]{1,0:T(8,128)(2,1)S(1)} %bitcast.73), channel_id=1, source_target_pairs={{0,1},{1,0},{2,3},{3,2},{4,5},{5,4},{6,7},{7,6},{8,9},{9,8},{10,11... | collective-permute-start | bytes 737288 | tf_op jit(solution)/shard_map/ppermute | solution.py:679

commit v3 on v2

--- a/solution.py
+++ b/solution.py
@@ -15,7 +15,7 @@
 BASES = 32
 UNROLL = 2
 PAIRS = ((0, 1), (2, 3), (4, 5), (6, 7), (8,))
-SCHEDULE = "".join(n + s for n in "01" for s in "HaTDb0G1cWd2E3eF4xVyUz")
+SCHEDULE = "0H0T0D000a01040G0b0J030c0W0d0p0E0e0F0x0V0y020U0z1H1T1D101a111b121G1J131c141d1p1E1e1F1y1x1V1U1z1W"
 WINDOW = 256
 KIND = (0, 1, 1, 1, 2, 2, 2, 2, 2)
 AXES = ("edge", "grp")
@@ -198,10 +198,17 @@
 ORDER = ((0, 1), (1, 0), (0, 2), (2, 0), (1, 2), (2, 1), (0, 0), (1, 1), (2, 2))
 
 
+def over_lanes(block, slots, lanes=LANES):
+    return jnp.concatenate(
+        [jnp.broadcast_to(block[:, s : s + 1], (block.shape[0], lanes)) for s in slots], axis=0
+    )
+
+
 class Network:
-    def __init__(self, rows, out, factors, basis, at, refs):
-        self.rows, self.out, self.factors, self.basis, self.refs = rows, out, factors, basis, refs
-        edges = rows.shape[1]
+    def __init__(self, dist, gate, out, factors, basis, at, refs):
+        self.dist, self.gate8 = dist, gate
+        self.out, self.factors, self.basis, self.refs = out, factors, basis, refs
+        edges = dist.shape[0] * dist.shape[1]
         self.here = pl.ds(pl.multiple_of(at * edges, edges), edges)
         self.half = pl.ds(pl.multiple_of(at * (edges // 2), edges // 2), edges // 2)
 
@@ -209,17 +216,18 @@
         self.layer1()
         self.active1()
         self.layer2()
-        self.active2()
+        self.active2(0)
+        self.active2(1)
         self.layer3()
         for kind in range(3):
             self.active3(kind)
 
     def layer1(self):
-        cols = jnp.transpose(self.rows)
-        self.gate = cols[:, 1:2]
-        deep = cols.shape[0] // 2
-        lane = lax.broadcasted_iota(jnp.int32, (deep, LANES), 1)
-        dist = jnp.where(lane < HALF, cols[:deep, 0:1], cols[deep:, 0:1])
+        slots = self.dist.shape[1]
+        self.gate = over_lanes(self.gate8, range(slots))
+        low = over_lanes(self.dist, range(slots // 2))
+        lane = lax.broadcasted_iota(jnp.int32, low.shape, 1)
+        dist = jnp.where(lane < HALF, low, over_lanes(self.dist, range(slots // 2, slots)))
         lane = lane % HALF
         off = dist - lane.astype(F32) * (CUTOFF / 31.0)
         basis = jnp.exp(off * off * (-0.5 * (31.0 / CUTOFF) ** 2))
@@ -240,11 +248,12 @@
         one = jnp.where(one, 1.0, 0.0).astype(BF16)
         self.inner = dot(jnp.concatenate([self.act, one], axis=1), self.refs[1][...])
 
-    def active2(self):
-        act, slope = half_silu(self.inner)
-        self.act = act.astype(BF16)
-        self.out[self.here, ACT2] = self.act
-        self.out[self.here, SLOPE2] = slope.astype(BF16)
+    def active2(self, n):
+        act, slope = half_silu(self.inner[:, col(n)])
+        act = act.astype(BF16)
+        self.act = jnp.concatenate([self.act, act], axis=1) if n else act
+        self.out[self.here, col(ACT2.start // LANES + n)] = act
+        self.out[self.here, col(SLOPE2.start // LANES + n)] = slope.astype(BF16)
 
     def layer3(self):
         self.inner = dot(self.act, self.refs[2][...])
@@ -273,16 +282,28 @@
     b3_s[...] = jnp.concatenate([half[3:4], half[4:5], half[5:6]], axis=1)
 
 
+def by_atom(ref):
+    return jnp.transpose(ref[...].astype(F32))
+
+
+def gating(dist, live):
+    return 0.5 * (jnp.cos(math.pi * dist / CUTOFF) + 1.0) * live
+
+
 def network_kernel(
-    rows_ref, w1_raw, w2_raw, w3_raw, bias_ref, out_ref, fac_ref, basis_ref, w1_s, w2_s, w3_s, b3_s
+    dist_ref, live_ref, w1_raw, w2_raw, w3_raw, bias_ref, out_ref, fac_ref, basis_ref, dist_s, gate_s, w1_s, w2_s,
+    w3_s, b3_s,
 ):
     net_refs = (w1_s, w2_s, w3_s, b3_s)
 
     @pl.when(pl.program_id(0) == 0)
     def _():
         halve_weights(w1_raw, w2_raw, w3_raw, bias_ref, *net_refs)
-
-    Network(rows_ref[0], out_ref, fac_ref, basis_ref, 0, net_refs).run()
+        dist_s[...] = by_atom(dist_ref)
+        gate_s[...] = gating(dist_s[...], by_atom(live_ref))
+
+    mine = pl.ds(pl.multiple_of(pl.program_id(0) * GROUP, GROUP), GROUP)
+    Network(dist_s[mine, :], gate_s[mine, :], out_ref, fac_ref, basis_ref, 0, net_refs).run()
 
 
 def window_key(link, first, w):
@@ -297,23 +318,31 @@
 
 
 def main_kernel(
-    win_ref, low_ref, own_ref, high_ref, outgrad_ref, rows_ref,
+    win_ref, near_ref, own_ref, far_ref, outgrad_ref, dist_ref, live_ref, link_ref,
     w1_raw, w2_raw, w3_raw, bias_ref,
     iso1_ref, anti1_ref, sym1_ref, iso2_ref, anti2_ref, sym2_ref, net_first, fac_first, basis_first,
-    upd_ref, rim_low_ref, own_out_ref, rim_high_ref, grads_ref,
+    upd_ref, rim_near_ref, own_out_ref, rim_far_ref, grads_ref,
     table, net_a, net_b, fac_a, fac_b, basis_a, basis_b, x_s, msg_s, gm_s, spread,
-    d3_ref, d2_ref, d1_ref, dw2_ref, w1_ref, w2_ref, w3_ref, b3_ref, sems,
+    d3_ref, d2_ref, d1_ref, dw2_ref, w1_ref, w2_ref, w3_ref, b3_ref,
+    dist_s, gate_s, link_s, sems,
 ):
     step = pl.program_id(0)
     steps = pl.num_programs(0)
-    edges = rows_ref.shape[2]
-    halo = low_ref.shape[1]
+    edges = GROUP * link_ref.shape[0]
+    halo = near_ref.shape[1]
+    odd = win_ref[win_ref.shape[0] - 1, 0]
+    far_side = halo + own_ref.shape[1]
+    near_at = pl.multiple_of((1 - odd) * far_side, 64)
+    far_at = pl.multiple_of(odd * far_side, 64)
     atoms = upd_ref.shape[1]
     chunks = atoms // GROUP
     slots = edges // GROUP
     pairs = edges // 16
     wide = 9 * LANES
     radial = (w1_ref, w2_ref, w3_ref, b3_ref)
+
+    def chunk_atoms(index):
+        return pl.ds(pl.multiple_of(index * GROUP, GROUP), GROUP)
 
     def fetches(j):
         here = pl.ds(pl.multiple_of(j * edges, edges), edges)
@@ -330,15 +359,16 @@
             for copy in fetches(j):
                 copy.start()
         halve_weights(w1_raw, w2_raw, w3_raw, bias_ref, *radial)
+        dist_s[...] = by_atom(dist_ref)
+        gate_s[...] = gating(dist_s[...], by_atom(live_ref))
+        link_s[...] = by_atom(link_ref)
         weights = (iso1_ref[...], anti1_ref[...], sym1_ref[...])
-        place = 0
-        for ref in (low_ref, own_ref, high_ref):
+        for ref, place in ((near_ref, near_at), (own_ref, halo), (far_ref, far_at)):
             for at in range(0, ref.shape[1], 64):
-                here = slice(place + at, place + at + 64)
                 mixed = mix_parts(parts_in(ref, at), weights)
                 for n, (p, q) in enumerate(ORDER):
-                    table[here, col(n)] = mixed[p][q].astype(BF16)
-            place += ref.shape[1]
+                    table[pl.ds(place + at, 64), col(n)] = mixed[p][q].astype(BF16)
+        place = far_side + halo
         table[place:, :] = jnp.zeros((table.shape[0] - place, wide), BF16)
         d3_ref[...] = jnp.zeros_like(d3_ref)
         d2_ref[...] = jnp.zeros_like(d2_ref)
@@ -348,15 +378,15 @@
 
         @pl.loop(AHEAD, chunks)
         def _(j):
-            Network(rows_ref[j], net_a, fac_a, basis_a, j, radial).run()
+            mine = chunk_atoms(j)
+            Network(dist_s[mine, :], gate_s[mine, :], net_a, fac_a, basis_a, j, radial).run()
 
     def gather(fac, j, w, more):
         here = pl.ds(pl.multiple_of(j * edges, edges), edges)
         index = step * chunks + j
-        key, base, off = window_key(rows_ref[index][2:3, :], win_ref[index, 0], w)
-        key = jnp.transpose(jnp.broadcast_to(key, (8, edges)))[:, 0:1]
+        key, base, off = window_key(link_s[chunk_atoms(index), :], win_ref[index, 0], w)
         near = lax.broadcasted_iota(jnp.int32, (edges, WINDOW), 1).astype(F32)
-        hot = (key == near).astype(BF16)
+        hot = (over_lanes(key, range(slots), WINDOW) == near).astype(BF16)
         kept = lax.broadcasted_iota(jnp.int32, (16, LANES), 0) >= off
         kept = jnp.where(kept, 1.0, 0.0).astype(BF16)[:, 0:1]
         factors = [fac[here, col(k)] for k in range(3)]
@@ -465,7 +495,13 @@
 
     def scatter_hot(j, w):
         index = step * chunks + j
-        key, base, off = window_key(rows_ref[index][2:3, :], win_ref[index, 0], w)
+        key, base, off = window_key(link_s[chunk_atoms(index), :], win_ref[index, 0], w)
+        lane = lax.broadcasted_iota(jnp.int32, (slots, edges), 1)
+        own_slot = lax.broadcasted_iota(jnp.int32, (slots, edges), 0) == lane // GROUP
+        copies = dot(key.astype(BF16), jnp.where(own_slot, 1.0, 0.0).astype(BF16))
+        lane = lax.broadcasted_iota(jnp.int32, (GROUP, edges), 1)
+        own_atom = lax.broadcasted_iota(jnp.int32, (GROUP, edges), 0) == lane % GROUP
+        key = jnp.sum(jnp.where(own_atom, copies, 0.0), axis=0, keepdims=True)
         near = lax.broadcasted_iota(jnp.int32, (WINDOW, edges), 0).astype(F32)
         kept = lax.broadcasted_iota(jnp.int32, (16, LANES), 0) >= off
         return (key == near).astype(BF16), base, kept
@@ -494,7 +530,8 @@
             self.half = pl.ds(pl.multiple_of(j * (edges // 2), edges // 2), edges // 2)
             self.ahead = None
             if after is not None:
-                self.ahead = Network(rows_ref[(step + 1) * chunks + j], *after, j, radial)
+                mine = chunk_atoms((step + 1) * chunks + j)
+                self.ahead = Network(dist_s[mine, :], gate_s[mine, :], *after, j, radial)
 
         def hot(self):
             self.key = scatter_hot(self.j, 0)
@@ -515,9 +552,10 @@
         def back3(self):
             self.inner2 = dot_last(self.grad3, w3_ref[...])
 
-        def grads2(self):
-            slope = self.net[self.here, SLOPE2].astype(F32)
-            self.grad2 = (self.inner2 * slope).astype(BF16)
+        def grads2(self, n):
+            slope = self.net[self.here, col(SLOPE2.start // LANES + n)].astype(F32)
+            grad2 = (self.inner2[:, col(n)] * slope).astype(BF16)
+            self.grad2 = jnp.concatenate([self.grad2, grad2], axis=1) if n else grad2
 
         def back2(self):
             self.inner1 = dot_last(self.grad2, w2_ref[:LANES, :])
@@ -545,11 +583,11 @@
             "H": lambda b: b.hot(), "T": lambda b: b.terms(),
             "0": lambda b: b.spread(0), "1": lambda b: b.spread(1), "2": lambda b: b.spread(2),
             "3": lambda b: b.spread(3), "4": lambda b: b.spread(4),
-            "D": lambda b: b.back3(), "G": lambda b: b.grads2(),
+            "D": lambda b: b.back3(), "G": lambda b: b.grads2(0), "J": lambda b: b.grads2(1),
             "E": lambda b: b.back2(), "F": lambda b: b.grads1(),
             "W": lambda b: b.weights3(), "V": lambda b: b.weights2(), "U": lambda b: b.weights1(),
             "a": lambda b: b.ahead.layer1(), "b": lambda b: b.ahead.active1(),
-            "c": lambda b: b.ahead.layer2(), "d": lambda b: b.ahead.active2(),
+            "c": lambda b: b.ahead.layer2(), "d": lambda b: b.ahead.active2(0), "p": lambda b: b.ahead.active2(1),
             "e": lambda b: b.ahead.layer3(), "x": lambda b: b.ahead.active3(0),
             "y": lambda b: b.ahead.active3(1), "z": lambda b: b.ahead.active3(2),
         }
@@ -583,17 +621,18 @@
     def _():
         sweep((net_b, fac_b, basis_b), None)
         grads = [None] * 3
-        place = 0
-        for ref, out in ((low_ref, rim_low_ref), (own_ref, own_out_ref), (high_ref, rim_high_ref)):
+        for ref, out, place in (
+            (near_ref, rim_near_ref, near_at),
+            (own_ref, own_out_ref, halo),
+            (far_ref, rim_far_ref, far_at),
+        ):
             for at in range(0, out.shape[0], 64):
-                here = slice(place + at, place + at + 64)
-                coords = [spread[here, col(c)] for c in range(9)]
+                coords = [spread[pl.ds(place + at, 64), col(c)] for c in range(9)]
                 for c in range(9):
                     out[at : at + 64, col(c)] = coords[c].astype(out.dtype)
                 seen = seen_by_kind(to_matrix(coords))
                 fresh = weight_grads(parts_in(ref, at), seen)
                 grads = [n if o is None else o + n for o, n in zip(grads, fresh)]
-            place += out.shape[0]
         first = d1_ref[:HALF, :LANES] + d1_ref[HALF:, LANES:]
         place = 0
         for value in (*grads, dw2_ref[...], first[:BASES]):
@@ -629,11 +668,11 @@
 
 
 def final_kernel(
-    own_ref, above_ref, below_ref, atoms_ref, outgrad_ref, iso1_ref, anti1_ref, sym1_ref, out_ref
+    own_ref, near_ref, far_ref, atoms_ref, outgrad_ref, iso1_ref, anti1_ref, sym1_ref, out_ref
 ):
     weights = (iso1_ref[...], anti1_ref[...], sym1_ref[...])
     grad_mixed = [
-        own_ref[:, col(c)] + above_ref[:, col(c)].astype(F32) + below_ref[:, col(c)].astype(F32)
+        own_ref[:, col(c)] + near_ref[:, col(c)].astype(F32) + far_ref[:, col(c)].astype(F32)
         for c in range(9)
     ]
     back = flat(to_matrix(primal_of_dual(back_parts(to_matrix(grad_mixed), weights)[1])))
@@ -665,7 +704,7 @@
     beside = list(beside)
 
     def between(v):
-        return lax.optimization_barrier((v, beside.pop(0)()))[0] if beside else v
+        return beside.pop(0)(v) if beside else v
 
     peers = math.prod(lax.axis_size(a) for a in axes)
     me = lax.axis_index(axes)
@@ -696,7 +735,7 @@
         full = lax.dynamic_update_index_in_dim(full, value, mine, 0)
         for k in range(1, size):
             full = lax.dynamic_update_index_in_dim(full, swapped(value, k * at), mine ^ k, 0)
-        value = full.reshape(size * value.shape[0], value.shape[1])
+        value = between(full.reshape(size * value.shape[0], value.shape[1]))
     return value
 
 
@@ -719,31 +758,22 @@
     vmem = 62 * 1024 * 1024
     me = lax.axis_index(AXES)
     peers = math.prod(lax.axis_size(a) for a in AXES)
-    up = [(i, i + 1) for i in range(peers - 1)]
-    down = [(i + 1, i) for i in range(peers - 1)]
+    near_pairs = [(i, i ^ 1) for i in range(peers) if i ^ 1 < peers]
+    far_pairs = [(i, i + 1 - 2 * (1 - i % 2)) for i in range(1, peers - 1)]
 
     by_component = jnp.swapaxes(atoms, 0, 1)
     out_grad_by_component = jnp.swapaxes(out_grad, 0, 1)
-    low = lax.ppermute(by_component, AXES, up)
-    high = lax.ppermute(by_component, AXES, down)
+    near = lax.ppermute(by_component, AXES, near_pairs)
+    far = lax.ppermute(by_component, AXES, far_pairs)
 
     links = neighbours - (me * rows - halo)
-    gating = 0.5 * (jnp.cos(math.pi * distances / CUTOFF) + 1.0) * live_mask.astype(F32)
-
-    def as_rows(v):
-        return jnp.swapaxes(v.reshape(chunk_count, GROUP, slots), 1, 2).reshape(
-            chunk_count, 1, edges
-        )
-
-    edge_rows = jnp.concatenate(
-        [as_rows(distances), as_rows(gating), as_rows(links.astype(F32))]
-        + [jnp.zeros((chunk_count, 5, edges), F32)],
-        axis=1,
-    )
-    grouped = links.reshape(chunk_count, edges)
-    first = jnp.min(grouped, axis=1)
-    count = (jnp.max(grouped, axis=1) - first) // WINDOW + 1
-    windows = jnp.stack([first, count], axis=1)
+    edge_args = [jnp.swapaxes(v, 0, 1) for v in (distances, live_mask, links)]
+    edge_specs = [whole(v.shape) for v in edge_args]
+    edge_scratch = [pltpu.VMEM((rows, slots), F32)] * 3
+    first = jnp.min(jnp.min(links, axis=1).reshape(chunk_count, GROUP), axis=1)
+    last = jnp.max(jnp.max(links, axis=1).reshape(chunk_count, GROUP), axis=1)
+    count = (last - first) // WINDOW + 1
+    windows = jnp.stack([jnp.append(first, me % 2), jnp.append(count, 0)], axis=1)
 
     biases = jnp.concatenate([b_rad1, b_rad2, b_rad3]).reshape(-1, LANES)
     mid_width, last_width = w_rad2.shape[1], w_rad3.shape[1]
@@ -760,7 +790,7 @@
     net0 = pl.pallas_call(
         network_kernel,
         grid=(AHEAD,),
-        in_specs=[block((1, 8, edges))] + net_specs,
+        in_specs=edge_specs[:2] + net_specs,
         out_specs=[
             block((edges, KEPT)), block((edges, last_width)), block((edges // 2, LANES))
         ],
@@ -768,23 +798,23 @@
             shape_of((AHEAD * edges, KEPT), BF16), shape_of((AHEAD * edges, last_width), F32),
             shape_of((AHEAD * edges // 2, LANES), BF16),
         ],
-        scratch_shapes=net_scratch,
+        scratch_shapes=edge_scratch[:2] + net_scratch,
         compiler_params=pltpu.CompilerParams(vmem_limit_bytes=vmem),
         cost_estimate=pl.CostEstimate(
             flops=2 * block_edges * 135168, bytes_accessed=block_edges * KEPT * 2, transcendentals=0
         ),
         name="network",
-    )(edge_rows, *net_args)
+    )(*edge_args[:2], *net_args)
 
     grad_rows = 6 * channels + BASES + mid_width // LANES * channels
     grad_rows += last_width // LANES * mid_width + 16
     grad_rows = -(-grad_rows // 128) * 128
-    updated, rim_low, own_grad, rim_high, grads = pl.pallas_call(
+    updated, rim_near, own_grad, rim_far, grads = pl.pallas_call(
         main_kernel,
         grid=(steps,),
         in_specs=[
-            smem, whole(low.shape), whole(by_component.shape), whole(high.shape),
-            components, whole((chunk_count, 8, edges)), *net_specs,
+            smem, whole(near.shape), whole(by_component.shape), whole(far.shape),
+            components, *edge_specs, *net_specs,
             small, small, small, small, small, small,
             *[pl.BlockSpec(memory_space=pl.ANY)] * 3,
         ],
@@ -814,36 +844,48 @@
             pltpu.VMEM((LANES, 2 * channels), F32),
             pltpu.VMEM((3 * channels, channels), F32),
             *net_scratch,
+            *edge_scratch,
             pltpu.SemaphoreType.DMA((AHEAD, 3)),
         ],
         compiler_params=pltpu.CompilerParams(vmem_limit_bytes=vmem),
         name="main",
     )(
-        windows, low, by_component, high, out_grad_by_component, edge_rows, *net_args,
+        windows, near, by_component, far, out_grad_by_component, *edge_args, *net_args,
         w_iso1, w_anti1, w_sym1, w_iso2, w_anti2, w_sym2, *net0,
     )
 
     kept = {}
 
-    def send_rims():
-        kept["above"] = lax.ppermute(rim_low, AXES, down)
-        kept["below"] = lax.ppermute(rim_high, AXES, up)
-        return kept["above"], kept["below"]
-
-    def finish():
+    def nothing(value):
+        return value
+
+    def send_rims(value):
+        value, to_near, to_far = lax.optimization_barrier((value, rim_near, rim_far))
+        kept["near"] = lax.ppermute(to_near, AXES, near_pairs)
+        kept["far"] = lax.ppermute(to_far, AXES, far_pairs)
+        return value
+
+    def have_rims(value):
+        value, kept["near"], kept["far"] = lax.optimization_barrier(
+            (value, kept["near"], kept["far"])
+        )
+        return value
+
+    def finish(value):
         grad_atoms = pl.pallas_call(
             final_kernel,
             out_shape=shape_of((9, rows, channels), F32),
             compiler_params=pltpu.CompilerParams(vmem_limit_bytes=vmem),
             name="final",
         )(
-            own_grad, kept["above"], kept["below"], by_component, out_grad_by_component,
+            own_grad, kept["near"], kept["far"], by_component, out_grad_by_component,
             w_iso1, w_anti1, w_sym1,
         )
-        kept["outs"] = jnp.swapaxes(updated, 0, 1), jnp.swapaxes(grad_atoms, 0, 1)
-        return kept["outs"]
-
-    summed = reduce_everywhere(grads, AXES, (lambda: (), send_rims, finish))
+        value, updated_out, grad_out = lax.optimization_barrier((value, updated, grad_atoms))
+        kept["outs"] = jnp.swapaxes(updated_out, 0, 1), jnp.swapaxes(grad_out, 0, 1)
+        return value
+
+    summed = reduce_everywhere(grads, AXES, (nothing, send_rims, have_rims, finish))
     square_shape = (channels, channels)
     shapes = [square_shape] * 6 + [w_rad1.shape, (1, channels), w_rad2.shape, (1, mid_width)]
     shapes += [w_rad3.shape, (1, last_width)]

time: 146 us -> 136 us (0.932)
  starting transfers between devices: 31 us -> 24.3 us
  Pallas kernels: 92.3 us -> 86.9 us
  waiting for transfers between devices: 11.1 us -> 16.3 us
  local copies, waits for them, and re-layouts: 5.93 us -> 3.11 us
    pallas_call x2, Pallas kernels: 87.4 us -> 82 us  [the longest x1 73.2 us: local(): pl.pallas_call(main_kernel, grid=(steps,), in_specs=[smem, whole(near.sha...]
    ppermute x11, waiting for transfers between devices: 11.1 us -> 16.3 us  [swapped(): return lax.ppermute(v, axes, [(i, i ^ by) for i in range(peers)])]
    ppermute x4, starting transfers between devices: 8.03 us -> 3.55 us  [the longest x1 1.64 us: send_rims(): kept['near'] = lax.ppermute(to_near, AXES, near_pairs)]
    ppermute x11, starting transfers between devices: 22.9 us -> 20.8 us  [swapped(): return lax.ppermute(v, axes, [(i, i ^ by) for i in range(peers)])]
    unnamed x10 -> x8, local copies, waits for them, and re-layouts: 2.86 us -> 1.01 us
  transfers between devices with their start and end apart: 15 -> 15, of which waited for: 7 -> 7; matrix products, arithmetic and copies ran while one was open for 6% -> 3% of each run, Pallas kernels for 9% -> 9%
where the time goes in v3:
time: 136 us
  Pallas kernels  86.9 us (64%)
  starting transfers between devices  24.3 us (18%)
  waiting for transfers between devices  16.3 us (12%)
  other arithmetic  4.79 us (4%)
  local copies, waits for them, and re-layouts  3.11 us (2%)
    pallas_call x1, Pallas kernels, local(): pl.pallas_call(main_kernel, grid=(steps,), in_specs=[smem, whole(near.sha...  73.2 us
    ppermute x11, starting transfers between devices, swapped(): return lax.ppermute(v, axes, [(i, i ^ by) for i in range(peers)])  20.8 us
    ppermute x11, waiting for transfers between devices, swapped(): return lax.ppermute(v, axes, [(i, i ^ by) for i in range(peers)])  16.3 us
    pallas_call x1, Pallas kernels, local(): pl.pallas_call(network_kernel, grid=(AHEAD,), in_specs=edge_specs[:2] + n...  8.8 us
    pallas_call x1, Pallas kernels, finish(): pl.pallas_call(final_kernel, out_shape=shape_of((9, rows, channels), F32)...  3.93 us
  transfers between devices with their start and end apart: 15, of which 7 were waited for; matrix products, arithmetic and copies ran while one was open for 3% of the time, Pallas kernels for 9%

profile of v3, /device:TPU:0, one launch (start us, length us, event | category | flops | bytes accessed | tf_op | source)
XLA Modules:
  0.0 136.3 jit_solution(4307695003942804893)
XLA Ops:
  0.6 0.5 collective-permute-start
  1.2 0.7 collective-permute-start.1
  1.9 1.5 %subtract_reduce_fusion.1 = (s32[256]{0:T(256)S(1)}, s32[256]{0:T(256)S(1)}, s32[64,256]{1,0:T(8,128)}) fusion(s32[256,64]{0,1:T(8,128)} %param.18, s32[]{:T(128)S(6)} %sub.25), kind=kLoop, calls=%fused_computation.19 | loop fusion | flops 48640 | bytes 133124 | tf_op jit(solution)/shard_map/reduce_min | solution.py:773
  3.4 0.1 reshape.59
  3.5 0.1 reduce_min.19
  3.7 0.1 reduce_max.19
  3.9 0.7 copy.35.win_ref
  4.6 1.3 maximum_bitcast_fusion.bias_ref
  5.9 8.8 %network.1 = (bf16[3072,1152]{1,0:T(8,128)(2,1)}, f32[3072,384]{1,0:T(8,128)}, bf16[1536,128]{1,0:T(8,128)(2,1)}) custom-call(f32[64,256]{1,0:T(8,128)} %bitcast.61, s32[64,256]{1,0:T(8,128)} %bitcast.63, bf16[32,128]{1,0:T(8,128)(2,1)} %w1_raw.3, bf16[128,256]{1,0:T(8,128)(2,1)} %w2_raw.3, bf16[256,384]{1,0:T(8,128)(2,1)} %w3_raw.3, ...), custom_call_target="tpu_custom_call" | custom-call | flops 1107296256 | bytes 9437184 | tf_op jit(solution)/shard_map/network/pallas_call | solution.py:790
  14.7 0.8 copy-done
  15.5 0.2 copy-done.1
  15.7 73.2 %main.1 = (bf16[9,256,128]{2,1,0:T(8,128)(2,1)}, bf16[256,1152]{1,0:T(8,128)(2,1)}, f32[256,1152]{1,0:T(8,128)}, bf16[256,1152]{1,0:T(8,128)(2,1)}, bf16[1920,128]{1,0:T(8,128)(2,1)}) custom-call(s32[33,2]{1,0:T(8,128)} %copy.35.win_ref, bf16[9,256,128]{2,1,0:T(8,128)(2,1)} %copy-done, bf16[9,256,128]{2,1,0:T(8,128)(2,1)} %bitcast.50, ...), custom_call_target="tpu_custom_call" | custom-call | tf_op jit(solution)/shard_map/main/pallas_call | solution.py:812
  88.9 1.0 dynamic-slice_bitcast_fusion
  89.9 4.4 %collective-permute-start.2 = (bf16[960,128]{1,0:T(8,128)(2,1)S(1)}, bf16[960,128]{1,0:T(8,128)(2,1)S(1)}, u32[]{:S(2)}, u32[]{:S(2)}) collective-permute-start(bf16[960,128]{1,0:T(8,128)(2,1)S(1)} %dynamic-slice_bitcast_fusion), channel_id=1, source_target_pairs={{0,1},{1,0},{2,3},{3,2},{4,5},{5,4},{6,7},{7,6},{8,9},{9,8},{10,11... | collective-permute-start | bytes 737288 | tf_op jit(solution)/shard_map/ppermute | solution.py:718
  94.3 1.1 collective-permute-done.2
  95.4 1.0 fusion
  96.5 4.0 %collective-permute-start.3 = (bf16[240,128]{1,0:T(8,128)(2,1)S(1)}, bf16[240,128]{1,0:T(8,128)(2,1)S(1)}, u32[]{:S(2)}, u32[]{:S(2)}) collective-permute-start(bf16[240,128]{1,0:T(8,128)(2,1)S(1)} %get-tuple-element.74), channel_id=1, source_target_pairs={{0,2},{1,3},{2,0},{3,1},{4,6},{5,7},{6,4},{7,5},{8,10},{9,11},{10,... | collective-permute-start | bytes 184328 | tf_op jit(solution)/shard_map/ppermute | solution.py:718
  100.5 1.5 %collective-permute-start.5 = (bf16[240,128]{1,0:T(8,128)(2,1)S(1)}, bf16[240,128]{1,0:T(8,128)(2,1)S(1)}, u32[]{:S(2)}, u32[]{:S(2)}) collective-permute-start(bf16[240,128]{1,0:T(8,128)(2,1)S(1)} %get-tuple-element.75), channel_id=1, source_target_pairs={{0,6},{1,7},{2,4},{3,5},{4,2},{5,3},{6,0},{7,1},{8,14},{9,15},{10,... | collective-permute-start | bytes 184328 | tf_op jit(solution)/shard_map/ppermute | solution.py:718
  102.0 0.9 collective-permute-done.3
  102.9 3.0 %collective-permute-done.4 = bf16[240,128]{1,0:T(8,128)(2,1)S(1)} collective-permute-done((bf16[240,128]{1,0:T(8,128)(2,1)S(1)}, bf16[240,128]{1,0:T(8,128)(2,1)S(1)}, u32[]{:S(2)}, u32[]{:S(2)}) %collective-permute-start.4) | collective-permute-done | bytes 61472 | tf_op jit(solution)/shard_map/ppermute | solution.py:718
  105.9 0.7 collective-permute-start.10
  106.7 1.6 %collective-permute-start.9 = (bf16[256,1152]{1,0:T(8,128)(2,1)}, bf16[256,1152]{1,0:T(8,128)(2,1)S(1)}, u32[]{:S(2)}, u32[]{:S(2)}) collective-permute-start(bf16[256,1152]{1,0:T(8,128)(2,1)} %get-tuple-element.50), channel_id=1, source_target_pairs={{0,1},{1,0},{2,3},{3,2},{4,5},{5,4},{6,7},{7,6},{8,9},{9,8},{10,11... | collective-permute-start | bytes 1769480 | tf_op jit(solution)/shard_map/ppermute | solution.py:864
  108.3 2.3 %collective-permute-start.6 = (bf16[240,128]{1,0:T(8,128)(2,1)S(1)}, bf16[240,128]{1,0:T(8,128)(2,1)S(1)}, u32[]{:S(2)}, u32[]{:S(2)}) collective-permute-start(bf16[240,128]{1,0:T(8,128)(2,1)S(1)} %fusion.3), channel_id=1, source_target_pairs={{0,8},{1,9},{2,10},{3,11},{4,12},{5,13},{6,14},{7,15},{8,0},{9,1},... | collective-permute-start | bytes 184328 | tf_op jit(solution)/shard_map/ppermute | solution.py:718
  110.6 5.0 %collective-permute-start.7 = (bf16[240,128]{1,0:T(8,128)(2,1)S(1)}, bf16[240,128]{1,0:T(8,128)(2,1)S(1)}, u32[]{:S(2)}, u32[]{:S(2)}) collective-permute-start(bf16[240,128]{1,0:T(8,128)(2,1)S(1)} %fusion.3), channel_id=1, source_target_pairs={{0,16},{1,17},{2,18},{3,19},{4,20},{5,21},{6,22},{7,23},{8,24},{9,... | collective-permute-start | bytes 184328 | tf_op jit(solution)/shard_map/ppermute | solution.py:718
  115.5 4.3 %collective-permute-done.6 = bf16[240,128]{1,0:T(8,128)(2,1)S(1)} collective-permute-done((bf16[240,128]{1,0:T(8,128)(2,1)S(1)}, bf16[240,128]{1,0:T(8,128)(2,1)S(1)}, u32[]{:S(2)}, u32[]{:S(2)}) %collective-permute-start.6) | collective-permute-done | bytes 61472 | tf_op jit(solution)/shard_map/ppermute | solution.py:718
  119.9 2.0 %collective-permute-done.7 = bf16[240,128]{1,0:T(8,128)(2,1)S(1)} collective-permute-done((bf16[240,128]{1,0:T(8,128)(2,1)S(1)}, bf16[240,128]{1,0:T(8,128)(2,1)S(1)}, u32[]{:S(2)}, u32[]{:S(2)}) %collective-permute-start.7) | collective-permute-done | bytes 61472 | tf_op jit(solution)/shard_map/ppermute | solution.py:718
  121.8 3.6 %collective-permute-done.8 = bf16[240,128]{1,0:T(8,128)(2,1)S(1)} collective-permute-done((bf16[240,128]{1,0:T(8,128)(2,1)S(1)}, bf16[240,128]{1,0:T(8,128)(2,1)S(1)}, u32[]{:S(2)}, u32[]{:S(2)}) %collective-permute-start.8) | collective-permute-done | bytes 61472 | tf_op jit(solution)/shard_map/ppermute | solution.py:718
  125.6 3.4 %collective-permute-start.13 = (bf16[240,128]{1,0:T(8,128)(2,1)S(1)}, bf16[240,128]{1,0:T(8,128)(2,1)S(1)}, u32[]{:S(2)}, u32[]{:S(2)}) collective-permute-start(bf16[240,128]{1,0:T(8,128)(2,1)S(1)} %add_convert_fusion), channel_id=1, source_target_pairs={{0,6},{1,7},{2,4},{3,5},{4,2},{5,3},{6,0},{7,1},{8,14},{9,15},{10,... | collective-permute-start | bytes 184328 | tf_op jit(solution)/shard_map/ppermute | solution.py:718
  129.1 3.9 %final.1 = f32[9,256,128]{2,1,0:T(8,128)} custom-call(f32[256,1152]{1,0:T(8,128)} %get-tuple-element.54.own_ref, bf16[256,1152]{1,0:T(8,128)(2,1)} %copy-done.3, bf16[256,1152]{1,0:T(8,128)(2,1)} %copy-done.2, bf16[9,256,128]{2,1,0:T(8,128)(2,1)} %bitcast.51, bf16[9,256,128]{2,1,0:T(8,128)(2,1)} %bitcast.53, bf16[128,128]{1,0:T(8,128)(2,1)} %iso1_ref.3, ...), custom_call_target="tpu_custom_call" | custom-call | tf_op jit(solution)/shard_map/final/pallas_call | solution.py:875
  133.3 1.4 %collective-permute-done.14 = bf16[960,128]{1,0:T(8,128)(2,1)S(1)} collective-permute-done((bf16[960,128]{1,0:T(8,128)(2,1)S(1)}, bf16[960,128]{1,0:T(8,128)(2,1)S(1)}, u32[]{:S(2)}, u32[]{:S(2)}) %collective-permute-start.14) | collective-permute-done | bytes 245792 | tf_op jit(solution)/shard_map/ppermute | solution.py:718
  134.8 1.0 unpack.1
  135.7 0.6 reduce
  (34 shorter events, 0.8 us)
Async XLA Ops:
  0.6 14.0 %collective-permute-start = (bf16[9,256,128]{2,1,0:T(8,128)(2,1)}, bf16[9,256,128]{2,1,0:T(8,128)(2,1)S(1)}, u32[]{:S(2)}, u32[]{:S(2)}) collective-permute-start(bf16[9,256,128]{2,1,0:T(8,128)(2,1)} %bitcast.48), channel_id=1, source_target_pairs={{0,1},{1,0},{2,3},{3,2},{4,5},{5,4},{6,7},{7,6},{8,9},{9,8},{10,11... | collective-permute-start | bytes 1769480 | tf_op jit(solution)/shard_map/ppermute | solution.py:766
  1.2 13.5 %collective-permute-start.1 = (bf16[9,256,128]{2,1,0:T(8,128)(2,1)}, bf16[9,256,128]{2,1,0:T(8,128)(2,1)S(1)}, u32[]{:S(2)}, u32[]{:S(2)}) collective-permute-start(bf16[9,256,128]{2,1,0:T(8,128)(2,1)} %bitcast.49), channel_id=1, source_target_pairs={{1,2},{2,1},{3,4},{4,3},{5,6},{6,5},{7,8},{8,7},{9,10},{10,9},{11,... | collective-permute-start | bytes 1769480 | tf_op jit(solution)/shard_map/ppermute | solution.py:767
  14.7 0.8 copy-start
  14.7 1.0 copy-start.1
  89.9 5.5 %collective-permute-start.2 = (bf16[960,128]{1,0:T(8,128)(2,1)S(1)}, bf16[960,128]{1,0:T(8,128)(2,1)S(1)}, u32[]{:S(2)}, u32[]{:S(2)}) collective-permute-start(bf16[960,128]{1,0:T(8,128)(2,1)S(1)} %dynamic-slice_bitcast_fusion), channel_id=1, source_target_pairs={{0,1},{1,0},{2,3},{3,2},{4,5},{5,4},{6,7},{7,6},{8,9},{9,8},{10,11... | collective-permute-start | bytes 737288 | tf_op jit(solution)/shard_map/ppermute | solution.py:718
  96.5 6.4 %collective-permute-start.3 = (bf16[240,128]{1,0:T(8,128)(2,1)S(1)}, bf16[240,128]{1,0:T(8,128)(2,1)S(1)}, u32[]{:S(2)}, u32[]{:S(2)}) collective-permute-start(bf16[240,128]{1,0:T(8,128)(2,1)S(1)} %get-tuple-element.74), channel_id=1, source_target_pairs={{0,2},{1,3},{2,0},{3,1},{4,6},{5,7},{6,4},{7,5},{8,10},{9,11},{10,... | collective-permute-start | bytes 184328 | tf_op jit(solution)/shard_map/ppermute | solution.py:718
  100.5 5.4 %collective-permute-start.4 = (bf16[240,128]{1,0:T(8,128)(2,1)S(1)}, bf16[240,128]{1,0:T(8,128)(2,1)S(1)}, u32[]{:S(2)}, u32[]{:S(2)}) collective-permute-start(bf16[240,128]{1,0:T(8,128)(2,1)S(1)} %get-tuple-element.76), channel_id=1, source_target_pairs={{0,4},{1,5},{2,6},{3,7},{4,0},{5,1},{6,2},{7,3},{8,12},{9,13},{10,... | collective-permute-start | bytes 184328 | tf_op jit(solution)/shard_map/ppermute | solution.py:718
  100.5 5.4 %collective-permute-start.5 = (bf16[240,128]{1,0:T(8,128)(2,1)S(1)}, bf16[240,128]{1,0:T(8,128)(2,1)S(1)}, u32[]{:S(2)}, u32[]{:S(2)}) collective-permute-start(bf16[240,128]{1,0:T(8,128)(2,1)S(1)} %get-tuple-element.75), channel_id=1, source_target_pairs={{0,6},{1,7},{2,4},{3,5},{4,2},{5,3},{6,0},{7,1},{8,14},{9,15},{10,... | collective-permute-start | bytes 184328 | tf_op jit(solution)/shard_map/ppermute | solution.py:718
  105.9 19.5 %collective-permute-start.10 = (bf16[256,1152]{1,0:T(8,128)(2,1)}, bf16[256,1152]{1,0:T(8,128)(2,1)S(1)}, u32[]{:S(2)}, u32[]{:S(2)}) collective-permute-start(bf16[256,1152]{1,0:T(8,128)(2,1)} %get-tuple-element.51), channel_id=1, source_target_pairs={{1,2},{2,1},{3,4},{4,3},{5,6},{6,5},{7,8},{8,7},{9,10},{10,9},{11,... | collective-permute-start | bytes 1769480 | tf_op jit(solution)/shard_map/ppermute | solution.py:865
  106.7 18.8 %collective-permute-start.9 = (bf16[256,1152]{1,0:T(8,128)(2,1)}, bf16[256,1152]{1,0:T(8,128)(2,1)S(1)}, u32[]{:S(2)}, u32[]{:S(2)}) collective-permute-start(bf16[256,1152]{1,0:T(8,128)(2,1)} %get-tuple-element.50), channel_id=1, source_target_pairs={{0,1},{1,0},{2,3},{3,2},{4,5},{5,4},{6,7},{7,6},{8,9},{9,8},{10,11... | collective-permute-start | bytes 1769480 | tf_op jit(solution)/shard_map/ppermute | solution.py:864
  108.3 11.6 %collective-permute-start.6 = (bf16[240,128]{1,0:T(8,128)(2,1)S(1)}, bf16[240,128]{1,0:T(8,128)(2,1)S(1)}, u32[]{:S(2)}, u32[]{:S(2)}) collective-permute-start(bf16[240,128]{1,0:T(8,128)(2,1)S(1)} %fusion.3), channel_id=1, source_target_pairs={{0,8},{1,9},{2,10},{3,11},{4,12},{5,13},{6,14},{7,15},{8,0},{9,1},... | collective-permute-start | bytes 184328 | tf_op jit(solution)/shard_map/ppermute | solution.py:718
  110.6 11.3 %collective-permute-start.7 = (bf16[240,128]{1,0:T(8,128)(2,1)S(1)}, bf16[240,128]{1,0:T(8,128)(2,1)S(1)}, u32[]{:S(2)}, u32[]{:S(2)}) collective-permute-start(bf16[240,128]{1,0:T(8,128)(2,1)S(1)} %fusion.3), channel_id=1, source_target_pairs={{0,16},{1,17},{2,18},{3,19},{4,20},{5,21},{6,22},{7,23},{8,24},{9,... | collective-permute-start | bytes 184328 | tf_op jit(solution)/shard_map/ppermute | solution.py:718
  115.5 9.9 %collective-permute-start.8 = (bf16[240,128]{1,0:T(8,128)(2,1)S(1)}, bf16[240,128]{1,0:T(8,128)(2,1)S(1)}, u32[]{:S(2)}, u32[]{:S(2)}) collective-permute-start(bf16[240,128]{1,0:T(8,128)(2,1)S(1)} %fusion.3), channel_id=1, source_target_pairs={{0,24},{1,25},{2,26},{3,27},{4,28},{5,29},{6,30},{7,31},{8,16},{9,... | collective-permute-start | bytes 184328 | tf_op jit(solution)/shard_map/ppermute | solution.py:718
  125.5 3.6 %copy-start.2 = (bf16[256,1152]{1,0:T(8,128)(2,1)}, bf16[256,1152]{1,0:T(8,128)(2,1)S(1)}, u32[]{:S(2)}) copy-start(bf16[256,1152]{1,0:T(8,128)(2,1)S(1)} %collective-permute-done.10.far_ref) | copy-start | bytes 1769476
  125.5 3.6 %copy-start.3 = (bf16[256,1152]{1,0:T(8,128)(2,1)}, bf16[256,1152]{1,0:T(8,128)(2,1)S(1)}, u32[]{:S(2)}) copy-start(bf16[256,1152]{1,0:T(8,128)(2,1)S(1)} %collective-permute-done.9.near_ref) | copy-start | bytes 1769476
  125.5 7.6 %collective-permute-start.11 = (bf16[240,128]{1,0:T(8,128)(2,1)S(1)}, bf16[240,128]{1,0:T(8,128)(2,1)S(1)}, u32[]{:S(2)}, u32[]{:S(2)}) collective-permute-start(bf16[240,128]{1,0:T(8,128)(2,1)S(1)} %add_convert_fusion), channel_id=1, source_target_pairs={{0,2},{1,3},{2,0},{3,1},{4,6},{5,7},{6,4},{7,5},{8,10},{9,11},{10,... | collective-permute-start | bytes 184328 | tf_op jit(solution)/shard_map/ppermute | solution.py:718
  125.6 7.5 %collective-permute-start.12 = (bf16[240,128]{1,0:T(8,128)(2,1)S(1)}, bf16[240,128]{1,0:T(8,128)(2,1)S(1)}, u32[]{:S(2)}, u32[]{:S(2)}) collective-permute-start(bf16[240,128]{1,0:T(8,128)(2,1)S(1)} %add_convert_fusion), channel_id=1, source_target_pairs={{0,4},{1,5},{2,6},{3,7},{4,0},{5,1},{6,2},{7,3},{8,12},{9,13},{10,... | collective-permute-start | bytes 184328 | tf_op jit(solution)/shard_map/ppermute | solution.py:718
  125.6 7.5 %collective-permute-start.13 = (bf16[240,128]{1,0:T(8,128)(2,1)S(1)}, bf16[240,128]{1,0:T(8,128)(2,1)S(1)}, u32[]{:S(2)}, u32[]{:S(2)}) collective-permute-start(bf16[240,128]{1,0:T(8,128)(2,1)S(1)} %add_convert_fusion), channel_id=1, source_target_pairs={{0,6},{1,7},{2,4},{3,5},{4,2},{5,3},{6,0},{7,1},{8,14},{9,15},{10,... | collective-permute-start | bytes 184328 | tf_op jit(solution)/shard_map/ppermute | solution.py:718
  133.1 1.6 %collective-permute-start.14 = (bf16[960,128]{1,0:T(8,128)(2,1)S(1)}, bf16[960,128]{1,0:T(8,128)(2,1)S(1)}, u32[]{:S(2)}, u32[]{:S(2)}) collective-permute-start(bf16[960,128]{1,0:T(8,128)(2,1)S(1)} %bitcast.57), channel_id=1, source_target_pairs={{0,1},{1,0},{2,3},{3,2},{4,5},{5,4},{6,7},{7,6},{8,9},{9,8},{10,11... | collective-permute-start | bytes 737288 | tf_op jit(solution)/shard_map/ppermute | solution.py:718

commit v4 on v3

--- a/solution.py
+++ b/solution.py
@@ -15,7 +15,8 @@
 BASES = 32
 UNROLL = 2
 PAIRS = ((0, 1), (2, 3), (4, 5), (6, 7), (8,))
-SCHEDULE = "0H0T0D000a01040G0b0J030c0W0d0p0E0e0F0x0V0y020U0z1H1T1D101a111b121G1J131c141d1p1E1e1F1y1x1V1U1z1W"
+GATHER = "0k0D0E0A0d0B0a0C0b1k0c1D1E1A1d1B1a1C1b1c"
+SCHEDULE = "".join(n + s for n in "01" for s in "HaTDb0GJ1cWdp2E3eF4xVyUz")
 WINDOW = 256
 KIND = (0, 1, 1, 1, 2, 2, 2, 2, 2)
 AXES = ("edge", "grp")
@@ -134,7 +135,7 @@
 
 
 def parts_in(atoms_ref, at):
-    values = [atoms_ref[c, at : at + 64, :].astype(F32) for c in range(9)]
+    values = [atoms_ref[c, at : at + BLOCK, :].astype(F32) for c in range(9)]
     scale = 1.0 / (1.0 + total([v * v for v in values]))
     return rounded_parts(square([v * scale for v in values]))
 
@@ -192,6 +193,7 @@
 SLOPE3, ACT2, SLOPE2 = slice(0, 384), slice(384, 640), slice(640, 896)
 ACT1, SLOPE1 = slice(896, 1024), slice(1024, 1152)
 KEPT = 1152
+BLOCK = 32
 HALF = 64
 AHEAD = 6
 
@@ -321,8 +323,8 @@
     win_ref, near_ref, own_ref, far_ref, outgrad_ref, dist_ref, live_ref, link_ref,
     w1_raw, w2_raw, w3_raw, bias_ref,
     iso1_ref, anti1_ref, sym1_ref, iso2_ref, anti2_ref, sym2_ref, net_first, fac_first, basis_first,
-    upd_ref, rim_near_ref, own_out_ref, rim_far_ref, grads_ref,
-    table, net_a, net_b, fac_a, fac_b, basis_a, basis_b, x_s, msg_s, gm_s, spread,
+    upd_ref, rim_near_ref, own_out_ref, rim_far_ref, mine_ref, other_ref,
+    table, parts_s, net_a, net_b, fac_a, fac_b, basis_a, basis_b, x_s, msg_s, gm_s, spread,
     d3_ref, d2_ref, d1_ref, dw2_ref, w1_ref, w2_ref, w3_ref, b3_ref,
     dist_s, gate_s, link_s, sems,
 ):
@@ -364,10 +366,14 @@
         link_s[...] = by_atom(link_ref)
         weights = (iso1_ref[...], anti1_ref[...], sym1_ref[...])
         for ref, place in ((near_ref, near_at), (own_ref, halo), (far_ref, far_at)):
-            for at in range(0, ref.shape[1], 64):
-                mixed = mix_parts(parts_in(ref, at), weights)
+            for at in range(0, ref.shape[1], BLOCK):
+                here = pl.ds(place + at, BLOCK)
+                parts = parts_in(ref, at)
+                for c, v in enumerate(parts):
+                    parts_s[here, col(c)] = v
+                mixed = mix_parts(parts, weights)
                 for n, (p, q) in enumerate(ORDER):
-                    table[pl.ds(place + at, 64), col(n)] = mixed[p][q].astype(BF16)
+                    table[here, col(n)] = mixed[p][q].astype(BF16)
         place = far_side + halo
         table[place:, :] = jnp.zeros((table.shape[0] - place, wide), BF16)
         d3_ref[...] = jnp.zeros_like(d3_ref)
@@ -381,42 +387,66 @@
             mine = chunk_atoms(j)
             Network(dist_s[mine, :], gate_s[mine, :], net_a, fac_a, basis_a, j, radial).run()
 
-    def gather(fac, j, w, more):
-        here = pl.ds(pl.multiple_of(j * edges, edges), edges)
-        index = step * chunks + j
-        key, base, off = window_key(link_s[chunk_atoms(index), :], win_ref[index, 0], w)
-        near = lax.broadcasted_iota(jnp.int32, (edges, WINDOW), 1).astype(F32)
-        hot = (over_lanes(key, range(slots), WINDOW) == near).astype(BF16)
-        kept = lax.broadcasted_iota(jnp.int32, (16, LANES), 0) >= off
-        kept = jnp.where(kept, 1.0, 0.0).astype(BF16)[:, 0:1]
-        factors = [fac[here, col(k)] for k in range(3)]
-        to = pl.ds(pl.multiple_of(j * GROUP, GROUP), GROUP)
-
-        def rows_of(lanes):
-            top = table[pl.ds(base, 16), lanes] * kept
-            top += table[pl.ds(base + WINDOW, 16), lanes] * (1.0 - kept)
-            rest = table[pl.ds(base + 16, WINDOW - 16), lanes]
-            got = dot(hot, jnp.concatenate([top, rest], axis=0))
-            return [got[:, col(n)] for n in range(got.shape[1] // LANES)]
-
-        def use(c, x):
+    class Gather:
+        def __init__(self, fac, j, w, more):
+            self.j, self.w, self.fac, self.more, self.got = j, w, fac, more, {}
+            self.here = pl.ds(pl.multiple_of(j * edges, edges), edges)
+            self.to = pl.ds(pl.multiple_of(j * GROUP, GROUP), GROUP)
+
+        def hot(self):
+            index = step * chunks + self.j
+            key, self.base, off = window_key(
+                link_s[chunk_atoms(index), :], win_ref[index, 0], self.w
+            )
+            near = lax.broadcasted_iota(jnp.int32, (edges, WINDOW), 1).astype(F32)
+            self.key = (over_lanes(key, range(slots), WINDOW) == near).astype(BF16)
+            kept = lax.broadcasted_iota(jnp.int32, (16, LANES), 0) >= off
+            self.kept = jnp.where(kept, 1.0, 0.0).astype(BF16)[:, 0:1]
+
+        def rows_of(self, first, past):
+            lanes = slice(first * LANES, past * LANES)
+            top = table[pl.ds(self.base, 16), lanes] * self.kept
+            top += table[pl.ds(self.base + WINDOW, 16), lanes] * (1.0 - self.kept)
+            rest = table[pl.ds(self.base + 16, WINDOW - 16), lanes]
+            got = dot(self.key, jnp.concatenate([top, rest], axis=0))
+            for n in range(past - first):
+                self.got[first + n] = got[:, col(n)]
+
+        def use(self, c, x):
             rounded = x.astype(BF16)
-            message = factors[KIND[c]] * x
+            message = self.fac[self.here, col(KIND[c])] * x
             message = jnp.sum(message.reshape(slots, GROUP, LANES), axis=0)
-            x_s[here, col(c)] = x_s[here, col(c)] + rounded if more else rounded
-            msg_s[to, col(c)] = msg_s[to, col(c)] + message if more else message
-
-        for n in range(3):
-            one, other = rows_of(slice(2 * n * LANES, 2 * (n + 1) * LANES))
-            use(1 + n, one - other)
-            use(4 + n, one + other)
-        x00, x11 = rows_of(slice(6 * LANES, 8 * LANES))
-        (x22,) = rows_of(slice(8 * LANES, 9 * LANES))
-        trace = x00 + x11 + x22
-        third = trace * (1.0 / 3.0)
-        use(0, trace)
-        use(7, x00 - third)
-        use(8, x11 - third)
+            if self.more:
+                rounded += x_s[self.here, col(c)]
+                message += msg_s[self.to, col(c)]
+            x_s[self.here, col(c)] = rounded
+            msg_s[self.to, col(c)] = message
+
+        def pair(self, n):
+            one, other = self.got.pop(2 * n), self.got.pop(2 * n + 1)
+            self.use(1 + n, one - other)
+            self.use(4 + n, one + other)
+
+        def diagonal(self):
+            x00, x11, x22 = (self.got.pop(n) for n in (6, 7, 8))
+            trace = x00 + x11 + x22
+            third = trace * (1.0 / 3.0)
+            self.use(0, trace)
+            self.use(7, x00 - third)
+            self.use(8, x11 - third)
+
+    def gather(fac, places, w, more, order):
+        steps_of = {
+            "k": lambda g: g.hot(),
+            "A": lambda g: g.rows_of(0, 2), "B": lambda g: g.rows_of(2, 4),
+            "C": lambda g: g.rows_of(4, 6), "D": lambda g: g.rows_of(6, 8),
+            "E": lambda g: g.rows_of(8, 9), "a": lambda g: g.pair(0), "b": lambda g: g.pair(1),
+            "c": lambda g: g.pair(2), "d": lambda g: g.diagonal(),
+        }
+        each = [Gather(fac, j, w, more) for j in places]
+        for which, name in zip(order[::2], order[1::2]):
+            if int(which) < len(each):
+                steps_of[name](each[int(which)])
 
     even = step % 2 == 0
 
@@ -431,14 +461,13 @@
                         for copy in fetches(pair * UNROLL + n):
                             copy.wait()
 
-            for n in range(UNROLL):
-                gather(fac, pair * UNROLL + n, 0, False)
+            gather(fac, [pair * UNROLL + n for n in range(UNROLL)], 0, False, GATHER)
 
         @pl.loop(0, chunks)
         def _(j):
             @pl.loop(1, win_ref[step * chunks + j, 1])
             def _(w):
-                gather(fac, j, w, True)
+                gather(fac, [j], w, True, GATHER)
 
     @pl.when(even)
     def _():
@@ -621,50 +650,86 @@
     def _():
         sweep((net_b, fac_b, basis_b), None)
         grads = [None] * 3
-        for ref, out, place in (
-            (near_ref, rim_near_ref, near_at),
-            (own_ref, own_out_ref, halo),
-            (far_ref, rim_far_ref, far_at),
+        for out, place in (
+            (rim_near_ref, near_at), (own_out_ref, halo), (rim_far_ref, far_at)
         ):
-            for at in range(0, out.shape[0], 64):
-                coords = [spread[pl.ds(place + at, 64), col(c)] for c in range(9)]
-                for c in range(9):
-                    out[at : at + 64, col(c)] = coords[c].astype(out.dtype)
-                seen = seen_by_kind(to_matrix(coords))
-                fresh = weight_grads(parts_in(ref, at), seen)
-                grads = [n if o is None else o + n for o, n in zip(grads, fresh)]
+            coords = []
+            for c in range(9):
+                value = spread[pl.ds(place, out.shape[0]), col(c)]
+                out[:, col(c)] = value.astype(out.dtype)
+                coords.append(value)
+            t, s00, s11 = coords[0], coords[7], coords[8]
+            right = [3.0 * t] + [2.0 * v for v in coords[1:7]] + [s00, s11, -s00 - s11]
+            left = [parts_s[pl.ds(place, out.shape[0]), col(c)] for c in range(10)]
+            fresh = [
+                dot_first(stack(left[lo:hi]), stack(right[lo:hi]))
+                for lo, hi in ((0, 1), (1, 4), (4, 10))
+            ]
+            grads = [n if o is None else o + n for o, n in zip(grads, fresh)]
         first = d1_ref[:HALF, :LANES] + d1_ref[HALF:, LANES:]
-        place = 0
-        for value in (*grads, dw2_ref[...], first[:BASES]):
-            grads_ref[place : place + value.shape[0], :] = value.astype(BF16)
-            place += value.shape[0]
+        deep = d3_ref.shape[0] - 16
+        thirds = [d3_ref[:deep, col(n)] for n in range(3)]
         biases = [first[BASES : BASES + 1]]
-        for ref in (d2_ref, d3_ref):
-            deep = ref.shape[0] - 16
-            for n in range(ref.shape[1] // LANES):
-                grads_ref[place : place + deep, :] = ref[:deep, col(n)].astype(BF16)
-                biases.append(ref[deep : deep + 1, col(n)])
-                place += deep
-        biases.append(jnp.zeros((grads_ref.shape[0] - place - len(biases), LANES), F32))
-        grads_ref[place:, :] = jnp.concatenate(biases, axis=0).astype(BF16)
-
-
-def unpack_kernel(grads_ref, *out_refs):
-    small, g_w1, g_w2, g_w3 = out_refs[:6], out_refs[6], out_refs[8], out_refs[10]
-    place = 0
-    for ref in (*small, g_w1):
-        ref[...] = grads_ref[place : place + ref.shape[0], :].astype(F32)
-        place += ref.shape[0]
-    for ref in (g_w2, g_w3):
-        for n in range(ref.shape[1] // LANES):
-            ref[:, col(n)] = grads_ref[place : place + ref.shape[0], :].astype(F32)
-            place += ref.shape[0]
-    biases = grads_ref[place : place + 16, :].astype(F32)
-    row = 0
-    for ref in (out_refs[7], out_refs[9], out_refs[11]):
-        for n in range(ref.shape[1] // LANES):
-            ref[:, col(n)] = biases[row : row + 1, :]
-            row += 1
+        biases += [d2_ref[LANES : LANES + 1, col(n)] for n in range(2)]
+        biases += [d3_ref[deep : deep + 1, col(n)] for n in range(3)]
+        biases.append(jnp.zeros((16 - len(biases), LANES), F32))
+        biases = jnp.concatenate(biases, axis=0)
+        halves = (
+            [*thirds, d2_ref[:LANES, col(0)], first[:BASES], biases],
+            [*grads, dw2_ref[...], d2_ref[:LANES, col(1)]],
+        )
+
+        def put_half(out, values):
+            place = 0
+            for value in values:
+                out[place : place + value.shape[0], :] = value.astype(out.dtype)
+                place += value.shape[0]
+            out[place:, :] = jnp.zeros((out.shape[0] - place, LANES), out.dtype)
+
+        for side in range(2):
+
+            @pl.when(odd == side)
+            def _():
+                put_half(mine_ref, halves[side])
+                put_half(other_ref, halves[1 - side])
+
+
+def unpack_kernel(shares, place_ref, mine_ref, other_ref, *out_refs):
+    small, (g_w1, g_b1, g_w2, g_b2, g_w3, g_b3) = out_refs[:6], out_refs[6:12]
+    mine_s, other_s = out_refs[12:]
+    rows = mine_ref.shape[0] // shares
+    for n in range(shares):
+        to = pl.ds(pl.multiple_of((place_ref[1] ^ n) * rows, 16), rows)
+        mine_s[to, :] = mine_ref[n * rows : (n + 1) * rows, :].astype(F32)
+        other_s[to, :] = other_ref[n * rows : (n + 1) * rows, :].astype(F32)
+
+    def unpack(one, two):
+        deep = g_w3.shape[0]
+        for n in range(3):
+            g_w3[:, col(n)] = one[n * deep : (n + 1) * deep, :]
+        place = 3 * deep
+        g_w2[:, col(0)] = one[place : place + LANES, :]
+        place += LANES
+        g_w1[...] = one[place : place + BASES, :]
+        place += BASES
+        biases = one[place : place + 16, :]
+        row = 0
+        for ref in (g_b1, g_b2, g_b3):
+            count = ref.shape[0] // LANES
+            for n in range(count):
+                ref[col(n)] = biases[row + n]
+            row += count
+        for n, ref in enumerate(small):
+            ref[...] = two[n * LANES : (n + 1) * LANES, :]
+        g_w2[:, col(1)] = two[6 * LANES : 7 * LANES, :]
+
+    @pl.when(place_ref[0] == 0)
+    def _():
+        unpack(mine_s, other_s)
+
+    @pl.when(place_ref[0] == 1)
+    def _():
+        unpack(other_s, mine_s)
 
 
 def final_kernel(
@@ -700,7 +765,7 @@
     return lax.dynamic_index_in_dim(value, index, 0, keepdims=False)
 
 
-def reduce_everywhere(value, axes, beside):
+def reduce_everywhere(mine, other, axes, beside):
     beside = list(beside)
 
     def between(v):
@@ -708,35 +773,42 @@
 
     peers = math.prod(lax.axis_size(a) for a in axes)
     me = lax.axis_index(axes)
-    runs, at = [], 1
+    runs, at = [], 2
     while at < peers:
-        size = min(2 if at == 1 else 4, peers // at)
-        runs.append((at, size))
-        at *= size
+        runs.append((at, min(4, peers // at)))
+        at *= runs[-1][1]
+    runs = runs[1:] + runs[:1]
 
     def swapped(v, by):
         return lax.ppermute(v, axes, [(i, i ^ by) for i in range(peers)])
 
+    value = between(mine + swapped(other, 1).astype(F32))
     for at, size in runs[:-1]:
         shares = value.reshape(size, value.shape[0] // size, value.shape[1])
-        mine = me // at % size
-        kept = part(shares, mine).astype(F32)
+        own = me // at % size
+        kept = part(shares, own)
         for k in range(1, size):
-            kept = kept + swapped(part(shares, mine ^ k), k * at).astype(F32)
-        value = between(kept.astype(BF16))
+            kept = kept + swapped(part(shares, own ^ k).astype(BF16), k * at).astype(F32)
+        value = between(kept)
     at, size = runs[-1]
-    kept = value.astype(F32)
-    for k in range(1, size):
-        kept = kept + swapped(value, k * at).astype(F32)
-    value = between(kept.astype(BF16))
-    for at, size in runs[-2::-1]:
-        mine = me // at % size
+    value = value.astype(BF16)
+    terms = [value] + [swapped(value, k * at) for k in range(1, size)]
+    terms[1] = between(terms[1])
+    terms = [v.astype(F32) for v in terms]
+    while len(terms) > 1:
+        terms = [a + b for a, b in zip(terms[::2], terms[1::2])]
+    value = between(terms[0].astype(BF16))
+    for at, size in runs[-2:0:-1]:
+        own = me // at % size
         full = jnp.zeros((size,) + value.shape, value.dtype)
-        full = lax.dynamic_update_index_in_dim(full, value, mine, 0)
+        full = lax.dynamic_update_index_in_dim(full, value, own, 0)
         for k in range(1, size):
-            full = lax.dynamic_update_index_in_dim(full, swapped(value, k * at), mine ^ k, 0)
-        value = between(full.reshape(size * value.shape[0], value.shape[1]))
-    return value
+            full = lax.dynamic_update_index_in_dim(full, swapped(value, k * at), own ^ k, 0)
+        value = full.reshape(size * value.shape[0], value.shape[1])
+    at, size = runs[0]
+    value = [value] + [swapped(value, k * at) for k in range(1, size)]
+    value = between(jnp.concatenate(value, axis=0))
+    return value, swapped(value, 1), me // at % size, size
 
 
 def local(
@@ -755,7 +827,7 @@
     chunks = chunk_count // steps
     block_atoms = rows // steps
     block_edges = block_atoms * slots
-    vmem = 62 * 1024 * 1024
+    vmem = 63 * 1024 * 1024
     me = lax.axis_index(AXES)
     peers = math.prod(lax.axis_size(a) for a in AXES)
     near_pairs = [(i, i ^ 1) for i in range(peers) if i ^ 1 < peers]
@@ -806,10 +878,9 @@
         name="network",
     )(*edge_args[:2], *net_args)
 
-    grad_rows = 6 * channels + BASES + mid_width // LANES * channels
-    grad_rows += last_width // LANES * mid_width + 16
-    grad_rows = -(-grad_rows // 128) * 128
-    updated, rim_near, own_grad, rim_far, grads = pl.pallas_call(
+    half_rows = max(3 * mid_width + channels + BASES + 16, 7 * channels)
+    half_rows = -(-half_rows // 64) * 64
+    updated, rim_near, own_grad, rim_far, mine, other = pl.pallas_call(
         main_kernel,
         grid=(steps,),
         in_specs=[
@@ -820,15 +891,17 @@
         ],
         out_specs=[
             components, whole((halo, wide)), whole((rows, wide)), whole((halo, wide)),
-            whole((grad_rows, channels)),
+            whole((half_rows, channels)), whole((half_rows, channels)),
         ],
         out_shape=[
             shape_of((9, rows, channels), BF16),
             shape_of((halo, wide), BF16), shape_of((rows, wide), F32),
-            shape_of((halo, wide), BF16), shape_of((grad_rows, channels), BF16),
+            shape_of((halo, wide), BF16),
+            shape_of((half_rows, channels), F32), shape_of((half_rows, channels), BF16),
         ],
         scratch_shapes=[
             pltpu.VMEM((ext + WINDOW, wide), BF16),
+            pltpu.VMEM((ext, 10 * channels), BF16),
             pltpu.VMEM((block_edges, KEPT), BF16),
             pltpu.VMEM((block_edges, KEPT), BF16),
             pltpu.VMEM((block_edges, last_width), F32),
@@ -860,7 +933,7 @@
         return value
 
     def send_rims(value):
-        value, to_near, to_far = lax.optimization_barrier((value, rim_near, rim_far))
+        to_near, to_far = rim_near, rim_far
         kept["near"] = lax.ppermute(to_near, AXES, near_pairs)
         kept["far"] = lax.ppermute(to_far, AXES, far_pairs)
         return value
@@ -875,7 +948,7 @@
         grad_atoms = pl.pallas_call(
             final_kernel,
             out_shape=shape_of((9, rows, channels), F32),
-            compiler_params=pltpu.CompilerParams(vmem_limit_bytes=vmem),
+            compiler_params=pltpu.CompilerParams(vmem_limit_bytes=24 * 1024 * 1024),
             name="final",
         )(
             own_grad, kept["near"], kept["far"], by_component, out_grad_by_component,
@@ -885,22 +958,20 @@
         kept["outs"] = jnp.swapaxes(updated_out, 0, 1), jnp.swapaxes(grad_out, 0, 1)
         return value
 
-    summed = reduce_everywhere(grads, AXES, (nothing, send_rims, have_rims, finish))
+    send_rims(mine)
+    summed, partner, place, shares = reduce_everywhere(mine, other, AXES, (nothing, nothing, nothing, have_rims, finish))
     square_shape = (channels, channels)
-    shapes = [square_shape] * 6 + [w_rad1.shape, (1, channels), w_rad2.shape, (1, mid_width)]
-    shapes += [w_rad3.shape, (1, last_width)]
+    shapes = [square_shape] * 6 + [w_rad1.shape, (channels,), w_rad2.shape, (mid_width,)]
+    shapes += [w_rad3.shape, (last_width,)]
     out = pl.pallas_call(
-        unpack_kernel,
+        functools.partial(unpack_kernel, shares),
+        in_specs=[smem, whole(summed.shape), whole(partner.shape)],
         out_shape=[shape_of(shape, F32) for shape in shapes],
         compiler_params=pltpu.CompilerParams(vmem_limit_bytes=16 * 1024 * 1024),
+        scratch_shapes=[pltpu.VMEM(summed.shape, F32)] * 2,
         name="unpack",
-    )(summed)
-    return (
-        *kept["outs"],
-        *out[:3],
-        *(v if n % 2 == 0 else v[0] for n, v in enumerate(out[6:])),
-        *out[3:6],
-    )
+    )(jnp.stack([me % 2, place]), summed, partner)
+    return (*kept["outs"], *out[:3], *out[6:], *out[3:6])
 
 
 def solution(mesh):

time: 136 us -> 131 us (0.963)
  waiting for transfers between devices: 16.3 us -> 13.4 us
  starting transfers between devices: 24.3 us -> 22.1 us
    ppermute x11, starting transfers between devices: 20.8 us -> 15.7 us  [swapped(): return lax.ppermute(v, axes, [(i, i ^ by) for i in range(peers)])]
    ppermute x11, waiting for transfers between devices: 16.3 us -> 13.4 us  [swapped(): return lax.ppermute(v, axes, [(i, i ^ by) for i in range(peers)])]
    unnamed x8 -> x14, local copies, waits for them, and re-layouts: 1.01 us -> 3.14 us
    ppermute x1, starting transfers between devices: 1.64 us -> 3.64 us  [send_rims(): kept['near'] = lax.ppermute(to_near, AXES, near_pairs)]
    pallas_call x1, Pallas kernels: 3.93 us -> 1.96 us  [finish(): pl.pallas_call(final_kernel, out_shape=shape_of((9, rows, channels), F32)...]
  transfers between devices with their start and end apart: 15 -> 15, of which waited for: 7 -> 7; matrix products, arithmetic and copies ran while one was open for 3% -> 4% of each run, Pallas kernels for 9% -> 8%
where the time goes in v4:
time: 131 us; the launch traced here: 130 us
  Pallas kernels  85.7 us (65%)
  starting transfers between devices  22.1 us (17%)
  waiting for transfers between devices  13.4 us (10%)
  other arithmetic  4.35 us (3%)
  local copies, waits for them, and re-layouts  4.04 us (3%)
    pallas_call x1, Pallas kernels, local(): pl.pallas_call(main_kernel, grid=(steps,), in_specs=[smem, whole(near.sha...  73.4 us
    ppermute x11, starting transfers between devices, swapped(): return lax.ppermute(v, axes, [(i, i ^ by) for i in range(peers)])  15.7 us
    ppermute x11, waiting for transfers between devices, swapped(): return lax.ppermute(v, axes, [(i, i ^ by) for i in range(peers)])  13.4 us
    pallas_call x1, Pallas kernels, local(): pl.pallas_call(network_kernel, grid=(AHEAD,), in_specs=edge_specs[:2] + n...  8.8 us
    ppermute x1, starting transfers between devices, send_rims(): kept['near'] = lax.ppermute(to_near, AXES, near_pairs)  3.64 us
    unnamed x14, local copies, waits for them, and re-layouts  3.14 us
  transfers between devices with their start and end apart: 15, of which 7 were waited for; matrix products, arithmetic and copies ran while one was open for 4% of the time, Pallas kernels for 8%

profile of v4, /device:TPU:0, one launch (start us, length us, event | category | flops | bytes accessed | tf_op | source)
XLA Modules:
  0.0 130.4 jit_solution(11677329979795663968)
XLA Ops:
  0.6 0.5 collective-permute-start
  1.2 1.5 %collective-permute-start.1 = (bf16[9,256,128]{2,1,0:T(8,128)(2,1)}, bf16[9,256,128]{2,1,0:T(8,128)(2,1)}, u32[]{:S(2)}, u32[]{:S(2)}) collective-permute-start(bf16[9,256,128]{2,1,0:T(8,128)(2,1)} %bitcast.32), channel_id=1, source_target_pairs={{1,2},{2,1},{3,4},{4,3},{5,6},{6,5},{7,8},{8,7},{9,10},{10,9},{11,... | collective-permute-start | bytes 1769480 | tf_op jit(solution)/shard_map/ppermute | solution.py:839
  2.7 1.5 %subtract_reduce_fusion.1 = (s32[256]{0:T(256)S(1)}, s32[256]{0:T(256)S(1)}, s32[64,256]{1,0:T(8,128)}) fusion(s32[256,64]{0,1:T(8,128)} %param.18, s32[]{:T(128)S(6)} %sub.23), kind=kLoop, calls=%fused_computation.15 | loop fusion | flops 48640 | bytes 133124 | tf_op jit(solution)/shard_map/reduce_min | solution.py:845
  4.1 0.1 reshape.49
  4.2 0.1 reshape.51
  4.3 0.1 reduce_min.19
  4.4 0.1 reduce_max.19
  4.7 0.7 copy.35.win_ref
  5.4 1.3 maximum_bitcast_fusion.bias_ref
  6.7 8.8 %network.1 = (bf16[3072,1152]{1,0:T(8,128)(2,1)}, f32[3072,384]{1,0:T(8,128)}, bf16[1536,128]{1,0:T(8,128)(2,1)}) custom-call(f32[64,256]{1,0:T(8,128)} %bitcast.40, s32[64,256]{1,0:T(8,128)} %bitcast.42, bf16[32,128]{1,0:T(8,128)(2,1)} %w1_raw.3, bf16[128,256]{1,0:T(8,128)(2,1)} %w2_raw.3, bf16[256,384]{1,0:T(8,128)(2,1)} %w3_raw.3, ...), custom_call_target="tpu_custom_call" | custom-call | flops 1107296256 | bytes 9437184 | tf_op jit(solution)/shard_map/network/pallas_call | solution.py:862
  15.5 0.8 copy-done.6
  16.3 73.4 %main.1 = (bf16[9,256,128]{2,1,0:T(8,128)(2,1)}, bf16[256,1152]{1,0:T(8,128)(2,1)}, f32[256,1152]{1,0:T(8,128)}, bf16[256,1152]{1,0:T(8,128)(2,1)}, f32[960,128]{1,0:T(8,128)}, /*index=5*/bf16[960,128]{1,0:T(8,128)(2,1)}) custom-call(s32[33,2]{1,0:T(8,128)} %copy.35.win_ref, bf16[9,256,128]{2,1,0:T(8,128)(2,1)} %copy-done.6, bf16[9,256,128]{2,1,0:T(8,128)(2,1)} %bitcast.33, ...), custom_call_target="tpu_custom_call" | custom-call | tf_op jit(solution)/shard_map/main/pallas_call | solution.py:883
  89.7 3.1 %collective-permute-start.2 = (bf16[960,128]{1,0:T(8,128)(2,1)}, bf16[960,128]{1,0:T(8,128)(2,1)S(1)}, u32[]{:S(2)}, u32[]{:S(2)}) collective-permute-start(bf16[960,128]{1,0:T(8,128)(2,1)} %get-tuple-element.45), channel_id=1, source_target_pairs={{0,1},{1,0},{2,3},{3,2},{4,5},{5,4},{6,7},{7,6},{8,9},{9,8},{10,11... | collective-permute-start | bytes 737288 | tf_op jit(solution)/shard_map/ppermute | solution.py:783
  92.8 0.7 collective-permute-start.10
  93.5 3.6 %collective-permute-start.9 = (bf16[256,1152]{1,0:T(8,128)(2,1)}, bf16[256,1152]{1,0:T(8,128)(2,1)S(1)}, u32[]{:S(2)}, u32[]{:S(2)}) collective-permute-start(bf16[256,1152]{1,0:T(8,128)(2,1)} %get-tuple-element.46), channel_id=1, source_target_pairs={{0,1},{1,0},{2,3},{3,2},{4,5},{5,4},{6,7},{7,6},{8,9},{9,8},{10,11... | collective-permute-start | bytes 1769480 | tf_op jit(solution)/shard_map/ppermute | solution.py:937
  97.1 1.1 convert_add_fusion
  98.2 1.5 %collective-permute-start.3 = (bf16[240,128]{1,0:T(8,128)(2,1)S(1)}, bf16[240,128]{1,0:T(8,128)(2,1)S(1)}, u32[]{:S(2)}, u32[]{:S(2)}) collective-permute-start(bf16[240,128]{1,0:T(8,128)(2,1)S(1)} %get-tuple-element.70), channel_id=1, source_target_pairs={{0,8},{1,9},{2,10},{3,11},{4,12},{5,13},{6,14},{7,15},{8,0},{9,1},... | collective-permute-start | bytes 184328 | tf_op jit(solution)/shard_map/ppermute | solution.py:783
  99.7 3.1 %collective-permute-start.4 = (bf16[240,128]{1,0:T(8,128)(2,1)S(1)}, bf16[240,128]{1,0:T(8,128)(2,1)S(1)}, u32[]{:S(2)}, u32[]{:S(2)}) collective-permute-start(bf16[240,128]{1,0:T(8,128)(2,1)S(1)} %get-tuple-element.72), channel_id=1, source_target_pairs={{0,16},{1,17},{2,18},{3,19},{4,20},{5,21},{6,22},{7,23},{8,24},{9,... | collective-permute-start | bytes 184328 | tf_op jit(solution)/shard_map/ppermute | solution.py:783
  102.8 5.7 %collective-permute-done.3 = bf16[240,128]{1,0:T(8,128)(2,1)S(1)} collective-permute-done((bf16[240,128]{1,0:T(8,128)(2,1)S(1)}, bf16[240,128]{1,0:T(8,128)(2,1)S(1)}, u32[]{:S(2)}, u32[]{:S(2)}) %collective-permute-start.3) | collective-permute-done | bytes 61472 | tf_op jit(solution)/shard_map/ppermute | solution.py:783
  108.4 2.5 %collective-permute-done.4 = bf16[240,128]{1,0:T(8,128)(2,1)S(1)} collective-permute-done((bf16[240,128]{1,0:T(8,128)(2,1)S(1)}, bf16[240,128]{1,0:T(8,128)(2,1)S(1)}, u32[]{:S(2)}, u32[]{:S(2)}) %collective-permute-start.4) | collective-permute-done | bytes 61472 | tf_op jit(solution)/shard_map/ppermute | solution.py:783
  110.9 1.6 %collective-permute-done.5 = bf16[240,128]{1,0:T(8,128)(2,1)S(1)} collective-permute-done((bf16[240,128]{1,0:T(8,128)(2,1)S(1)}, bf16[240,128]{1,0:T(8,128)(2,1)S(1)}, u32[]{:S(2)}, u32[]{:S(2)}) %collective-permute-start.5) | collective-permute-done | bytes 61472 | tf_op jit(solution)/shard_map/ppermute | solution.py:783
  112.7 3.4 %collective-permute-start.8 = (bf16[240,128]{1,0:T(8,128)(2,1)S(1)}, bf16[240,128]{1,0:T(8,128)(2,1)S(1)}, u32[]{:S(2)}, u32[]{:S(2)}) collective-permute-start(bf16[240,128]{1,0:T(8,128)(2,1)S(1)} %fusion.2), channel_id=1, source_target_pairs={{0,6},{1,7},{2,4},{3,5},{4,2},{5,3},{6,0},{7,1},{8,14},{9,15},{10,... | collective-permute-start | bytes 184328 | tf_op jit(solution)/shard_map/ppermute | solution.py:783
  116.1 0.7 collective-permute-done.6
  116.9 0.1 collective-permute-done.7
  117.0 1.4 %collective-permute-done.8 = bf16[240,128]{1,0:T(8,128)(2,1)S(1)} collective-permute-done((bf16[240,128]{1,0:T(8,128)(2,1)S(1)}, bf16[240,128]{1,0:T(8,128)(2,1)S(1)}, u32[]{:S(2)}, u32[]{:S(2)}) %collective-permute-start.8) | collective-permute-done | bytes 61472 | tf_op jit(solution)/shard_map/ppermute | solution.py:783
  118.4 1.0 collective-permute-start.11
  119.4 3.5 %collective-permute-start.13 = (bf16[240,128]{1,0:T(8,128)(2,1)S(1)}, bf16[240,128]{1,0:T(8,128)(2,1)S(1)}, u32[]{:S(2)}, u32[]{:S(2)}) collective-permute-start(bf16[240,128]{1,0:T(8,128)(2,1)S(1)} %add_convert_fusion), channel_id=1, source_target_pairs={{0,24},{1,25},{2,26},{3,27},{4,28},{5,29},{6,30},{7,31},{8,16},{9,... | collective-permute-start | bytes 184328 | tf_op jit(solution)/shard_map/ppermute | solution.py:783
  122.9 1.1 copy-done.1
  123.9 1.3 copy-done.2
  125.2 2.0 %final.1 = f32[9,256,128]{2,1,0:T(8,128)} custom-call(f32[256,1152]{1,0:T(8,128)S(1)} %copy-done.2, bf16[256,1152]{1,0:T(8,128)(2,1)S(1)} %collective-permute-done.9.near_ref, bf16[256,1152]{1,0:T(8,128)(2,1)S(1)} %collective-permute-done.10.far_ref, bf16[9,256,128]{2,1,0:T(8,128)(2,1)S(1)} %bitcast.34, bf16[9,256,128]{2,1,0:T(8,128)(2,1)S(1)} %bitcast.36, ...), custom_call_target="tpu_custom_call" | custom-call | tf_op jit(solution)/shard_map/final/pallas_call | solution.py:948
  127.4 1.4 %collective-permute-done.14.other_ref = bf16[960,128]{1,0:T(8,128)(2,1)S(1)} collective-permute-done((bf16[960,128]{1,0:T(8,128)(2,1)S(1)}, bf16[960,128]{1,0:T(8,128)(2,1)S(1)}, u32[]{:S(2)}, u32[]{:S(2)}) %collective-permute-start.14) | collective-permute-done | bytes 245792 | tf_op jit(solution)/shard_map/ppermute | solution.py:783
  128.8 1.6 %unpack.1 = (f32[128,128]{1,0:T(8,128)}, f32[128,128]{1,0:T(8,128)}, f32[128,128]{1,0:T(8,128)}, f32[128,128]{1,0:T(8,128)}, f32[128,128]{1,0:T(8,128)}, /*index...) custom-call(s32[2]{0:T(128)S(1)} %pad_add_fusion.1.place_ref, ...), custom_call_target="tpu_custom_call" | custom-call | tf_op jit(solution)/shard_map/unpack/pallas_call | solution.py:966
  (32 shorter events, 0.6 us)
Async XLA Ops:
  0.6 14.8 %collective-permute-start = (bf16[9,256,128]{2,1,0:T(8,128)(2,1)}, bf16[9,256,128]{2,1,0:T(8,128)(2,1)S(1)}, u32[]{:S(2)}, u32[]{:S(2)}) collective-permute-start(bf16[9,256,128]{2,1,0:T(8,128)(2,1)} %bitcast.31), channel_id=1, source_target_pairs={{0,1},{1,0},{2,3},{3,2},{4,5},{5,4},{6,7},{7,6},{8,9},{9,8},{10,11... | collective-permute-start | bytes 1769480 | tf_op jit(solution)/shard_map/ppermute | solution.py:838
  1.2 14.3 %collective-permute-start.1 = (bf16[9,256,128]{2,1,0:T(8,128)(2,1)}, bf16[9,256,128]{2,1,0:T(8,128)(2,1)}, u32[]{:S(2)}, u32[]{:S(2)}) collective-permute-start(bf16[9,256,128]{2,1,0:T(8,128)(2,1)} %bitcast.32), channel_id=1, source_target_pairs={{1,2},{2,1},{3,4},{4,3},{5,6},{6,5},{7,8},{8,7},{9,10},{10,9},{11,... | collective-permute-start | bytes 1769480 | tf_op jit(solution)/shard_map/ppermute | solution.py:839
  15.5 0.8 copy-start.6
  16.3 106.6 %copy-start = (bf16[256,9,128]{2,0,1:T(8,128)(2,1)S(1)}, bf16[256,9,128]{2,0,1:T(8,128)(2,1)}, u32[]{:S(2)}) copy-start(bf16[256,9,128]{2,0,1:T(8,128)(2,1)} %param.17) | copy-start | bytes 1769476
  16.3 106.6 %copy-start.3 = (bf16[128,128]{1,0:T(8,128)(2,1)S(1)}, bf16[128,128]{1,0:T(8,128)(2,1)}, u32[]{:S(2)}) copy-start(bf16[128,128]{1,0:T(8,128)(2,1)} %iso1_ref.3) | copy-start | bytes 98308
  16.3 106.6 %copy-start.4 = (bf16[128,128]{1,0:T(8,128)(2,1)S(1)}, bf16[128,128]{1,0:T(8,128)(2,1)}, u32[]{:S(2)}) copy-start(bf16[128,128]{1,0:T(8,128)(2,1)} %anti1_ref.3) | copy-start | bytes 98308
  16.3 106.6 %copy-start.5 = (bf16[128,128]{1,0:T(8,128)(2,1)S(1)}, bf16[128,128]{1,0:T(8,128)(2,1)}, u32[]{:S(2)}) copy-start(bf16[128,128]{1,0:T(8,128)(2,1)} %sym1_ref.3) | copy-start | bytes 98308
  89.7 7.5 %collective-permute-start.2 = (bf16[960,128]{1,0:T(8,128)(2,1)}, bf16[960,128]{1,0:T(8,128)(2,1)S(1)}, u32[]{:S(2)}, u32[]{:S(2)}) collective-permute-start(bf16[960,128]{1,0:T(8,128)(2,1)} %get-tuple-element.45), channel_id=1, source_target_pairs={{0,1},{1,0},{2,3},{3,2},{4,5},{5,4},{6,7},{7,6},{8,9},{9,8},{10,11... | collective-permute-start | bytes 737288 | tf_op jit(solution)/shard_map/ppermute | solution.py:783
  92.8 25.6 %collective-permute-start.10 = (bf16[256,1152]{1,0:T(8,128)(2,1)}, bf16[256,1152]{1,0:T(8,128)(2,1)S(1)}, u32[]{:S(2)}, u32[]{:S(2)}) collective-permute-start(bf16[256,1152]{1,0:T(8,128)(2,1)} %get-tuple-element.47), channel_id=1, source_target_pairs={{1,2},{2,1},{3,4},{4,3},{5,6},{6,5},{7,8},{8,7},{9,10},{10,9},{11,... | collective-permute-start | bytes 1769480 | tf_op jit(solution)/shard_map/ppermute | solution.py:938
  93.5 24.9 %collective-permute-start.9 = (bf16[256,1152]{1,0:T(8,128)(2,1)}, bf16[256,1152]{1,0:T(8,128)(2,1)S(1)}, u32[]{:S(2)}, u32[]{:S(2)}) collective-permute-start(bf16[256,1152]{1,0:T(8,128)(2,1)} %get-tuple-element.46), channel_id=1, source_target_pairs={{0,1},{1,0},{2,3},{3,2},{4,5},{5,4},{6,7},{7,6},{8,9},{9,8},{10,11... | collective-permute-start | bytes 1769480 | tf_op jit(solution)/shard_map/ppermute | solution.py:937
  98.2 10.2 %collective-permute-start.3 = (bf16[240,128]{1,0:T(8,128)(2,1)S(1)}, bf16[240,128]{1,0:T(8,128)(2,1)S(1)}, u32[]{:S(2)}, u32[]{:S(2)}) collective-permute-start(bf16[240,128]{1,0:T(8,128)(2,1)S(1)} %get-tuple-element.70), channel_id=1, source_target_pairs={{0,8},{1,9},{2,10},{3,11},{4,12},{5,13},{6,14},{7,15},{8,0},{9,1},... | collective-permute-start | bytes 184328 | tf_op jit(solution)/shard_map/ppermute | solution.py:783
  99.7 11.2 %collective-permute-start.4 = (bf16[240,128]{1,0:T(8,128)(2,1)S(1)}, bf16[240,128]{1,0:T(8,128)(2,1)S(1)}, u32[]{:S(2)}, u32[]{:S(2)}) collective-permute-start(bf16[240,128]{1,0:T(8,128)(2,1)S(1)} %get-tuple-element.72), channel_id=1, source_target_pairs={{0,16},{1,17},{2,18},{3,19},{4,20},{5,21},{6,22},{7,23},{8,24},{9,... | collective-permute-start | bytes 184328 | tf_op jit(solution)/shard_map/ppermute | solution.py:783
  102.8 9.8 %collective-permute-start.5 = (bf16[240,128]{1,0:T(8,128)(2,1)S(1)}, bf16[240,128]{1,0:T(8,128)(2,1)S(1)}, u32[]{:S(2)}, u32[]{:S(2)}) collective-permute-start(bf16[240,128]{1,0:T(8,128)(2,1)S(1)} %get-tuple-element.71), channel_id=1, source_target_pairs={{0,24},{1,25},{2,26},{3,27},{4,28},{5,29},{6,30},{7,31},{8,16},{9,... | collective-permute-start | bytes 184328 | tf_op jit(solution)/shard_map/ppermute | solution.py:783
  112.6 4.3 %collective-permute-start.6 = (bf16[240,128]{1,0:T(8,128)(2,1)S(1)}, bf16[240,128]{1,0:T(8,128)(2,1)S(1)}, u32[]{:S(2)}, u32[]{:S(2)}) collective-permute-start(bf16[240,128]{1,0:T(8,128)(2,1)S(1)} %fusion.2), channel_id=1, source_target_pairs={{0,2},{1,3},{2,0},{3,1},{4,6},{5,7},{6,4},{7,5},{8,10},{9,11},{10,... | collective-permute-start | bytes 184328 | tf_op jit(solution)/shard_map/ppermute | solution.py:783
  112.7 4.3 %collective-permute-start.7 = (bf16[240,128]{1,0:T(8,128)(2,1)S(1)}, bf16[240,128]{1,0:T(8,128)(2,1)S(1)}, u32[]{:S(2)}, u32[]{:S(2)}) collective-permute-start(bf16[240,128]{1,0:T(8,128)(2,1)S(1)} %fusion.2), channel_id=1, source_target_pairs={{0,4},{1,5},{2,6},{3,7},{4,0},{5,1},{6,2},{7,3},{8,12},{9,13},{10,... | collective-permute-start | bytes 184328 | tf_op jit(solution)/shard_map/ppermute | solution.py:783
  112.7 5.6 %collective-permute-start.8 = (bf16[240,128]{1,0:T(8,128)(2,1)S(1)}, bf16[240,128]{1,0:T(8,128)(2,1)S(1)}, u32[]{:S(2)}, u32[]{:S(2)}) collective-permute-start(bf16[240,128]{1,0:T(8,128)(2,1)S(1)} %fusion.2), channel_id=1, source_target_pairs={{0,6},{1,7},{2,4},{3,5},{4,2},{5,3},{6,0},{7,1},{8,14},{9,15},{10,... | collective-permute-start | bytes 184328 | tf_op jit(solution)/shard_map/ppermute | solution.py:783
  118.4 8.8 %collective-permute-start.11 = (bf16[240,128]{1,0:T(8,128)(2,1)S(1)}, bf16[240,128]{1,0:T(8,128)(2,1)S(1)}, u32[]{:S(2)}, u32[]{:S(2)}) collective-permute-start(bf16[240,128]{1,0:T(8,128)(2,1)S(1)} %add_convert_fusion), channel_id=1, source_target_pairs={{0,8},{1,9},{2,10},{3,11},{4,12},{5,13},{6,14},{7,15},{8,0},{9,1},... | collective-permute-start | bytes 184328 | tf_op jit(solution)/shard_map/ppermute | solution.py:783
  119.4 7.8 %collective-permute-start.12 = (bf16[240,128]{1,0:T(8,128)(2,1)S(1)}, bf16[240,128]{1,0:T(8,128)(2,1)S(1)}, u32[]{:S(2)}, u32[]{:S(2)}) collective-permute-start(bf16[240,128]{1,0:T(8,128)(2,1)S(1)} %add_convert_fusion), channel_id=1, source_target_pairs={{0,16},{1,17},{2,18},{3,19},{4,20},{5,21},{6,22},{7,23},{8,24},{9,... | collective-permute-start | bytes 184328 | tf_op jit(solution)/shard_map/ppermute | solution.py:783
  119.4 7.8 %collective-permute-start.13 = (bf16[240,128]{1,0:T(8,128)(2,1)S(1)}, bf16[240,128]{1,0:T(8,128)(2,1)S(1)}, u32[]{:S(2)}, u32[]{:S(2)}) collective-permute-start(bf16[240,128]{1,0:T(8,128)(2,1)S(1)} %add_convert_fusion), channel_id=1, source_target_pairs={{0,24},{1,25},{2,26},{3,27},{4,28},{5,29},{6,30},{7,31},{8,16},{9,... | collective-permute-start | bytes 184328 | tf_op jit(solution)/shard_map/ppermute | solution.py:783
  122.9 1.1 copy-start.1
  123.9 1.3 copy-start.2
  127.2 1.6 %collective-permute-start.14 = (bf16[960,128]{1,0:T(8,128)(2,1)S(1)}, bf16[960,128]{1,0:T(8,128)(2,1)S(1)}, u32[]{:S(2)}, u32[]{:S(2)}) collective-permute-start(bf16[960,128]{1,0:T(8,128)(2,1)S(1)} %pad_maximum_fusion.mine_ref), channel_id=1, source_target_pairs={{0,1},{1,0},{2,3},{3,2},{4,5},{5,4},{6,7},{7,6},{8,9},{9,8},{10,11... | collective-permute-start | bytes 737288 | tf_op jit(solution)/shard_map/ppermute | solution.py:783

commit v5 on v4

--- a/solution.py
+++ b/solution.py
@@ -13,10 +13,11 @@
 LANES = 128
 GROUP = 8
 BASES = 32
-UNROLL = 2
+UNROLL = 4
 PAIRS = ((0, 1), (2, 3), (4, 5), (6, 7), (8,))
-GATHER = "0k0D0E0A0d0B0a0C0b1k0c1D1E1A1d1B1a1C1b1c"
-SCHEDULE = "".join(n + s for n in "01" for s in "HaTDb0GJ1cWdp2E3eF4xVyUz")
+GATHERED = 8
+GATHER = "kDEAdBaCbc"
+SCHEDULE = "".join(n + s for n in "0123" for s in "HaTDb0GJ1cWdp2E3eF4xVyUz")
 WINDOW = 256
 KIND = (0, 1, 1, 1, 2, 2, 2, 2, 2)
 AXES = ("edge", "grp")
@@ -346,20 +347,22 @@
     def chunk_atoms(index):
         return pl.ds(pl.multiple_of(index * GROUP, GROUP), GROUP)
 
-    def fetches(j):
+    def fetch_factors(j):
+        here = pl.ds(pl.multiple_of(j * edges, edges), edges)
+        return pltpu.make_async_copy(fac_first.at[here], fac_a.at[here], sems.at[j, 0])
+
+    def fetch_rest(j):
         here = pl.ds(pl.multiple_of(j * edges, edges), edges)
         half = pl.ds(pl.multiple_of(j * (edges // 2), edges // 2), edges // 2)
         return (
-            pltpu.make_async_copy(net_first.at[here], net_a.at[here], sems.at[j, 0]),
-            pltpu.make_async_copy(fac_first.at[here], fac_a.at[here], sems.at[j, 1]),
+            pltpu.make_async_copy(net_first.at[here], net_a.at[here], sems.at[j, 1]),
             pltpu.make_async_copy(basis_first.at[half], basis_a.at[half], sems.at[j, 2]),
         )
 
     @pl.when(step == 0)
     def _():
         for j in range(AHEAD):
-            for copy in fetches(j):
-                copy.start()
+            fetch_factors(j).start()
         halve_weights(w1_raw, w2_raw, w3_raw, bias_ref, *radial)
         dist_s[...] = by_atom(dist_ref)
         gate_s[...] = gating(dist_s[...], by_atom(live_ref))
@@ -387,6 +390,12 @@
             mine = chunk_atoms(j)
             Network(dist_s[mine, :], gate_s[mine, :], net_a, fac_a, basis_a, j, radial).run()
 
+    @pl.when(step == 0)
+    def _():
+        for j in range(AHEAD):
+            for copy in fetch_rest(j):
+                copy.start()
+
     class Gather:
         def __init__(self, fac, j, w, more):
             self.j, self.w, self.fac, self.more, self.got = j, w, fac, more, {}
@@ -443,25 +452,24 @@
             "E": lambda g: g.rows_of(8, 9), "a": lambda g: g.pair(0), "b": lambda g: g.pair(1),
             "c": lambda g: g.pair(2), "d": lambda g: g.diagonal(),
         }
-        each = [Gather(fac, j, w, more) for j in places]
-        for which, name in zip(order[::2], order[1::2]):
-            if int(which) < len(each):
-                steps_of[name](each[int(which)])
+        for each in [Gather(fac, j, w, more) for j in places]:
+            for name in order:
+                steps_of[name](each)
 
     even = step % 2 == 0
 
     def collect(fac):
-        @pl.loop(0, chunks // UNROLL)
-        def _(pair):
+        @pl.loop(0, chunks // GATHERED)
+        def _(turn):
+            places = [turn * GATHERED + n for n in range(GATHERED)]
             if fac is fac_a:
-
-                @pl.when(jnp.logical_and(step == 0, pair < AHEAD // UNROLL))
-                def _():
-                    for n in range(UNROLL):
-                        for copy in fetches(pair * UNROLL + n):
-                            copy.wait()
-
-            gather(fac, [pair * UNROLL + n for n in range(UNROLL)], 0, False, GATHER)
+                for j in places:
+
+                    @pl.when(jnp.logical_and(step == 0, j < AHEAD))
+                    def _():
+                        fetch_factors(j).wait()
+
+            gather(fac, places, 0, False, GATHER)
 
         @pl.loop(0, chunks)
         def _(j):
@@ -623,6 +631,15 @@
 
         @pl.loop(0, chunks // UNROLL)
         def _(pair):
+            if now[0] is net_a:
+
+                for n in range(UNROLL):
+
+                    @pl.when(jnp.logical_and(step == 0, pair * UNROLL + n < AHEAD))
+                    def _():
+                        for copy in fetch_rest(pair * UNROLL + n):
+                            copy.wait()
+
             both = [Backward(pair * UNROLL + n, now, after) for n in range(UNROLL)]
             for which, name in zip(SCHEDULE[::2], SCHEDULE[1::2]):
                 if after is not None or not name.islower():

time: 131 us -> 128 us (0.977)
  Pallas kernels: 85.7 us -> 83.1 us
    pallas_call x1, Pallas kernels: 73.4 us -> 70.8 us  [local(): pl.pallas_call(main_kernel, grid=(steps,), in_specs=[smem, whole(near.sha...]
    ppermute x1, starting transfers between devices: 3.64 us -> 5.44 us  [send_rims(): kept['near'] = lax.ppermute(to_near, AXES, near_pairs)]
  transfers between devices with their start and end apart: 15 -> 15, of which waited for: 7 -> 6; matrix products, arithmetic and copies ran while one was open for 4% -> 4% of each run, Pallas kernels for 8% -> 8%
where the time goes in v5:
time: 128 us
  Pallas kernels  83.1 us (65%)
  starting transfers between devices  22.7 us (18%)
  waiting for transfers between devices  12.5 us (10%)
  other arithmetic  4.35 us (3%)
  local copies, waits for them, and re-layouts  4.04 us (3%)
    pallas_call x1, Pallas kernels, local(): pl.pallas_call(main_kernel, grid=(steps,), in_specs=[smem, whole(near.sha...  70.8 us
    ppermute x11, starting transfers between devices, swapped(): return lax.ppermute(v, axes, [(i, i ^ by) for i in range(peers)])  14.5 us
    ppermute x11, waiting for transfers between devices, swapped(): return lax.ppermute(v, axes, [(i, i ^ by) for i in range(peers)])  12.5 us
    pallas_call x1, Pallas kernels, local(): pl.pallas_call(network_kernel, grid=(AHEAD,), in_specs=edge_specs[:2] + n...  8.8 us
    ppermute x1, starting transfers between devices, send_rims(): kept['near'] = lax.ppermute(to_near, AXES, near_pairs)  5.44 us
    unnamed x14, local copies, waits for them, and re-layouts  3.14 us
  transfers between devices with their start and end apart: 15, of which 6 were waited for; matrix products, arithmetic and copies ran while one was open for 4% of the time, Pallas kernels for 8%

profile of v5, /device:TPU:0, one launch (start us, length us, event | category | flops | bytes accessed | tf_op | source)
XLA Modules:
  0.0 127.5 jit_solution(2402856281570688797)
XLA Ops:
  0.6 0.5 collective-permute-start
  1.2 1.5 %collective-permute-start.1 = (bf16[9,256,128]{2,1,0:T(8,128)(2,1)}, bf16[9,256,128]{2,1,0:T(8,128)(2,1)}, u32[]{:S(2)}, u32[]{:S(2)}) collective-permute-start(bf16[9,256,128]{2,1,0:T(8,128)(2,1)} %bitcast.32), channel_id=1, source_target_pairs={{1,2},{2,1},{3,4},{4,3},{5,6},{6,5},{7,8},{8,7},{9,10},{10,9},{11,... | collective-permute-start | bytes 1769480 | tf_op jit(solution)/shard_map/ppermute | solution.py:856
  2.7 1.5 %subtract_reduce_fusion.1 = (s32[256]{0:T(256)S(1)}, s32[256]{0:T(256)S(1)}, s32[64,256]{1,0:T(8,128)}) fusion(s32[256,64]{0,1:T(8,128)} %param.18, s32[]{:T(128)S(6)} %sub.23), kind=kLoop, calls=%fused_computation.15 | loop fusion | flops 48640 | bytes 133124 | tf_op jit(solution)/shard_map/reduce_min | solution.py:862
  4.1 0.1 reshape.49
  4.2 0.1 reshape.51
  4.3 0.1 reduce_min.19
  4.4 0.1 reduce_max.19
  4.7 0.7 copy.35.win_ref
  5.4 1.3 %maximum_bitcast_fusion.bias_ref = bf16[6,128]{1,0:T(8,128)(2,1)} fusion(bf16[384]{0:T(512)(128)(2,1)} %param.29, bf16[256]{0:T(256)(128)(2,1)} %param.27, bf16[128]{0:T(256)(128)(2,1)} %param.25), kind=kLoop, calls=%fused_computation.16 | loop fusion | flops 4608 | bytes 3072 | tf_op jit(solution)/shard_map/reshape | solution.py:867
  6.7 8.8 %network.1 = (bf16[3072,1152]{1,0:T(8,128)(2,1)}, f32[3072,384]{1,0:T(8,128)}, bf16[1536,128]{1,0:T(8,128)(2,1)}) custom-call(f32[64,256]{1,0:T(8,128)} %bitcast.40, s32[64,256]{1,0:T(8,128)} %bitcast.42, bf16[32,128]{1,0:T(8,128)(2,1)} %w1_raw.3, bf16[128,256]{1,0:T(8,128)(2,1)} %w2_raw.3, bf16[256,384]{1,0:T(8,128)(2,1)} %w3_raw.3, ...), custom_call_target="tpu_custom_call" | custom-call | flops 1107296256 | bytes 9437184 | tf_op jit(solution)/shard_map/network/pallas_call | solution.py:879
  15.5 0.8 copy-done.6
  16.3 70.8 %main.1 = (bf16[9,256,128]{2,1,0:T(8,128)(2,1)}, bf16[256,1152]{1,0:T(8,128)(2,1)}, f32[256,1152]{1,0:T(8,128)}, bf16[256,1152]{1,0:T(8,128)(2,1)}, f32[960,128]{1,0:T(8,128)}, /*index=5*/bf16[960,128]{1,0:T(8,128)(2,1)}) custom-call(s32[33,2]{1,0:T(8,128)} %copy.35.win_ref, bf16[9,256,128]{2,1,0:T(8,128)(2,1)} %copy-done.6, bf16[9,256,128]{2,1,0:T(8,128)(2,1)} %bitcast.33, ...), custom_call_target="tpu_custom_call" | custom-call | tf_op jit(solution)/shard_map/main/pallas_call | solution.py:900
  87.1 2.0 %collective-permute-start.2 = (bf16[960,128]{1,0:T(8,128)(2,1)}, bf16[960,128]{1,0:T(8,128)(2,1)S(1)}, u32[]{:S(2)}, u32[]{:S(2)}) collective-permute-start(bf16[960,128]{1,0:T(8,128)(2,1)} %get-tuple-element.45), channel_id=1, source_target_pairs={{0,1},{1,0},{2,3},{3,2},{4,5},{5,4},{6,7},{7,6},{8,9},{9,8},{10,11... | collective-permute-start | bytes 737288 | tf_op jit(solution)/shard_map/ppermute | solution.py:800
  89.1 0.7 collective-permute-start.10
  89.8 5.4 %collective-permute-start.9 = (bf16[256,1152]{1,0:T(8,128)(2,1)}, bf16[256,1152]{1,0:T(8,128)(2,1)S(1)}, u32[]{:S(2)}, u32[]{:S(2)}) collective-permute-start(bf16[256,1152]{1,0:T(8,128)(2,1)} %get-tuple-element.46), channel_id=1, source_target_pairs={{0,1},{1,0},{2,3},{3,2},{4,5},{5,4},{6,7},{7,6},{8,9},{9,8},{10,11... | collective-permute-start | bytes 1769480 | tf_op jit(solution)/shard_map/ppermute | solution.py:954
  95.2 1.1 convert_add_fusion
  96.3 1.5 %collective-permute-start.3 = (bf16[240,128]{1,0:T(8,128)(2,1)S(1)}, bf16[240,128]{1,0:T(8,128)(2,1)S(1)}, u32[]{:S(2)}, u32[]{:S(2)}) collective-permute-start(bf16[240,128]{1,0:T(8,128)(2,1)S(1)} %get-tuple-element.70), channel_id=1, source_target_pairs={{0,8},{1,9},{2,10},{3,11},{4,12},{5,13},{6,14},{7,15},{8,0},{9,1},... | collective-permute-start | bytes 184328 | tf_op jit(solution)/shard_map/ppermute | solution.py:800
  97.8 2.6 %collective-permute-start.4 = (bf16[240,128]{1,0:T(8,128)(2,1)S(1)}, bf16[240,128]{1,0:T(8,128)(2,1)S(1)}, u32[]{:S(2)}, u32[]{:S(2)}) collective-permute-start(bf16[240,128]{1,0:T(8,128)(2,1)S(1)} %get-tuple-element.72), channel_id=1, source_target_pairs={{0,16},{1,17},{2,18},{3,19},{4,20},{5,21},{6,22},{7,23},{8,24},{9,... | collective-permute-start | bytes 184328 | tf_op jit(solution)/shard_map/ppermute | solution.py:800
  100.4 0.4 collective-permute-start.5
  100.8 6.9 %collective-permute-done.3 = bf16[240,128]{1,0:T(8,128)(2,1)S(1)} collective-permute-done((bf16[240,128]{1,0:T(8,128)(2,1)S(1)}, bf16[240,128]{1,0:T(8,128)(2,1)S(1)}, u32[]{:S(2)}, u32[]{:S(2)}) %collective-permute-start.3) | collective-permute-done | bytes 61472 | tf_op jit(solution)/shard_map/ppermute | solution.py:800
  107.7 2.0 %collective-permute-done.5 = bf16[240,128]{1,0:T(8,128)(2,1)S(1)} collective-permute-done((bf16[240,128]{1,0:T(8,128)(2,1)S(1)}, bf16[240,128]{1,0:T(8,128)(2,1)S(1)}, u32[]{:S(2)}, u32[]{:S(2)}) %collective-permute-start.5) | collective-permute-done | bytes 61472 | tf_op jit(solution)/shard_map/ppermute | solution.py:800
  109.9 3.4 %collective-permute-start.8 = (bf16[240,128]{1,0:T(8,128)(2,1)S(1)}, bf16[240,128]{1,0:T(8,128)(2,1)S(1)}, u32[]{:S(2)}, u32[]{:S(2)}) collective-permute-start(bf16[240,128]{1,0:T(8,128)(2,1)S(1)} %fusion.2), channel_id=1, source_target_pairs={{0,6},{1,7},{2,4},{3,5},{4,2},{5,3},{6,0},{7,1},{8,14},{9,15},{10,... | collective-permute-start | bytes 184328 | tf_op jit(solution)/shard_map/ppermute | solution.py:800
  113.2 0.7 collective-permute-done.6
  114.1 1.4 %collective-permute-done.8 = bf16[240,128]{1,0:T(8,128)(2,1)S(1)} collective-permute-done((bf16[240,128]{1,0:T(8,128)(2,1)S(1)}, bf16[240,128]{1,0:T(8,128)(2,1)S(1)}, u32[]{:S(2)}, u32[]{:S(2)}) %collective-permute-start.8) | collective-permute-done | bytes 61472 | tf_op jit(solution)/shard_map/ppermute | solution.py:800
  115.5 0.2 collective-permute-start.11
  115.7 2.5 %collective-permute-start.12 = (bf16[240,128]{1,0:T(8,128)(2,1)S(1)}, bf16[240,128]{1,0:T(8,128)(2,1)S(1)}, u32[]{:S(2)}, u32[]{:S(2)}) collective-permute-start(bf16[240,128]{1,0:T(8,128)(2,1)S(1)} %add_convert_fusion), channel_id=1, source_target_pairs={{0,16},{1,17},{2,18},{3,19},{4,20},{5,21},{6,22},{7,23},{8,24},{9,... | collective-permute-start | bytes 184328 | tf_op jit(solution)/shard_map/ppermute | solution.py:800
  118.1 1.8 %collective-permute-start.13 = (bf16[240,128]{1,0:T(8,128)(2,1)S(1)}, bf16[240,128]{1,0:T(8,128)(2,1)S(1)}, u32[]{:S(2)}, u32[]{:S(2)}) collective-permute-start(bf16[240,128]{1,0:T(8,128)(2,1)S(1)} %add_convert_fusion), channel_id=1, source_target_pairs={{0,24},{1,25},{2,26},{3,27},{4,28},{5,29},{6,30},{7,31},{8,16},{9,... | collective-permute-start | bytes 184328 | tf_op jit(solution)/shard_map/ppermute | solution.py:800
  120.0 1.1 copy-done.1
  121.0 1.3 copy-done.2
  122.3 2.0 %final.1 = f32[9,256,128]{2,1,0:T(8,128)} custom-call(f32[256,1152]{1,0:T(8,128)S(1)} %copy-done.2, bf16[256,1152]{1,0:T(8,128)(2,1)S(1)} %collective-permute-done.9.near_ref, bf16[256,1152]{1,0:T(8,128)(2,1)S(1)} %collective-permute-done.10.far_ref, bf16[9,256,128]{2,1,0:T(8,128)(2,1)S(1)} %bitcast.34, bf16[9,256,128]{2,1,0:T(8,128)(2,1)S(1)} %bitcast.36, ...), custom_call_target="tpu_custom_call" | custom-call | tf_op jit(solution)/shard_map/final/pallas_call | solution.py:965
  124.5 1.4 %collective-permute-done.14.other_ref = bf16[960,128]{1,0:T(8,128)(2,1)S(1)} collective-permute-done((bf16[960,128]{1,0:T(8,128)(2,1)S(1)}, bf16[960,128]{1,0:T(8,128)(2,1)S(1)}, u32[]{:S(2)}, u32[]{:S(2)}) %collective-permute-start.14) | collective-permute-done | bytes 245792 | tf_op jit(solution)/shard_map/ppermute | solution.py:800
  125.9 1.6 %unpack.1 = (f32[128,128]{1,0:T(8,128)}, f32[128,128]{1,0:T(8,128)}, f32[128,128]{1,0:T(8,128)}, f32[128,128]{1,0:T(8,128)}, f32[128,128]{1,0:T(8,128)}, /*index...) custom-call(s32[2]{0:T(128)S(1)} %pad_add_fusion.1.place_ref, ...), custom_call_target="tpu_custom_call" | custom-call | tf_op jit(solution)/shard_map/unpack/pallas_call | solution.py:983
  (32 shorter events, 0.6 us)
Async XLA Ops:
  0.6 14.8 %collective-permute-start = (bf16[9,256,128]{2,1,0:T(8,128)(2,1)}, bf16[9,256,128]{2,1,0:T(8,128)(2,1)S(1)}, u32[]{:S(2)}, u32[]{:S(2)}) collective-permute-start(bf16[9,256,128]{2,1,0:T(8,128)(2,1)} %bitcast.31), channel_id=1, source_target_pairs={{0,1},{1,0},{2,3},{3,2},{4,5},{5,4},{6,7},{7,6},{8,9},{9,8},{10,11... | collective-permute-start | bytes 1769480 | tf_op jit(solution)/shard_map/ppermute | solution.py:855
  1.2 14.3 %collective-permute-start.1 = (bf16[9,256,128]{2,1,0:T(8,128)(2,1)}, bf16[9,256,128]{2,1,0:T(8,128)(2,1)}, u32[]{:S(2)}, u32[]{:S(2)}) collective-permute-start(bf16[9,256,128]{2,1,0:T(8,128)(2,1)} %bitcast.32), channel_id=1, source_target_pairs={{1,2},{2,1},{3,4},{4,3},{5,6},{6,5},{7,8},{8,7},{9,10},{10,9},{11,... | collective-permute-start | bytes 1769480 | tf_op jit(solution)/shard_map/ppermute | solution.py:856
  15.5 0.8 copy-start.6
  16.3 103.7 %copy-start = (bf16[256,9,128]{2,0,1:T(8,128)(2,1)S(1)}, bf16[256,9,128]{2,0,1:T(8,128)(2,1)}, u32[]{:S(2)}) copy-start(bf16[256,9,128]{2,0,1:T(8,128)(2,1)} %param.17) | copy-start | bytes 1769476
  16.3 103.7 %copy-start.3 = (bf16[128,128]{1,0:T(8,128)(2,1)S(1)}, bf16[128,128]{1,0:T(8,128)(2,1)}, u32[]{:S(2)}) copy-start(bf16[128,128]{1,0:T(8,128)(2,1)} %iso1_ref.3) | copy-start | bytes 98308
  16.3 103.7 %copy-start.4 = (bf16[128,128]{1,0:T(8,128)(2,1)S(1)}, bf16[128,128]{1,0:T(8,128)(2,1)}, u32[]{:S(2)}) copy-start(bf16[128,128]{1,0:T(8,128)(2,1)} %anti1_ref.3) | copy-start | bytes 98308
  16.3 103.7 %copy-start.5 = (bf16[128,128]{1,0:T(8,128)(2,1)S(1)}, bf16[128,128]{1,0:T(8,128)(2,1)}, u32[]{:S(2)}) copy-start(bf16[128,128]{1,0:T(8,128)(2,1)} %sym1_ref.3) | copy-start | bytes 98308
  87.1 8.1 %collective-permute-start.2 = (bf16[960,128]{1,0:T(8,128)(2,1)}, bf16[960,128]{1,0:T(8,128)(2,1)S(1)}, u32[]{:S(2)}, u32[]{:S(2)}) collective-permute-start(bf16[960,128]{1,0:T(8,128)(2,1)} %get-tuple-element.45), channel_id=1, source_target_pairs={{0,1},{1,0},{2,3},{3,2},{4,5},{5,4},{6,7},{7,6},{8,9},{9,8},{10,11... | collective-permute-start | bytes 737288 | tf_op jit(solution)/shard_map/ppermute | solution.py:800
  89.1 26.4 %collective-permute-start.10 = (bf16[256,1152]{1,0:T(8,128)(2,1)}, bf16[256,1152]{1,0:T(8,128)(2,1)S(1)}, u32[]{:S(2)}, u32[]{:S(2)}) collective-permute-start(bf16[256,1152]{1,0:T(8,128)(2,1)} %get-tuple-element.47), channel_id=1, source_target_pairs={{1,2},{2,1},{3,4},{4,3},{5,6},{6,5},{7,8},{8,7},{9,10},{10,9},{11,... | collective-permute-start | bytes 1769480 | tf_op jit(solution)/shard_map/ppermute | solution.py:955
  89.8 25.7 %collective-permute-start.9 = (bf16[256,1152]{1,0:T(8,128)(2,1)}, bf16[256,1152]{1,0:T(8,128)(2,1)S(1)}, u32[]{:S(2)}, u32[]{:S(2)}) collective-permute-start(bf16[256,1152]{1,0:T(8,128)(2,1)} %get-tuple-element.46), channel_id=1, source_target_pairs={{0,1},{1,0},{2,3},{3,2},{4,5},{5,4},{6,7},{7,6},{8,9},{9,8},{10,11... | collective-permute-start | bytes 1769480 | tf_op jit(solution)/shard_map/ppermute | solution.py:954
  96.3 11.3 %collective-permute-start.3 = (bf16[240,128]{1,0:T(8,128)(2,1)S(1)}, bf16[240,128]{1,0:T(8,128)(2,1)S(1)}, u32[]{:S(2)}, u32[]{:S(2)}) collective-permute-start(bf16[240,128]{1,0:T(8,128)(2,1)S(1)} %get-tuple-element.70), channel_id=1, source_target_pairs={{0,8},{1,9},{2,10},{3,11},{4,12},{5,13},{6,14},{7,15},{8,0},{9,1},... | collective-permute-start | bytes 184328 | tf_op jit(solution)/shard_map/ppermute | solution.py:800
  97.8 9.8 %collective-permute-start.4 = (bf16[240,128]{1,0:T(8,128)(2,1)S(1)}, bf16[240,128]{1,0:T(8,128)(2,1)S(1)}, u32[]{:S(2)}, u32[]{:S(2)}) collective-permute-start(bf16[240,128]{1,0:T(8,128)(2,1)S(1)} %get-tuple-element.72), channel_id=1, source_target_pairs={{0,16},{1,17},{2,18},{3,19},{4,20},{5,21},{6,22},{7,23},{8,24},{9,... | collective-permute-start | bytes 184328 | tf_op jit(solution)/shard_map/ppermute | solution.py:800
  100.4 9.3 %collective-permute-start.5 = (bf16[240,128]{1,0:T(8,128)(2,1)S(1)}, bf16[240,128]{1,0:T(8,128)(2,1)S(1)}, u32[]{:S(2)}, u32[]{:S(2)}) collective-permute-start(bf16[240,128]{1,0:T(8,128)(2,1)S(1)} %get-tuple-element.71), channel_id=1, source_target_pairs={{0,24},{1,25},{2,26},{3,27},{4,28},{5,29},{6,30},{7,31},{8,16},{9,... | collective-permute-start | bytes 184328 | tf_op jit(solution)/shard_map/ppermute | solution.py:800
  109.7 4.3 %collective-permute-start.6 = (bf16[240,128]{1,0:T(8,128)(2,1)S(1)}, bf16[240,128]{1,0:T(8,128)(2,1)S(1)}, u32[]{:S(2)}, u32[]{:S(2)}) collective-permute-start(bf16[240,128]{1,0:T(8,128)(2,1)S(1)} %fusion.2), channel_id=1, source_target_pairs={{0,2},{1,3},{2,0},{3,1},{4,6},{5,7},{6,4},{7,5},{8,10},{9,11},{10,... | collective-permute-start | bytes 184328 | tf_op jit(solution)/shard_map/ppermute | solution.py:800
  109.8 4.3 %collective-permute-start.7 = (bf16[240,128]{1,0:T(8,128)(2,1)S(1)}, bf16[240,128]{1,0:T(8,128)(2,1)S(1)}, u32[]{:S(2)}, u32[]{:S(2)}) collective-permute-start(bf16[240,128]{1,0:T(8,128)(2,1)S(1)} %fusion.2), channel_id=1, source_target_pairs={{0,4},{1,5},{2,6},{3,7},{4,0},{5,1},{6,2},{7,3},{8,12},{9,13},{10,... | collective-permute-start | bytes 184328 | tf_op jit(solution)/shard_map/ppermute | solution.py:800
  109.9 5.6 %collective-permute-start.8 = (bf16[240,128]{1,0:T(8,128)(2,1)S(1)}, bf16[240,128]{1,0:T(8,128)(2,1)S(1)}, u32[]{:S(2)}, u32[]{:S(2)}) collective-permute-start(bf16[240,128]{1,0:T(8,128)(2,1)S(1)} %fusion.2), channel_id=1, source_target_pairs={{0,6},{1,7},{2,4},{3,5},{4,2},{5,3},{6,0},{7,1},{8,14},{9,15},{10,... | collective-permute-start | bytes 184328 | tf_op jit(solution)/shard_map/ppermute | solution.py:800
  115.5 8.8 %collective-permute-start.11 = (bf16[240,128]{1,0:T(8,128)(2,1)S(1)}, bf16[240,128]{1,0:T(8,128)(2,1)S(1)}, u32[]{:S(2)}, u32[]{:S(2)}) collective-permute-start(bf16[240,128]{1,0:T(8,128)(2,1)S(1)} %add_convert_fusion), channel_id=1, source_target_pairs={{0,8},{1,9},{2,10},{3,11},{4,12},{5,13},{6,14},{7,15},{8,0},{9,1},... | collective-permute-start | bytes 184328 | tf_op jit(solution)/shard_map/ppermute | solution.py:800
  115.7 8.6 %collective-permute-start.12 = (bf16[240,128]{1,0:T(8,128)(2,1)S(1)}, bf16[240,128]{1,0:T(8,128)(2,1)S(1)}, u32[]{:S(2)}, u32[]{:S(2)}) collective-permute-start(bf16[240,128]{1,0:T(8,128)(2,1)S(1)} %add_convert_fusion), channel_id=1, source_target_pairs={{0,16},{1,17},{2,18},{3,19},{4,20},{5,21},{6,22},{7,23},{8,24},{9,... | collective-permute-start | bytes 184328 | tf_op jit(solution)/shard_map/ppermute | solution.py:800
  118.1 6.1 %collective-permute-start.13 = (bf16[240,128]{1,0:T(8,128)(2,1)S(1)}, bf16[240,128]{1,0:T(8,128)(2,1)S(1)}, u32[]{:S(2)}, u32[]{:S(2)}) collective-permute-start(bf16[240,128]{1,0:T(8,128)(2,1)S(1)} %add_convert_fusion), channel_id=1, source_target_pairs={{0,24},{1,25},{2,26},{3,27},{4,28},{5,29},{6,30},{7,31},{8,16},{9,... | collective-permute-start | bytes 184328 | tf_op jit(solution)/shard_map/ppermute | solution.py:800
  120.0 1.1 copy-start.1
  121.0 1.3 copy-start.2
  124.3 1.6 %collective-permute-start.14 = (bf16[960,128]{1,0:T(8,128)(2,1)S(1)}, bf16[960,128]{1,0:T(8,128)(2,1)S(1)}, u32[]{:S(2)}, u32[]{:S(2)}) collective-permute-start(bf16[960,128]{1,0:T(8,128)(2,1)S(1)} %pad_maximum_fusion.mine_ref), channel_id=1, source_target_pairs={{0,1},{1,0},{2,3},{3,2},{4,5},{5,4},{6,7},{7,6},{8,9},{9,8},{10,11... | collective-permute-start | bytes 737288 | tf_op jit(solution)/shard_map/ppermute | solution.py:800

commit v6 on v5

--- a/solution.py
+++ b/solution.py
@@ -267,8 +267,8 @@
         self.out[self.here, col(kind)] = (slope * (0.5 * self.gate)).astype(BF16)
 
 
-def halve_weights(w1_ref, w2_ref, w3_ref, bias_ref, w1_s, w2_s, w3_s, b3_s):
-    half = 0.5 * bias_ref[...].astype(F32)
+def halve_weights(w1_ref, w2_ref, w3_ref, b1_ref, b2_ref, b3_ref, w1_s, w2_s, w3_s, b3_s):
+    half = [0.5 * ref[...].astype(F32).reshape(1, -1) for ref in (b1_ref, b2_ref, b3_ref)]
 
     def biased(weights, bias, rows):
         below = lax.broadcasted_iota(jnp.int32, (rows - weights.shape[0], bias.shape[1]), 0)
@@ -276,13 +276,12 @@
         return jnp.concatenate([0.5 * weights.astype(F32), bias], axis=0).astype(BF16)
 
     w1_s[...] = jnp.zeros_like(w1_s)
-    first = biased(w1_ref[...], half[0:1], HALF)
+    first = biased(w1_ref[...], half[0], HALF)
     w1_s[:HALF, :LANES] = first
     w1_s[HALF:, LANES:] = first
-    wide2 = jnp.concatenate([half[1:2], half[2:3]], axis=1)
-    w2_s[...] = biased(w2_ref[...], wide2, w2_s.shape[0])
+    w2_s[...] = biased(w2_ref[...], half[1], w2_s.shape[0])
     w3_s[...] = (0.5 * w3_ref[...].astype(F32)).astype(BF16)
-    b3_s[...] = jnp.concatenate([half[3:4], half[4:5], half[5:6]], axis=1)
+    b3_s[...] = half[2]
 
 
 def by_atom(ref):
@@ -294,14 +293,14 @@
 
 
 def network_kernel(
-    dist_ref, live_ref, w1_raw, w2_raw, w3_raw, bias_ref, out_ref, fac_ref, basis_ref, dist_s, gate_s, w1_s, w2_s,
+    dist_ref, live_ref, w1_raw, w2_raw, w3_raw, b1_raw, b2_raw, b3_raw, out_ref, fac_ref, basis_ref, dist_s, gate_s, w1_s, w2_s,
     w3_s, b3_s,
 ):
     net_refs = (w1_s, w2_s, w3_s, b3_s)
 
     @pl.when(pl.program_id(0) == 0)
     def _():
-        halve_weights(w1_raw, w2_raw, w3_raw, bias_ref, *net_refs)
+        halve_weights(w1_raw, w2_raw, w3_raw, b1_raw, b2_raw, b3_raw, *net_refs)
         dist_s[...] = by_atom(dist_ref)
         gate_s[...] = gating(dist_s[...], by_atom(live_ref))
 
@@ -322,7 +321,7 @@
 
 def main_kernel(
     win_ref, near_ref, own_ref, far_ref, outgrad_ref, dist_ref, live_ref, link_ref,
-    w1_raw, w2_raw, w3_raw, bias_ref,
+    w1_raw, w2_raw, w3_raw, b1_raw, b2_raw, b3_raw,
     iso1_ref, anti1_ref, sym1_ref, iso2_ref, anti2_ref, sym2_ref, net_first, fac_first, basis_first,
     upd_ref, rim_near_ref, own_out_ref, rim_far_ref, mine_ref, other_ref,
     table, parts_s, net_a, net_b, fac_a, fac_b, basis_a, basis_b, x_s, msg_s, gm_s, spread,
@@ -363,7 +362,7 @@
     def _():
         for j in range(AHEAD):
             fetch_factors(j).start()
-        halve_weights(w1_raw, w2_raw, w3_raw, bias_ref, *radial)
+        halve_weights(w1_raw, w2_raw, w3_raw, b1_raw, b2_raw, b3_raw, *radial)
         dist_s[...] = by_atom(dist_ref)
         gate_s[...] = gating(dist_s[...], by_atom(live_ref))
         link_s[...] = by_atom(link_ref)
@@ -385,7 +384,7 @@
         dw2_ref[...] = jnp.zeros_like(dw2_ref)
         spread[...] = jnp.zeros_like(spread)
 
-        @pl.loop(AHEAD, chunks)
+        @pl.loop(AHEAD, chunks, unroll=2)
         def _(j):
             mine = chunk_atoms(j)
             Network(dist_s[mine, :], gate_s[mine, :], net_a, fac_a, basis_a, j, radial).run()
@@ -864,12 +863,11 @@
     count = (last - first) // WINDOW + 1
     windows = jnp.stack([jnp.append(first, me % 2), jnp.append(count, 0)], axis=1)
 
-    biases = jnp.concatenate([b_rad1, b_rad2, b_rad3]).reshape(-1, LANES)
     mid_width, last_width = w_rad2.shape[1], w_rad3.shape[1]
     small = whole((channels, channels))
     components = pl.BlockSpec((9, block_atoms, channels), lambda i: (0, i, 0))
     smem = pl.BlockSpec(memory_space=pltpu.SMEM)
-    net_args = (w_rad1, w_rad2, w_rad3, biases)
+    net_args = (w_rad1, w_rad2, w_rad3, b_rad1, b_rad2, b_rad3)
     net_specs = [whole(v.shape) for v in net_args]
     net_scratch = [
         pltpu.VMEM((LANES, 2 * channels), BF16),

time: 128 us -> 129 us (level)
  starting transfers between devices: 22.7 us -> 26.8 us
  Pallas kernels: 83.1 us -> 81.5 us
    ppermute x11, starting transfers between devices: 14.5 us -> 17.7 us  [swapped(): return lax.ppermute(v, axes, [(i, i ^ by) for i in range(peers)])]
    pallas_call x1, Pallas kernels: 70.8 us -> 69.1 us  [local(): pl.pallas_call(main_kernel, grid=(steps,), in_specs=[smem, whole(near.sha...]
  transfers between devices with their start and end apart: 15 -> 15, of which waited for: 6 -> 7; matrix products, arithmetic and copies ran while one was open for 4% -> 3% of each run, Pallas kernels for 8% -> 8%
where the time goes in v6:
time: 129 us
  Pallas kernels  81.5 us (63%)
  starting transfers between devices  26.8 us (21%)
  waiting for transfers between devices  12.6 us (10%)
  local copies, waits for them, and re-layouts  4.04 us (3%)
  other arithmetic  3.06 us (2%)
    pallas_call x1, Pallas kernels, local(): pl.pallas_call(main_kernel, grid=(steps,), in_specs=[smem, whole(near.sha...  69.1 us
    ppermute x11, starting transfers between devices, swapped(): return lax.ppermute(v, axes, [(i, i ^ by) for i in range(peers)])  17.7 us
    ppermute x11, waiting for transfers between devices, swapped(): return lax.ppermute(v, axes, [(i, i ^ by) for i in range(peers)])  12.6 us
    pallas_call x1, Pallas kernels, local(): pl.pallas_call(network_kernel, grid=(AHEAD,), in_specs=edge_specs[:2] + n...  8.83 us
    ppermute x1, starting transfers between devices, send_rims(): kept['near'] = lax.ppermute(to_near, AXES, near_pairs)  6.47 us
    unnamed x14, local copies, waits for them, and re-layouts  3.14 us
  transfers between devices with their start and end apart: 15, of which 7 were waited for; matrix products, arithmetic and copies ran while one was open for 3% of the time, Pallas kernels for 8%

profile of v6, /device:TPU:0, one launch (start us, length us, event | category | flops | bytes accessed | tf_op | source)
XLA Modules:
  0.0 128.8 jit_solution(7576326435488590969)
XLA Ops:
  0.6 0.5 collective-permute-start
  1.2 1.5 %collective-permute-start.1 = (bf16[9,256,128]{2,1,0:T(8,128)(2,1)}, bf16[9,256,128]{2,1,0:T(8,128)(2,1)}, u32[]{:S(2)}, u32[]{:S(2)}) collective-permute-start(bf16[9,256,128]{2,1,0:T(8,128)(2,1)} %bitcast.30), channel_id=1, source_target_pairs={{1,2},{2,1},{3,4},{4,3},{5,6},{6,5},{7,8},{8,7},{9,10},{10,9},{11,... | collective-permute-start | bytes 1769480 | tf_op jit(solution)/shard_map/ppermute | solution.py:855
  2.7 1.5 %subtract_reduce_fusion.1 = (s32[256]{0:T(256)S(1)}, s32[256]{0:T(256)S(1)}, s32[64,256]{1,0:T(8,128)}) fusion(s32[256,64]{0,1:T(8,128)} %param.18, s32[]{:T(128)S(6)} %sub.23), kind=kLoop, calls=%fused_computation.15 | loop fusion | flops 48640 | bytes 133124 | tf_op jit(solution)/shard_map/reduce_min | solution.py:861
  4.1 0.1 reshape.46
  4.2 0.1 reshape.48
  4.3 0.1 reduce_min.19
  4.4 0.1 reduce_max.19
  4.7 0.7 copy.35.win_ref
  5.4 8.8 %network.1 = (bf16[3072,1152]{1,0:T(8,128)(2,1)}, f32[3072,384]{1,0:T(8,128)}, bf16[1536,128]{1,0:T(8,128)(2,1)}) custom-call(f32[64,256]{1,0:T(8,128)} %bitcast.38, s32[64,256]{1,0:T(8,128)} %bitcast.40, bf16[32,128]{1,0:T(8,128)(2,1)} %w1_raw.3, bf16[128,256]{1,0:T(8,128)(2,1)} %w2_raw.3, bf16[256,384]{1,0:T(8,128)(2,1)} %w3_raw.3, bf16[128]{0:T(256)(128)(2,1)} %b1_raw.3, ...), custom_call_target="tpu_custom_call" | custom-call | flops 1107296256 | bytes 9437184 | tf_op jit(solution)/shard_map/network/pallas_call | solution.py:877
  14.2 0.8 copy-done.6
  15.0 69.1 %main.1 = (bf16[9,256,128]{2,1,0:T(8,128)(2,1)}, bf16[256,1152]{1,0:T(8,128)(2,1)}, f32[256,1152]{1,0:T(8,128)}, bf16[256,1152]{1,0:T(8,128)(2,1)}, f32[960,128]{1,0:T(8,128)}, /*index=5*/bf16[960,128]{1,0:T(8,128)(2,1)}) custom-call(s32[33,2]{1,0:T(8,128)} %copy.35.win_ref, bf16[9,256,128]{2,1,0:T(8,128)(2,1)} %copy-done.6, bf16[9,256,128]{2,1,0:T(8,128)(2,1)} %bitcast.31, ...), custom_call_target="tpu_custom_call" | custom-call | tf_op jit(solution)/shard_map/main/pallas_call | solution.py:898
  84.1 5.1 %collective-permute-start.2 = (bf16[960,128]{1,0:T(8,128)(2,1)}, bf16[960,128]{1,0:T(8,128)(2,1)S(1)}, u32[]{:S(2)}, u32[]{:S(2)}) collective-permute-start(bf16[960,128]{1,0:T(8,128)(2,1)} %get-tuple-element.45), channel_id=1, source_target_pairs={{0,1},{1,0},{2,3},{3,2},{4,5},{5,4},{6,7},{7,6},{8,9},{9,8},{10,11... | collective-permute-start | bytes 737288 | tf_op jit(solution)/shard_map/ppermute | solution.py:799
  89.3 0.7 collective-permute-start.10
  90.0 6.5 %collective-permute-start.9 = (bf16[256,1152]{1,0:T(8,128)(2,1)}, bf16[256,1152]{1,0:T(8,128)(2,1)S(1)}, u32[]{:S(2)}, u32[]{:S(2)}) collective-permute-start(bf16[256,1152]{1,0:T(8,128)(2,1)} %get-tuple-element.46), channel_id=1, source_target_pairs={{0,1},{1,0},{2,3},{3,2},{4,5},{5,4},{6,7},{7,6},{8,9},{9,8},{10,11... | collective-permute-start | bytes 1769480 | tf_op jit(solution)/shard_map/ppermute | solution.py:952
  96.5 1.1 convert_add_fusion
  97.6 1.0 collective-permute-start.3
  98.6 2.2 %collective-permute-start.4 = (bf16[240,128]{1,0:T(8,128)(2,1)S(1)}, bf16[240,128]{1,0:T(8,128)(2,1)S(1)}, u32[]{:S(2)}, u32[]{:S(2)}) collective-permute-start(bf16[240,128]{1,0:T(8,128)(2,1)S(1)} %get-tuple-element.72), channel_id=1, source_target_pairs={{0,16},{1,17},{2,18},{3,19},{4,20},{5,21},{6,22},{7,23},{8,24},{9,... | collective-permute-start | bytes 184328 | tf_op jit(solution)/shard_map/ppermute | solution.py:799
  100.8 1.2 collective-permute-start.5
  102.0 5.0 %collective-permute-done.3 = bf16[240,128]{1,0:T(8,128)(2,1)S(1)} collective-permute-done((bf16[240,128]{1,0:T(8,128)(2,1)S(1)}, bf16[240,128]{1,0:T(8,128)(2,1)S(1)}, u32[]{:S(2)}, u32[]{:S(2)}) %collective-permute-start.3) | collective-permute-done | bytes 61472 | tf_op jit(solution)/shard_map/ppermute | solution.py:799
  107.1 1.7 %collective-permute-done.4 = bf16[240,128]{1,0:T(8,128)(2,1)S(1)} collective-permute-done((bf16[240,128]{1,0:T(8,128)(2,1)S(1)}, bf16[240,128]{1,0:T(8,128)(2,1)S(1)}, u32[]{:S(2)}, u32[]{:S(2)}) %collective-permute-start.4) | collective-permute-done | bytes 61472 | tf_op jit(solution)/shard_map/ppermute | solution.py:799
  108.7 2.3 %collective-permute-done.5 = bf16[240,128]{1,0:T(8,128)(2,1)S(1)} collective-permute-done((bf16[240,128]{1,0:T(8,128)(2,1)S(1)}, bf16[240,128]{1,0:T(8,128)(2,1)S(1)}, u32[]{:S(2)}, u32[]{:S(2)}) %collective-permute-start.5) | collective-permute-done | bytes 61472 | tf_op jit(solution)/shard_map/ppermute | solution.py:799
  111.2 3.4 %collective-permute-start.8 = (bf16[240,128]{1,0:T(8,128)(2,1)S(1)}, bf16[240,128]{1,0:T(8,128)(2,1)S(1)}, u32[]{:S(2)}, u32[]{:S(2)}) collective-permute-start(bf16[240,128]{1,0:T(8,128)(2,1)S(1)} %fusion.2), channel_id=1, source_target_pairs={{0,6},{1,7},{2,4},{3,5},{4,2},{5,3},{6,0},{7,1},{8,14},{9,15},{10,... | collective-permute-start | bytes 184328 | tf_op jit(solution)/shard_map/ppermute | solution.py:799
  114.6 0.7 collective-permute-done.6
  115.3 0.1 collective-permute-done.7
  115.4 1.4 %collective-permute-done.8 = bf16[240,128]{1,0:T(8,128)(2,1)S(1)} collective-permute-done((bf16[240,128]{1,0:T(8,128)(2,1)S(1)}, bf16[240,128]{1,0:T(8,128)(2,1)S(1)}, u32[]{:S(2)}, u32[]{:S(2)}) %collective-permute-start.8) | collective-permute-done | bytes 61472 | tf_op jit(solution)/shard_map/ppermute | solution.py:799
  116.9 1.8 %collective-permute-start.12 = (bf16[240,128]{1,0:T(8,128)(2,1)S(1)}, bf16[240,128]{1,0:T(8,128)(2,1)S(1)}, u32[]{:S(2)}, u32[]{:S(2)}) collective-permute-start(bf16[240,128]{1,0:T(8,128)(2,1)S(1)} %add_convert_fusion), channel_id=1, source_target_pairs={{0,16},{1,17},{2,18},{3,19},{4,20},{5,21},{6,22},{7,23},{8,24},{9,... | collective-permute-start | bytes 184328 | tf_op jit(solution)/shard_map/ppermute | solution.py:799
  118.7 2.6 %collective-permute-start.13 = (bf16[240,128]{1,0:T(8,128)(2,1)S(1)}, bf16[240,128]{1,0:T(8,128)(2,1)S(1)}, u32[]{:S(2)}, u32[]{:S(2)}) collective-permute-start(bf16[240,128]{1,0:T(8,128)(2,1)S(1)} %add_convert_fusion), channel_id=1, source_target_pairs={{0,24},{1,25},{2,26},{3,27},{4,28},{5,29},{6,30},{7,31},{8,16},{9,... | collective-permute-start | bytes 184328 | tf_op jit(solution)/shard_map/ppermute | solution.py:799
  121.3 1.1 copy-done.1
  122.4 1.3 copy-done.2
  123.7 2.0 %final.1 = f32[9,256,128]{2,1,0:T(8,128)} custom-call(f32[256,1152]{1,0:T(8,128)S(1)} %copy-done.2, bf16[256,1152]{1,0:T(8,128)(2,1)S(1)} %collective-permute-done.9.near_ref, bf16[256,1152]{1,0:T(8,128)(2,1)S(1)} %collective-permute-done.10.far_ref, bf16[9,256,128]{2,1,0:T(8,128)(2,1)S(1)} %bitcast.32, bf16[9,256,128]{2,1,0:T(8,128)(2,1)S(1)} %bitcast.34, ...), custom_call_target="tpu_custom_call" | custom-call | tf_op jit(solution)/shard_map/final/pallas_call | solution.py:963
  125.8 1.4 %collective-permute-done.14.other_ref = bf16[960,128]{1,0:T(8,128)(2,1)S(1)} collective-permute-done((bf16[960,128]{1,0:T(8,128)(2,1)S(1)}, bf16[960,128]{1,0:T(8,128)(2,1)S(1)}, u32[]{:S(2)}, u32[]{:S(2)}) %collective-permute-start.14) | collective-permute-done | bytes 245792 | tf_op jit(solution)/shard_map/ppermute | solution.py:799
  127.2 1.6 %unpack.1 = (f32[128,128]{1,0:T(8,128)}, f32[128,128]{1,0:T(8,128)}, f32[128,128]{1,0:T(8,128)}, f32[128,128]{1,0:T(8,128)}, f32[128,128]{1,0:T(8,128)}, /*index...) custom-call(s32[2]{0:T(128)S(1)} %pad_add_fusion.1.place_ref, ...), custom_call_target="tpu_custom_call" | custom-call | tf_op jit(solution)/shard_map/unpack/pallas_call | solution.py:981
  (31 shorter events, 0.6 us)
Async XLA Ops:
  0.6 13.6 %collective-permute-start = (bf16[9,256,128]{2,1,0:T(8,128)(2,1)}, bf16[9,256,128]{2,1,0:T(8,128)(2,1)S(1)}, u32[]{:S(2)}, u32[]{:S(2)}) collective-permute-start(bf16[9,256,128]{2,1,0:T(8,128)(2,1)} %bitcast.29), channel_id=1, source_target_pairs={{0,1},{1,0},{2,3},{3,2},{4,5},{5,4},{6,7},{7,6},{8,9},{9,8},{10,11... | collective-permute-start | bytes 1769480 | tf_op jit(solution)/shard_map/ppermute | solution.py:854
  1.2 13.1 %collective-permute-start.1 = (bf16[9,256,128]{2,1,0:T(8,128)(2,1)}, bf16[9,256,128]{2,1,0:T(8,128)(2,1)}, u32[]{:S(2)}, u32[]{:S(2)}) collective-permute-start(bf16[9,256,128]{2,1,0:T(8,128)(2,1)} %bitcast.30), channel_id=1, source_target_pairs={{1,2},{2,1},{3,4},{4,3},{5,6},{6,5},{7,8},{8,7},{9,10},{10,9},{11,... | collective-permute-start | bytes 1769480 | tf_op jit(solution)/shard_map/ppermute | solution.py:855
  14.2 0.8 copy-start.6
  15.0 106.3 %copy-start = (bf16[256,9,128]{2,0,1:T(8,128)(2,1)S(1)}, bf16[256,9,128]{2,0,1:T(8,128)(2,1)}, u32[]{:S(2)}) copy-start(bf16[256,9,128]{2,0,1:T(8,128)(2,1)} %param.17) | copy-start | bytes 1769476
  15.0 106.3 %copy-start.3 = (bf16[128,128]{1,0:T(8,128)(2,1)S(1)}, bf16[128,128]{1,0:T(8,128)(2,1)}, u32[]{:S(2)}) copy-start(bf16[128,128]{1,0:T(8,128)(2,1)} %iso1_ref.3) | copy-start | bytes 98308
  15.0 106.3 %copy-start.4 = (bf16[128,128]{1,0:T(8,128)(2,1)S(1)}, bf16[128,128]{1,0:T(8,128)(2,1)}, u32[]{:S(2)}) copy-start(bf16[128,128]{1,0:T(8,128)(2,1)} %anti1_ref.3) | copy-start | bytes 98308
  15.0 106.3 %copy-start.5 = (bf16[128,128]{1,0:T(8,128)(2,1)S(1)}, bf16[128,128]{1,0:T(8,128)(2,1)}, u32[]{:S(2)}) copy-start(bf16[128,128]{1,0:T(8,128)(2,1)} %sym1_ref.3) | copy-start | bytes 98308
  84.1 12.3 %collective-permute-start.2 = (bf16[960,128]{1,0:T(8,128)(2,1)}, bf16[960,128]{1,0:T(8,128)(2,1)S(1)}, u32[]{:S(2)}, u32[]{:S(2)}) collective-permute-start(bf16[960,128]{1,0:T(8,128)(2,1)} %get-tuple-element.45), channel_id=1, source_target_pairs={{0,1},{1,0},{2,3},{3,2},{4,5},{5,4},{6,7},{7,6},{8,9},{9,8},{10,11... | collective-permute-start | bytes 737288 | tf_op jit(solution)/shard_map/ppermute | solution.py:799
  89.3 27.5 %collective-permute-start.10 = (bf16[256,1152]{1,0:T(8,128)(2,1)}, bf16[256,1152]{1,0:T(8,128)(2,1)S(1)}, u32[]{:S(2)}, u32[]{:S(2)}) collective-permute-start(bf16[256,1152]{1,0:T(8,128)(2,1)} %get-tuple-element.47), channel_id=1, source_target_pairs={{1,2},{2,1},{3,4},{4,3},{5,6},{6,5},{7,8},{8,7},{9,10},{10,9},{11,... | collective-permute-start | bytes 1769480 | tf_op jit(solution)/shard_map/ppermute | solution.py:953
  90.0 26.9 %collective-permute-start.9 = (bf16[256,1152]{1,0:T(8,128)(2,1)}, bf16[256,1152]{1,0:T(8,128)(2,1)S(1)}, u32[]{:S(2)}, u32[]{:S(2)}) collective-permute-start(bf16[256,1152]{1,0:T(8,128)(2,1)} %get-tuple-element.46), channel_id=1, source_target_pairs={{0,1},{1,0},{2,3},{3,2},{4,5},{5,4},{6,7},{7,6},{8,9},{9,8},{10,11... | collective-permute-start | bytes 1769480 | tf_op jit(solution)/shard_map/ppermute | solution.py:952
  97.6 9.5 %collective-permute-start.3 = (bf16[240,128]{1,0:T(8,128)(2,1)S(1)}, bf16[240,128]{1,0:T(8,128)(2,1)S(1)}, u32[]{:S(2)}, u32[]{:S(2)}) collective-permute-start(bf16[240,128]{1,0:T(8,128)(2,1)S(1)} %get-tuple-element.70), channel_id=1, source_target_pairs={{0,8},{1,9},{2,10},{3,11},{4,12},{5,13},{6,14},{7,15},{8,0},{9,1},... | collective-permute-start | bytes 184328 | tf_op jit(solution)/shard_map/ppermute | solution.py:799
  98.6 10.1 %collective-permute-start.4 = (bf16[240,128]{1,0:T(8,128)(2,1)S(1)}, bf16[240,128]{1,0:T(8,128)(2,1)S(1)}, u32[]{:S(2)}, u32[]{:S(2)}) collective-permute-start(bf16[240,128]{1,0:T(8,128)(2,1)S(1)} %get-tuple-element.72), channel_id=1, source_target_pairs={{0,16},{1,17},{2,18},{3,19},{4,20},{5,21},{6,22},{7,23},{8,24},{9,... | collective-permute-start | bytes 184328 | tf_op jit(solution)/shard_map/ppermute | solution.py:799
  100.8 10.2 %collective-permute-start.5 = (bf16[240,128]{1,0:T(8,128)(2,1)S(1)}, bf16[240,128]{1,0:T(8,128)(2,1)S(1)}, u32[]{:S(2)}, u32[]{:S(2)}) collective-permute-start(bf16[240,128]{1,0:T(8,128)(2,1)S(1)} %get-tuple-element.71), channel_id=1, source_target_pairs={{0,24},{1,25},{2,26},{3,27},{4,28},{5,29},{6,30},{7,31},{8,16},{9,... | collective-permute-start | bytes 184328 | tf_op jit(solution)/shard_map/ppermute | solution.py:799
  111.0 4.3 %collective-permute-start.6 = (bf16[240,128]{1,0:T(8,128)(2,1)S(1)}, bf16[240,128]{1,0:T(8,128)(2,1)S(1)}, u32[]{:S(2)}, u32[]{:S(2)}) collective-permute-start(bf16[240,128]{1,0:T(8,128)(2,1)S(1)} %fusion.2), channel_id=1, source_target_pairs={{0,2},{1,3},{2,0},{3,1},{4,6},{5,7},{6,4},{7,5},{8,10},{9,11},{10,... | collective-permute-start | bytes 184328 | tf_op jit(solution)/shard_map/ppermute | solution.py:799
  111.1 4.3 %collective-permute-start.7 = (bf16[240,128]{1,0:T(8,128)(2,1)S(1)}, bf16[240,128]{1,0:T(8,128)(2,1)S(1)}, u32[]{:S(2)}, u32[]{:S(2)}) collective-permute-start(bf16[240,128]{1,0:T(8,128)(2,1)S(1)} %fusion.2), channel_id=1, source_target_pairs={{0,4},{1,5},{2,6},{3,7},{4,0},{5,1},{6,2},{7,3},{8,12},{9,13},{10,... | collective-permute-start | bytes 184328 | tf_op jit(solution)/shard_map/ppermute | solution.py:799
  111.2 5.6 %collective-permute-start.8 = (bf16[240,128]{1,0:T(8,128)(2,1)S(1)}, bf16[240,128]{1,0:T(8,128)(2,1)S(1)}, u32[]{:S(2)}, u32[]{:S(2)}) collective-permute-start(bf16[240,128]{1,0:T(8,128)(2,1)S(1)} %fusion.2), channel_id=1, source_target_pairs={{0,6},{1,7},{2,4},{3,5},{4,2},{5,3},{6,0},{7,1},{8,14},{9,15},{10,... | collective-permute-start | bytes 184328 | tf_op jit(solution)/shard_map/ppermute | solution.py:799
  116.8 8.8 %collective-permute-start.11 = (bf16[240,128]{1,0:T(8,128)(2,1)S(1)}, bf16[240,128]{1,0:T(8,128)(2,1)S(1)}, u32[]{:S(2)}, u32[]{:S(2)}) collective-permute-start(bf16[240,128]{1,0:T(8,128)(2,1)S(1)} %add_convert_fusion), channel_id=1, source_target_pairs={{0,8},{1,9},{2,10},{3,11},{4,12},{5,13},{6,14},{7,15},{8,0},{9,1},... | collective-permute-start | bytes 184328 | tf_op jit(solution)/shard_map/ppermute | solution.py:799
  116.9 8.7 %collective-permute-start.12 = (bf16[240,128]{1,0:T(8,128)(2,1)S(1)}, bf16[240,128]{1,0:T(8,128)(2,1)S(1)}, u32[]{:S(2)}, u32[]{:S(2)}) collective-permute-start(bf16[240,128]{1,0:T(8,128)(2,1)S(1)} %add_convert_fusion), channel_id=1, source_target_pairs={{0,16},{1,17},{2,18},{3,19},{4,20},{5,21},{6,22},{7,23},{8,24},{9,... | collective-permute-start | bytes 184328 | tf_op jit(solution)/shard_map/ppermute | solution.py:799
  118.7 6.9 %collective-permute-start.13 = (bf16[240,128]{1,0:T(8,128)(2,1)S(1)}, bf16[240,128]{1,0:T(8,128)(2,1)S(1)}, u32[]{:S(2)}, u32[]{:S(2)}) collective-permute-start(bf16[240,128]{1,0:T(8,128)(2,1)S(1)} %add_convert_fusion), channel_id=1, source_target_pairs={{0,24},{1,25},{2,26},{3,27},{4,28},{5,29},{6,30},{7,31},{8,16},{9,... | collective-permute-start | bytes 184328 | tf_op jit(solution)/shard_map/ppermute | solution.py:799
  121.3 1.1 copy-start.1
  122.4 1.3 copy-start.2
  125.6 1.6 %collective-permute-start.14 = (bf16[960,128]{1,0:T(8,128)(2,1)S(1)}, bf16[960,128]{1,0:T(8,128)(2,1)S(1)}, u32[]{:S(2)}, u32[]{:S(2)}) collective-permute-start(bf16[960,128]{1,0:T(8,128)(2,1)S(1)} %pad_maximum_fusion.mine_ref), channel_id=1, source_target_pairs={{0,1},{1,0},{2,3},{3,2},{4,5},{5,4},{6,7},{7,6},{8,9},{9,8},{10,11... | collective-permute-start | bytes 737288 | tf_op jit(solution)/shard_map/ppermute | solution.py:799
